TPU v7x, 512 devices: a whole 4x4x16 slice. The times are simulated.
512 devices in a mesh: rows: 128 (over z, y, core), cols: 4 (over x).
Axes of the slice: x: 4, y: 4, z: 16, core: 2. Of those that a mesh axis runs over, the one named last changes fastest.
Arguments:
- latent: bfloat16 [4, 128, 1024], P(None, 'rows', 'cols'), may hold values from -18 to 18
- deep: bfloat16 [320, 128, 1024], P(None, 'rows', 'cols'), may hold values from -6 to 6
- timestep: int32 [1], replicated, may hold values from 0 to 999
- in_weight: bfloat16 [36, 320], replicated, may hold values from -1 to 1
- front_weight: bfloat16 [5760, 320], P('rows'), may hold values from -0.078125 to 0.078125
- middle_weight: bfloat16 [2880, 320], P('cols'), may hold values from -0.109375 to 0.109375
- skip_weight: bfloat16 [640, 320], P('cols'), may hold values from -0.25 to 0.25
- out_weight: bfloat16 [2880, 4], replicated, may hold values from -0.109375 to 0.109375
- time_weight: bfloat16 [320, 1280], replicated, may hold values from -0.3125 to 0.3125
- time_second: bfloat16 [1280, 1280], P('cols'), may hold values from -0.15625 to 0.15625
- time_proj: bfloat16 [1280, 320], replicated, may hold values from -0.15625 to 0.15625
- input_gain: float32 [640], replicated, may hold values from 0.1 to 1.9
- middle_gain: float32 [320], replicated, may hold values from 0.1 to 1.9
- output_gain: float32 [320], replicated, may hold values from 0.1 to 1.9
Outputs:
- noise: float32 [4, 128, 1024], P(None, 'rows', 'cols')
All inputs are finite; a program needn't handle non-finite values.
Results may differ from a plain program's by a relative error of at most 0.0047.
Values may be sent and summed in bfloat16 or wider, within the bound.
No kernel may reach another device: no remote copies, remote signals or barrier semaphores. Data moves between devices by JAX's collectives and lax.ppermute only.
A program may use at most 64 MiB of HBM per device.

v0:
```python
import math

import jax
import jax.numpy as jnp
from jax import lax
from jax.sharding import Mesh
from jax.sharding import PartitionSpec as P

GROUPS = 32
ROWS = ("rows_0", "rows_1", "rows_2")


epsilon = 1e-05


def from_everyone(x, axis):
    count = lax.axis_size(axis)
    return lax.all_to_all(jnp.broadcast_to(x[None], (count, *x.shape)), axis, 0, 0, tiled=True)


def taken_together(x, axis):
    return from_everyone(x, axis).sum(axis=0)


def over_axes(x, axes):
    far, near = axes
    nearer = taken_together(x, near)
    return taken_together(nearer, far)


def together(arrays, axis):
    vector, at, finished = (jnp.concatenate([a.reshape(-1) for a in arrays]), 0, [])
    subtotal = over_axes(vector, axis)
    for a in arrays:
        finished.append(subtotal[at : at + a.size].reshape(a.shape))
        at += a.size
    return tuple(finished)


def laid_out(parts, dim):
    shape = list(parts.shape[1:])
    shape[dim] *= parts.shape[0]
    return jnp.moveaxis(parts, 0, dim).reshape(shape)


def gather_directly(x, axis, dim):
    return laid_out(from_everyone(x, axis), dim)


def padded_2(cells, sides, width):
    for axis, dim in sides:
        count = lax.axis_size(axis)
        ends = count - 1
        head = lax.slice_in_dim(cells, 0, width, axis=dim)
        tail = lax.slice_in_dim(cells, cells.shape[dim] - width, cells.shape[dim], axis=dim)
        cells = jnp.concatenate(
            [
                lax.ppermute(tail, axis, [(i, (i + 1) % count) for i in range(ends)]),
                cells,
                lax.ppermute(head, axis, [((i + 1) % count, i) for i in range(ends)]),
            ],
            axis=dim,
        )
    return cells


def unfold(padded, row_count, col_count):
    shifted = [
        padded[:, row_step : row_step + row_count, col_step : col_step + col_count]
        for row_step in range(3)
        for col_step in range(3)
    ]
    return jnp.stack(shifted, 0).reshape(9 * padded.shape[0], row_count * col_count)


def project(weight, columns):
    return lax.dot_general(
        weight, columns, (((0,), (0,)), ((), ())), preferred_element_type=jnp.float32
    )


def norm_silu(values, gain, members):
    grouped = values.reshape(GROUPS, -1)
    totals, squares = together(
        (jnp.sum(grouped, axis=1), jnp.sum(grouped * grouped, axis=1)),
        (("rows_0", "rows_1"), ("rows_2", "cols")),
    )
    center = totals / members
    offsets = grouped - center[:, None]
    spread = squares / members - center * center
    scaled = (offsets * lax.rsqrt(spread + epsilon)[:, None]).reshape(values.shape) * gain[:, None]
    return jax.nn.silu(scaled).astype(jnp.bfloat16)


def time_shift_of(timestep, time_weight, time_second, time_proj):
    half_width = time_weight.shape[0] // 2
    ratios = jnp.exp(-math.log(10000.0) * jnp.arange(half_width, dtype=jnp.float32) / half_width)
    angles = timestep[0].astype(jnp.float32) * ratios
    features = jnp.concatenate([jnp.cos(angles), jnp.sin(angles)])
    hidden = jax.nn.silu(
        jnp.dot(features, time_weight.astype(jnp.float32), precision=lax.Precision.HIGHEST)
    )
    embedded = jnp.dot(hidden, time_second.astype(jnp.float32), precision=lax.Precision.HIGHEST)
    return jnp.dot(
        jax.nn.silu(embedded), time_proj.astype(jnp.float32), precision=lax.Precision.HIGHEST
    )


def shards(
    latent,
    deep,
    timestep,
    in_weight,
    front_weight,
    middle_weight,
    skip_weight,
    out_weight,
    time_weight,
    time_second,
    time_proj,
    input_gain,
    middle_gain,
    output_gain,
):
    rows_here = latent.shape[1]
    cols_here = latent.shape[2]
    pixels = rows_here * cols_here
    image_cells = pixels * lax.axis_size(ROWS) * lax.axis_size("cols")
    channels = deep.shape[0]
    full_middle, full_skip, full_second = (
        gather_directly(middle_weight, "cols", 0),
        gather_directly(skip_weight, "cols", 0),
        gather_directly(time_second, "cols", 0),
    )
    time_shift = time_shift_of(timestep, time_weight, full_second, time_proj)
    padded_latent = padded_2(latent, ((ROWS, 1), ("cols", 2)), 1)
    skip_feat = project(in_weight, unfold(padded_latent, rows_here, cols_here)).astype(jnp.bfloat16)
    joined = jnp.concatenate([deep.reshape(channels, pixels), skip_feat], axis=0)
    members_wide = float(joined.shape[0] // GROUPS * image_cells)
    act_one = norm_silu(joined.astype(jnp.float32), input_gain, members_wide)
    padded_one = padded_2(act_one.reshape(-1, rows_here, cols_here), ((ROWS, 1), ("cols", 2)), 1)
    columns_one = unfold(padded_one, rows_here, cols_here)
    out_channels = front_weight.shape[1]
    hidden_one = project(lax.all_gather(front_weight, ROWS, axis=0, tiled=True), columns_one)
    hidden_one = hidden_one + time_shift[:, None]
    members_narrow = float(out_channels // GROUPS * image_cells)
    act_two = norm_silu(hidden_one, middle_gain, members_narrow)
    padded_two = padded_2(act_two.reshape(-1, rows_here, cols_here), ((ROWS, 1), ("cols", 2)), 1)
    block_out = project(full_middle, unfold(padded_two, rows_here, cols_here)) + project(
        full_skip, joined
    )
    act_three = norm_silu(block_out, output_gain, members_narrow)
    padded_three = padded_2(
        act_three.reshape(-1, rows_here, cols_here), ((ROWS, 1), ("cols", 2)), 1
    )
    noise = project(out_weight, unfold(padded_three, rows_here, cols_here))
    return noise.reshape(out_weight.shape[1], rows_here, cols_here)


def solution(mesh):
    finer = Mesh(
        mesh.devices.reshape(16, 4, 2, mesh.shape["cols"]), ("rows_0", "rows_1", "rows_2", "cols")
    )
    in_specs = (
        P(None, ROWS, "cols"),
        P(None, ROWS, "cols"),
        P(),
        P(),
        P(ROWS, None),
        P("cols", None),
        P("cols", None),
        P(),
        P(),
        P("cols", None),
        P(),
        P(),
        P(),
        P(),
    )
    out_specs = P(None, ROWS, "cols")
    return jax.shard_map(
        shards, mesh=finer, in_specs=in_specs, out_specs=out_specs, check_vma=False
    )
```

profile of v0, /device:TPU:1, one launch (start us, length us, event | category | flops | bytes accessed | tf_op | source)
XLA Modules:
  0.0 323.6 jit_solution(3858233901648060752)
XLA Ops:
  7.3 4.6 %collective-permute-start = (bf16[4,1,256]{2,0,1:T(4,128)(2,1)}, bf16[4,1,256]{2,0,1:T(4,128)(2,1)S(1)}, u32[]{:S(2)}, u32[]{:S(2)}) collective-permute-start(bf16[4,1,256]{2,0,1:T(4,128)(2,1)} %param.14), channel_id=1, source_target_pairs={{0,4},{4,8},{8,12},{12,16},{16,20},{20,24},{24,28},{28,32},{32,36}... | collective-permute-start | bytes 6152 | tf_op jit(solution)/shard_map/ppermute | solution.py:58
  11.9 5.5 %collective-permute-start.1 = (bf16[4,1,256]{2,0,1:T(4,128)(2,1)}, bf16[4,1,256]{2,0,1:T(4,128)(2,1)S(1)}, u32[]{:S(2)}, u32[]{:S(2)}) collective-permute-start(bf16[4,1,256]{2,0,1:T(4,128)(2,1)} %param.14), channel_id=1, source_target_pairs={{4,0},{8,4},{12,8},{16,12},{20,16},{24,20},{28,24},{32,28},{36,32}... | collective-permute-start | bytes 6152 | tf_op jit(solution)/shard_map/ppermute | solution.py:60
  21.6 2.9 collective-permute-done.3
  28.3 8.5 %all_to_all.51 = f32[8,1,64]{2,1,0:T(1,128)S(1)} all-to-all(f32[8,1,64]{2,1,0:T(1,128)S(1)} %broadcast_in_dim.18), channel_id=1, replica_groups=mesh['rows_0'=16,'rows_1'=4,'rows_2'=2,'cols'=4] {'rows_2','cols'}, dimensions={0} | all-to-all | bytes 4096 | tf_op jit(solution)/shard_map/all_to_all | solution.py:18
  37.5 20.3 %all-to-all-start.1 = ((f32[64,1,64]{2,1,0:T(1,128)}), f32[64,1,64]{2,1,0:T(1,128)S(1)}, u32[]{:S(2)}, u32[]{:S(2)}) async-start(f32[64,1,64]{2,1,0:T(1,128)} %broadcast_in_dim.19), calls=%async_computation.1 | async-start | bytes 65536 | tf_op jit(solution)/shard_map/all_to_all | solution.py:18
  58.4 13.0 %all-to-all-done.1 = f32[64,1,64]{2,1,0:T(1,128)S(1)} async-done(((f32[64,1,64]{2,1,0:T(1,128)}), f32[64,1,64]{2,1,0:T(1,128)S(1)}, u32[]{:S(2)}, u32[]{:S(2)}) %all-to-all-start.1) | async-done | bytes 16416 | tf_op jit(solution)/shard_map/all_to_all | solution.py:18
  73.4 4.8 %all-to-all-start.2 = ((bf16[4,320,1280]{2,1,0:T(8,128)(2,1)}), bf16[4,320,1280]{2,1,0:T(8,128)(2,1)}, u32[]{:S(2)}, u32[]{:S(2)}) async-start(bf16[4,320,1280]{2,1,0:T(8,128)(2,1)} %broadcast_in_dim.20), calls=%async_computation.2 | async-start | bytes 6553600 | tf_op jit(solution)/shard_map/all_to_all | solution.py:18
  79.0 3.9 %collective-permute-start.4 = (bf16[640,1,256]{2,0,1:T(8,128)(2,1)S(1)}, bf16[640,1,256]{2,0,1:T(8,128)(2,1)S(1)}, u32[]{:S(2)}, u32[]{:S(2)}) collective-permute-start(bf16[640,1,256]{2,0,1:T(8,128)(2,1)S(1)} %multiply_convert_fusion.1), channel_id=1, source_target_pairs={{0,4},{4,8},{8,12},{12,16},{16,20},{20,24},{24,28},{28,32},{32,36}... | collective-permute-start | bytes 983048 | tf_op jit(solution)/shard_map/ppermute | solution.py:58
  87.0 4.8 %collective-permute-done.5 = bf16[640,1,256]{2,0,1:T(8,128)(2,1)S(1)} collective-permute-done((bf16[640,1,256]{2,0,1:T(8,128)(2,1)S(1)}, bf16[640,1,256]{2,0,1:T(8,128)(2,1)S(1)}, u32[]{:S(2)}, u32[]{:S(2)}) %collective-permute-start.5) | collective-permute-done | bytes 327712 | tf_op jit(solution)/shard_map/ppermute | solution.py:60
  92.1 3.6 %collective-permute-start.6 = (bf16[640,3,1]{2,0,1:T(8,128)(2,1)S(1)}, bf16[640,3,1]{2,0,1:T(8,128)(2,1)S(1)}, u32[]{:S(2)}, u32[]{:S(2)}) collective-permute-start(bf16[640,3,1]{2,0,1:T(8,128)(2,1)S(1)} %get-tuple-element.12), channel_id=1, source_target_pairs={{0,1},{1,2},{2,3},{4,5},{5,6},{6,7},{8,9},{9,10},{10,11},{12,13},{... | collective-permute-start | bytes 11528 | tf_op jit(solution)/shard_map/ppermute | solution.py:58
  97.1 25.3 %collective-permute-done.6 = bf16[640,3,1]{2,0,1:T(8,128)(2,1)S(1)} collective-permute-done((bf16[640,3,1]{2,0,1:T(8,128)(2,1)S(1)}, bf16[640,3,1]{2,0,1:T(8,128)(2,1)S(1)}, u32[]{:S(2)}, u32[]{:S(2)}) %collective-permute-start.6) | collective-permute-done | bytes 3872 | tf_op jit(solution)/shard_map/ppermute | solution.py:58
  130.8 3.4 %convolution_reduce_fusion = f32[1280]{0:T(1024)S(1)} fusion(f32[1280,1]{0,1:T(1,128)S(1)} %reshape.374, bf16[1280,1280]{1,0:T(8,128)(2,1)} %bitcast.27), kind=kOutput, calls=%fused_computation.3 | convolution fusion | flops 19660800 | bytes 3287040 | tf_op jit(solution)/shard_map/dot_general | solution.py:103
  135.1 24.0 %all-gather.3.cloned.1.call-done = bf16[128,45,320]{2,1,0:T(8,128)(2,1)} async-done(((bf16[1,45,320]{2,1,0:T(8,128)(2,1)}), bf16[128,45,320]{2,1,0:T(8,128)(2,1)}) %all-gather.3.cloned.1.call-update) | async-done | bytes 3686416 | tf_op jit(solution)/shard_map/all_gather | solution.py:144
  159.1 7.6 %reshape.371 = bf16[5760,320]{1,0:T(8,128)(2,1)} reshape(bf16[128,45,320]{2,1,0:T(8,128)(2,1)} %all-gather.3.cloned.1.call-done) | data formatting | bytes 7372800
  166.7 5.7 %fusion.41 = (f32[320]{0:T(512)S(1)}, f32[320]{0:T(512)S(1)}, f32[256,320]{0,1:T(8,128)}) fusion(f32[320]{0:T(512)S(1)} %convolution_reduce_fusion.2, bf16[5760,256]{1,0:T(8,128)(2,1)} %bitcast.24, bf16[5760,320]{1,0:T(8,128)(2,1)} %reshape.371), kind=kOutput, calls=%fused_computation.131 | convolution fusion | flops 944045440 | bytes 6967040 | tf_op jit(solution)/shard_map/dot_general | solution.py:77
  173.0 8.9 %all_to_all.52 = f32[8,1,64]{2,1,0:T(1,128)S(1)} all-to-all(f32[8,1,64]{2,1,0:T(1,128)S(1)} %broadcast_in_dim.21), channel_id=1, replica_groups=mesh['rows_0'=16,'rows_1'=4,'rows_2'=2,'cols'=4] {'rows_2','cols'}, dimensions={0} | all-to-all | bytes 4096 | tf_op jit(solution)/shard_map/all_to_all | solution.py:18
  182.6 3.5 %all-to-all-start.6 = ((bf16[4,160,320]{2,1,0:T(8,128)(2,1)}), bf16[4,160,320]{2,1,0:T(8,128)(2,1)S(1)}, u32[]{:S(2)}, u32[]{:S(2)}) async-start(bf16[4,160,320]{2,1,0:T(8,128)(2,1)} %broadcast_in_dim.24), calls=%async_computation.6 | async-start | bytes 983040 | tf_op jit(solution)/shard_map/all_to_all | solution.py:18
  186.1 8.5 %all-to-all-done.6 = bf16[4,160,320]{2,1,0:T(8,128)(2,1)S(1)} async-done(((bf16[4,160,320]{2,1,0:T(8,128)(2,1)}), bf16[4,160,320]{2,1,0:T(8,128)(2,1)S(1)}, u32[]{:S(2)}, u32[]{:S(2)}) %all-to-all-start.6) | async-done | bytes 409632 | tf_op jit(solution)/shard_map/all_to_all | solution.py:18
  194.6 22.5 %all_to_all.53 = f32[64,1,64]{2,1,0:T(1,128)S(1)} all-to-all(f32[64,1,64]{2,1,0:T(1,128)S(1)} %broadcast_in_dim.22), channel_id=1, replica_groups=mesh['rows_0'=16,'rows_1'=4,'rows_2'=2,'cols'=4] {'rows_0','rows_1'}, dimensions={0} | all-to-all | bytes 32768 | tf_op jit(solution)/shard_map/all_to_all | solution.py:18
  218.5 3.7 %all-to-all-start.5 = ((bf16[4,720,320]{1,2,0:T(8,128)(2,1)}), bf16[4,720,320]{1,2,0:T(8,128)(2,1)S(1)}, u32[]{:S(2)}, u32[]{:S(2)}) async-start(bf16[4,720,320]{1,2,0:T(8,128)(2,1)} %broadcast_in_dim.23), calls=%async_computation.5 | async-start | bytes 3932160 | tf_op jit(solution)/shard_map/all_to_all | solution.py:18
  224.0 5.4 %collective-permute-start.8 = (bf16[320,1,256]{2,0,1:T(8,128)(2,1)S(1)}, bf16[320,1,256]{2,0,1:T(8,128)(2,1)S(1)}, u32[]{:S(2)}, u32[]{:S(2)}) collective-permute-start(bf16[320,1,256]{2,0,1:T(8,128)(2,1)S(1)} %fusion.62), channel_id=1, source_target_pairs={{0,4},{4,8},{8,12},{12,16},{16,20},{20,24},{24,28},{28,32},{32,36}... | collective-permute-start | bytes 491528 | tf_op jit(solution)/shard_map/ppermute | solution.py:58
  231.7 4.7 %collective-permute-done.9 = bf16[320,1,256]{2,0,1:T(8,128)(2,1)S(1)} collective-permute-done((bf16[320,1,256]{2,0,1:T(8,128)(2,1)S(1)}, bf16[320,1,256]{2,0,1:T(8,128)(2,1)S(1)}, u32[]{:S(2)}, u32[]{:S(2)}) %collective-permute-start.9) | collective-permute-done | bytes 163872 | tf_op jit(solution)/shard_map/ppermute | solution.py:60
  237.3 4.3 %collective-permute-start.10 = (bf16[320,3,1]{2,0,1:T(8,128)(2,1)}, bf16[320,3,1]{2,0,1:T(8,128)(2,1)}, u32[]{:S(2)}, u32[]{:S(2)}) collective-permute-start(bf16[320,3,1]{2,0,1:T(8,128)(2,1)} %get-tuple-element.16), channel_id=1, source_target_pairs={{0,1},{1,2},{2,3},{4,5},{5,6},{6,7},{8,9},{9,10},{10,11},{12,13},{... | collective-permute-start | bytes 5768 | tf_op jit(solution)/shard_map/ppermute | solution.py:58
  244.1 2.8 copy.28
  246.9 3.8 %reshape.365 = bf16[2880,320]{0,1:T(8,128)(2,1)S(1)} reshape(bf16[4,720,320]{1,0,2:T(4,128)(2,1)} %copy.28) | data formatting | bytes 3686400 | tf_op jit(solution)/shard_map/reshape | solution.py:43
  253.2 4.6 %collective-permute-done.11 = bf16[320,3,1]{2,0,1:T(8,128)(2,1)S(1)} collective-permute-done((bf16[320,3,1]{2,0,1:T(8,128)(2,1)S(1)}, bf16[320,3,1]{2,0,1:T(8,128)(2,1)S(1)}, u32[]{:S(2)}, u32[]{:S(2)}) %collective-permute-start.11) | collective-permute-done | bytes 1952 | tf_op jit(solution)/shard_map/ppermute | solution.py:60
  261.9 14.7 %all_to_all.54 = f32[8,1,64]{2,1,0:T(1,128)S(1)} all-to-all(f32[8,1,64]{2,1,0:T(1,128)S(1)} %broadcast_in_dim.25), channel_id=1, replica_groups=mesh['rows_0'=16,'rows_1'=4,'rows_2'=2,'cols'=4] {'rows_2','cols'}, dimensions={0} | all-to-all | bytes 4096 | tf_op jit(solution)/shard_map/all_to_all | solution.py:18
  276.6 17.4 %all_to_all.55 = f32[64,1,64]{2,1,0:T(1,128)S(1)} all-to-all(f32[64,1,64]{2,1,0:T(1,128)S(1)} %broadcast_in_dim.26), channel_id=1, replica_groups=mesh['rows_0'=16,'rows_1'=4,'rows_2'=2,'cols'=4] {'rows_0','rows_1'}, dimensions={0} | all-to-all | bytes 32768 | tf_op jit(solution)/shard_map/all_to_all | solution.py:18
  294.7 3.9 %collective-permute-start.12 = (bf16[320,1,256]{2,0,1:T(8,128)(2,1)S(1)}, bf16[320,1,256]{2,0,1:T(8,128)(2,1)S(1)}, u32[]{:S(2)}, u32[]{:S(2)}) collective-permute-start(bf16[320,1,256]{2,0,1:T(8,128)(2,1)S(1)} %fusion.61), channel_id=1, source_target_pairs={{0,4},{4,8},{8,12},{12,16},{16,20},{20,24},{24,28},{28,32},{32,36}... | collective-permute-start | bytes 491528 | tf_op jit(solution)/shard_map/ppermute | solution.py:58
  300.8 4.4 %collective-permute-done.13 = bf16[320,1,256]{2,0,1:T(8,128)(2,1)S(1)} collective-permute-done((bf16[320,1,256]{2,0,1:T(8,128)(2,1)S(1)}, bf16[320,1,256]{2,0,1:T(8,128)(2,1)S(1)}, u32[]{:S(2)}, u32[]{:S(2)}) %collective-permute-start.13) | collective-permute-done | bytes 163872 | tf_op jit(solution)/shard_map/ppermute | solution.py:60
  305.4 2.2 collective-permute-start.14
  310.9 3.7 %collective-permute-done.15 = bf16[320,3,1]{2,0,1:T(8,128)(2,1)S(1)} collective-permute-done((bf16[320,3,1]{2,0,1:T(8,128)(2,1)S(1)}, bf16[320,3,1]{2,0,1:T(8,128)(2,1)S(1)}, u32[]{:S(2)}, u32[]{:S(2)}) %collective-permute-start.15) | collective-permute-done | bytes 1952 | tf_op jit(solution)/shard_map/ppermute | solution.py:60
  (161 shorter events, 52.0 us)
Async XLA Ops:
  6.5 78.5 %copy-start = (bf16[320,1280]{1,0:T(8,128)(2,1)S(1)}, bf16[320,1280]{1,0:T(8,128)(2,1)}, u32[]{:S(2)}) copy-start(bf16[320,1280]{1,0:T(8,128)(2,1)} %param.22) | copy-start | bytes 2457604
  6.5 64.8 %copy-start.6 = (bf16[320,1280]{1,0:T(8,128)(2,1)S(1)}, bf16[320,1280]{1,0:T(8,128)(2,1)}, u32[]{:S(2)}) copy-start(bf16[320,1280]{1,0:T(8,128)(2,1)} %param.23) | copy-start | bytes 2457604
  6.5 152.6 %all-gather.3.cloned.1.call-start = ((), (), s32[]{:S(2)}) async-start(), calls=%async_computation.9 | async-start | bytes 4755456 | tf_op jit(solution)/shard_map/all_gather | solution.py:144
  7.3 10.1 %collective-permute-start = (bf16[4,1,256]{2,0,1:T(4,128)(2,1)}, bf16[4,1,256]{2,0,1:T(4,128)(2,1)S(1)}, u32[]{:S(2)}, u32[]{:S(2)}) collective-permute-start(bf16[4,1,256]{2,0,1:T(4,128)(2,1)} %param.14), channel_id=1, source_target_pairs={{0,4},{4,8},{8,12},{12,16},{16,20},{20,24},{24,28},{28,32},{32,36}... | collective-permute-start | bytes 6152 | tf_op jit(solution)/shard_map/ppermute | solution.py:58
  11.9 6.5 %collective-permute-start.1 = (bf16[4,1,256]{2,0,1:T(4,128)(2,1)}, bf16[4,1,256]{2,0,1:T(4,128)(2,1)S(1)}, u32[]{:S(2)}, u32[]{:S(2)}) collective-permute-start(bf16[4,1,256]{2,0,1:T(4,128)(2,1)} %param.14), channel_id=1, source_target_pairs={{4,0},{8,4},{12,8},{16,12},{20,16},{24,20},{28,24},{32,28},{36,32}... | collective-permute-start | bytes 6152 | tf_op jit(solution)/shard_map/ppermute | solution.py:60
  18.5 3.0 collective-permute-start.2
  20.2 4.3 %collective-permute-start.3 = (bf16[4,3,1]{2,0,1:T(4,128)(2,1)S(1)}, bf16[4,3,1]{2,0,1:T(4,128)(2,1)S(1)}, u32[]{:S(2)}, u32[]{:S(2)}) collective-permute-start(bf16[4,3,1]{2,0,1:T(4,128)(2,1)S(1)} %get-tuple-element.17), channel_id=1, source_target_pairs={{1,0},{2,1},{3,2},{5,4},{6,5},{7,6},{9,8},{10,9},{11,10},{13,12},{... | collective-permute-start | bytes 80 | tf_op jit(solution)/shard_map/ppermute | solution.py:60
  37.5 33.9 %all-to-all-start.1 = ((f32[64,1,64]{2,1,0:T(1,128)}), f32[64,1,64]{2,1,0:T(1,128)S(1)}, u32[]{:S(2)}, u32[]{:S(2)}) async-start(f32[64,1,64]{2,1,0:T(1,128)} %broadcast_in_dim.19), calls=%async_computation.1 | async-start | bytes 65536 | tf_op jit(solution)/shard_map/all_to_all | solution.py:18
  73.4 5.3 %copy-start.1 = (bf16[320,1,256]{2,0,1:T(8,128)(2,1)S(1)}, bf16[320,1,256]{2,0,1:T(8,128)(2,1)}, u32[]{:S(2)}) copy-start(bf16[320,1,256]{2,0,1:T(8,128)(2,1)} %param.15) | copy-start | bytes 491524
  73.4 5.3 %copy-start.12 = (f32[640]{0:T(1024)S(1)}, f32[640]{0:T(1024)}, u32[]{:S(2)}) copy-start(f32[640]{0:T(1024)} %param.25) | copy-start | bytes 7684
  73.4 57.4 %all-to-all-start.2 = ((bf16[4,320,1280]{2,1,0:T(8,128)(2,1)}), bf16[4,320,1280]{2,1,0:T(8,128)(2,1)}, u32[]{:S(2)}, u32[]{:S(2)}) async-start(bf16[4,320,1280]{2,1,0:T(8,128)(2,1)} %broadcast_in_dim.20), calls=%async_computation.2 | async-start | bytes 6553600 | tf_op jit(solution)/shard_map/all_to_all | solution.py:18
  79.0 7.9 %collective-permute-start.4 = (bf16[640,1,256]{2,0,1:T(8,128)(2,1)S(1)}, bf16[640,1,256]{2,0,1:T(8,128)(2,1)S(1)}, u32[]{:S(2)}, u32[]{:S(2)}) collective-permute-start(bf16[640,1,256]{2,0,1:T(8,128)(2,1)S(1)} %multiply_convert_fusion.1), channel_id=1, source_target_pairs={{0,4},{4,8},{8,12},{12,16},{16,20},{20,24},{24,28},{28,32},{32,36}... | collective-permute-start | bytes 983048 | tf_op jit(solution)/shard_map/ppermute | solution.py:58
  83.0 8.8 %collective-permute-start.5 = (bf16[640,1,256]{2,0,1:T(8,128)(2,1)S(1)}, bf16[640,1,256]{2,0,1:T(8,128)(2,1)S(1)}, u32[]{:S(2)}, u32[]{:S(2)}) collective-permute-start(bf16[640,1,256]{2,0,1:T(8,128)(2,1)S(1)} %multiply_convert_fusion.1), channel_id=1, source_target_pairs={{4,0},{8,4},{12,8},{16,12},{20,16},{24,20},{28,24},{32,28},{36,32}... | collective-permute-start | bytes 983048 | tf_op jit(solution)/shard_map/ppermute | solution.py:60
  92.1 30.3 %collective-permute-start.6 = (bf16[640,3,1]{2,0,1:T(8,128)(2,1)S(1)}, bf16[640,3,1]{2,0,1:T(8,128)(2,1)S(1)}, u32[]{:S(2)}, u32[]{:S(2)}) collective-permute-start(bf16[640,3,1]{2,0,1:T(8,128)(2,1)S(1)} %get-tuple-element.12), channel_id=1, source_target_pairs={{0,1},{1,2},{2,3},{4,5},{5,6},{6,7},{8,9},{9,10},{10,11},{12,13},{... | collective-permute-start | bytes 11528 | tf_op jit(solution)/shard_map/ppermute | solution.py:58
  95.8 28.5 %collective-permute-start.7 = (bf16[640,3,1]{2,0,1:T(8,128)(2,1)S(1)}, bf16[640,3,1]{2,0,1:T(8,128)(2,1)S(1)}, u32[]{:S(2)}, u32[]{:S(2)}) collective-permute-start(bf16[640,3,1]{2,0,1:T(8,128)(2,1)S(1)} %get-tuple-element.11), channel_id=1, source_target_pairs={{1,0},{2,1},{3,2},{5,4},{6,5},{7,6},{9,8},{10,9},{11,10},{13,12},{... | collective-permute-start | bytes 11528 | tf_op jit(solution)/shard_map/ppermute | solution.py:60
  166.7 15.1 %copy-start.10 = (bf16[160,320]{1,0:T(8,128)(2,1)S(1)}, bf16[160,320]{1,0:T(8,128)(2,1)}, u32[]{:S(2)}) copy-start(bf16[160,320]{1,0:T(8,128)(2,1)} %param.20) | copy-start | bytes 307204
  172.4 44.7 %copy-start.7 = (bf16[720,320]{0,1:T(8,128)(2,1)S(1)}, bf16[720,320]{0,1:T(8,128)(2,1)}, u32[]{:S(2)}) copy-start(bf16[720,320]{0,1:T(8,128)(2,1)} %param.19) | copy-start | bytes 1382404
  182.6 12.0 %all-to-all-start.6 = ((bf16[4,160,320]{2,1,0:T(8,128)(2,1)}), bf16[4,160,320]{2,1,0:T(8,128)(2,1)S(1)}, u32[]{:S(2)}, u32[]{:S(2)}) async-start(bf16[4,160,320]{2,1,0:T(8,128)(2,1)} %broadcast_in_dim.24), calls=%async_computation.6 | async-start | bytes 983040 | tf_op jit(solution)/shard_map/all_to_all | solution.py:18
  194.6 23.9 %copy-start.2 = (bf16[4,160,320]{2,1,0:T(8,128)(2,1)}, bf16[4,160,320]{2,1,0:T(8,128)(2,1)S(1)}, u32[]{:S(2)}) copy-start(bf16[4,160,320]{2,1,0:T(8,128)(2,1)S(1)} %all-to-all-done.6) | copy-start | bytes 1228804
  218.5 4.2 %copy-start.13 = (f32[320]{0:T(512)S(1)}, f32[320]{0:T(512)}, u32[]{:S(2)}) copy-start(f32[320]{0:T(512)} %param.26) | copy-start | bytes 3844
  218.5 25.6 %all-to-all-start.5 = ((bf16[4,720,320]{1,2,0:T(8,128)(2,1)}), bf16[4,720,320]{1,2,0:T(8,128)(2,1)S(1)}, u32[]{:S(2)}, u32[]{:S(2)}) async-start(bf16[4,720,320]{1,2,0:T(8,128)(2,1)} %broadcast_in_dim.23), calls=%async_computation.5 | async-start | bytes 3932160 | tf_op jit(solution)/shard_map/all_to_all | solution.py:18
  222.7 18.9 %copy-start.3 = (bf16[4,160,320]{2,1,0:T(8,128)(2,1)S(1)}, bf16[4,160,320]{2,1,0:T(8,128)(2,1)}, u32[]{:S(2)}) copy-start(bf16[4,160,320]{2,1,0:T(8,128)(2,1)} %copy-done.2) | copy-start | bytes 1228804
  224.0 7.7 %collective-permute-start.8 = (bf16[320,1,256]{2,0,1:T(8,128)(2,1)S(1)}, bf16[320,1,256]{2,0,1:T(8,128)(2,1)S(1)}, u32[]{:S(2)}, u32[]{:S(2)}) collective-permute-start(bf16[320,1,256]{2,0,1:T(8,128)(2,1)S(1)} %fusion.62), channel_id=1, source_target_pairs={{0,4},{4,8},{8,12},{12,16},{16,20},{20,24},{24,28},{28,32},{32,36}... | collective-permute-start | bytes 491528 | tf_op jit(solution)/shard_map/ppermute | solution.py:58
  229.4 6.9 %collective-permute-start.9 = (bf16[320,1,256]{2,0,1:T(8,128)(2,1)S(1)}, bf16[320,1,256]{2,0,1:T(8,128)(2,1)S(1)}, u32[]{:S(2)}, u32[]{:S(2)}) collective-permute-start(bf16[320,1,256]{2,0,1:T(8,128)(2,1)S(1)} %fusion.62), channel_id=1, source_target_pairs={{4,0},{8,4},{12,8},{16,12},{20,16},{24,20},{28,24},{32,28},{36,32}... | collective-permute-start | bytes 491528 | tf_op jit(solution)/shard_map/ppermute | solution.py:60
  237.3 14.8 %collective-permute-start.10 = (bf16[320,3,1]{2,0,1:T(8,128)(2,1)}, bf16[320,3,1]{2,0,1:T(8,128)(2,1)}, u32[]{:S(2)}, u32[]{:S(2)}) collective-permute-start(bf16[320,3,1]{2,0,1:T(8,128)(2,1)} %get-tuple-element.16), channel_id=1, source_target_pairs={{0,1},{1,2},{2,3},{4,5},{5,6},{6,7},{8,9},{9,10},{10,11},{12,13},{... | collective-permute-start | bytes 5768 | tf_op jit(solution)/shard_map/ppermute | solution.py:58
  250.7 8.2 %copy-start.4 = (f32[256,320]{0,1:T(8,128)S(1)}, f32[256,320]{0,1:T(8,128)}, u32[]{:S(2)}) copy-start(f32[256,320]{0,1:T(8,128)} %get-tuple-element.25) | copy-start | bytes 983044
  250.7 7.1 %collective-permute-start.11 = (bf16[320,3,1]{2,0,1:T(8,128)(2,1)S(1)}, bf16[320,3,1]{2,0,1:T(8,128)(2,1)S(1)}, u32[]{:S(2)}, u32[]{:S(2)}) collective-permute-start(bf16[320,3,1]{2,0,1:T(8,128)(2,1)S(1)} %copy-done.9), channel_id=1, source_target_pairs={{1,0},{2,1},{3,2},{5,4},{6,5},{7,6},{9,8},{10,9},{11,10},{13,12},{... | collective-permute-start | bytes 5768 | tf_op jit(solution)/shard_map/ppermute | solution.py:60
  260.5 33.9 %copy-start.14 = (f32[320]{0:T(512)S(1)}, f32[320]{0:T(512)}, u32[]{:S(2)}) copy-start(f32[320]{0:T(512)} %param.27) | copy-start | bytes 3844
  294.7 6.2 %collective-permute-start.12 = (bf16[320,1,256]{2,0,1:T(8,128)(2,1)S(1)}, bf16[320,1,256]{2,0,1:T(8,128)(2,1)S(1)}, u32[]{:S(2)}, u32[]{:S(2)}) collective-permute-start(bf16[320,1,256]{2,0,1:T(8,128)(2,1)S(1)} %fusion.61), channel_id=1, source_target_pairs={{0,4},{4,8},{8,12},{12,16},{16,20},{20,24},{24,28},{28,32},{32,36}... | collective-permute-start | bytes 491528 | tf_op jit(solution)/shard_map/ppermute | solution.py:58
  298.6 6.6 %collective-permute-start.13 = (bf16[320,1,256]{2,0,1:T(8,128)(2,1)S(1)}, bf16[320,1,256]{2,0,1:T(8,128)(2,1)S(1)}, u32[]{:S(2)}, u32[]{:S(2)}) collective-permute-start(bf16[320,1,256]{2,0,1:T(8,128)(2,1)S(1)} %fusion.61), channel_id=1, source_target_pairs={{4,0},{8,4},{12,8},{16,12},{20,16},{24,20},{28,24},{32,28},{36,32}... | collective-permute-start | bytes 491528 | tf_op jit(solution)/shard_map/ppermute | solution.py:60
  305.4 5.3 %collective-permute-start.14 = (bf16[320,3,1]{2,0,1:T(8,128)(2,1)S(1)}, bf16[320,3,1]{2,0,1:T(8,128)(2,1)S(1)}, u32[]{:S(2)}, u32[]{:S(2)}) collective-permute-start(bf16[320,3,1]{2,0,1:T(8,128)(2,1)S(1)} %get-tuple-element.14), channel_id=1, source_target_pairs={{0,1},{1,2},{2,3},{4,5},{5,6},{6,7},{8,9},{9,10},{10,11},{12,13},{... | collective-permute-start | bytes 5768 | tf_op jit(solution)/shard_map/ppermute | solution.py:58
  307.6 7.0 %collective-permute-start.15 = (bf16[320,3,1]{2,0,1:T(8,128)(2,1)S(1)}, bf16[320,3,1]{2,0,1:T(8,128)(2,1)S(1)}, u32[]{:S(2)}, u32[]{:S(2)}) collective-permute-start(bf16[320,3,1]{2,0,1:T(8,128)(2,1)S(1)} %get-tuple-element.13), channel_id=1, source_target_pairs={{1,0},{2,1},{3,2},{5,4},{6,5},{7,6},{9,8},{10,9},{11,10},{13,12},{... | collective-permute-start | bytes 5768 | tf_op jit(solution)/shard_map/ppermute | solution.py:60
  (4 other events, 9.3 us)
Sparse Core Ops, SparseCore 0:
  10.4 148.6 all-gather.2
where the time goes:
time: 326 us; the launch traced here: 324 us
  waiting for transfers between devices  102 us (31%)
  starting transfers between devices  78.6 us (24%)
  blocking collectives  71.8 us (22%)
  local copies, waits for them, and re-layouts  26.1 us (8%)
  other arithmetic  16.3 us (5%)
  between operations  14.7 us (5%)
  matrix products  14.4 us (4%)
    all_to_all x5, blocking collectives, from_everyone(): lax.all_to_all(jnp.broadcast_to(x[None], (count, *x.shape)), axis, 0, 0,...  71.8 us
    all_to_all x4, starting transfers between devices, from_everyone(): lax.all_to_all(jnp.broadcast_to(x[None], (count, *x.shape)), axis, 0, 0,...  32.3 us
    ppermute x8, starting transfers between devices, padded_2(): lax.ppermute(tail, axis, [(i, (i + 1) % count) for i in range(ends)])  29.7 us
    ppermute x8, waiting for transfers between devices, padded_2(): lax.ppermute(tail, axis, [(i, (i + 1) % count) for i in range(ends)])  29.2 us
    ppermute x8, waiting for transfers between devices, padded_2(): lax.ppermute(head, axis, [((i + 1) % count, i) for i in range(ends)])  25.8 us
    all_gather x1, waiting for transfers between devices, shards(): lax.all_gather(front_weight, ROWS, axis=0, tiled=True)  24 us
    all_to_all x4, waiting for transfers between devices, from_everyone(): lax.all_to_all(jnp.broadcast_to(x[None], (count, *x.shape)), axis, 0, 0,...  21.9 us
    ppermute x8, starting transfers between devices, padded_2(): lax.ppermute(head, axis, [((i + 1) % count, i) for i in range(ends)])  16.5 us
  transfers between devices with their start and end apart: 21, of which 17 were waited for; matrix products, arithmetic and copies ran while one was open for 10% of the time, Pallas kernels for 0%

commit v1 on v0

v1 whole, which is shorter than its diff:
```python
import math

import jax
import jax.numpy as jnp
from jax import lax
from jax.experimental import pallas as pl
from jax.experimental.pallas import tpu as pltpu
from jax.sharding import Mesh
from jax.sharding import PartitionSpec as P

ROWS = ("zp", "zl", "y", "core")
DEPTH = ("zp", "zl")
PLANE = ("y", "core", "x")
EPS = 1e-05
F32 = jnp.float32
BF16 = jnp.bfloat16
HIGH = lax.Precision.HIGHEST

C = 320
HALF = 160
WIDE = 256
GAP = 16
SEG = WIDE + GAP
IN_ROWS = 8
MID_ROWS = 6
OUT_ROWS = 4
A_LEN = IN_ROWS * SEG + GAP
H_LEN = MID_ROWS * SEG + GAP
B_LEN = OUT_ROWS * SEG + GAP
MERGED = 512
LANES = 384
CHUNK = 48
VMEM = pl.BlockSpec(memory_space=pltpu.VMEM)
SMEM = pl.BlockSpec(memory_space=pltpu.SMEM)


def call(kernel, out_shape, in_specs, scratch=()):
    return pl.pallas_call(
        kernel,
        out_shape=out_shape,
        in_specs=in_specs,
        out_specs=jax.tree.map(lambda _: VMEM, out_shape),
        scratch_shapes=list(scratch),
        compiler_params=pltpu.CompilerParams(vmem_limit_bytes=40 * 1024 * 1024),
    )


def sds(shape, dtype):
    return jax.ShapeDtypeStruct(shape, dtype)


def rows_at(start, size):
    return pl.ds(pl.multiple_of(start, 16), size)


def same_group(n, m, size_n, size_m):
    i = lax.broadcasted_iota(jnp.int32, (n, m), 0)
    j = lax.broadcasted_iota(jnp.int32, (n, m), 1)
    return ((i // size_n) == (j // size_m)).astype(F32)


def exact_dot(a, b):
    return jnp.dot(a, b, preferred_element_type=F32, precision=HIGH)


def tap_dot(a, b):
    return jnp.dot(a, b, preferred_element_type=F32)


def silu_half(h):
    return h + h * jnp.tanh(h)


def pack_kernel(deep_ref, prev_ref, here_ref, next_ref, out_ref, first_ref, last_ref, tall):
    tall[0:C, :] = deep_ref[...].astype(F32)
    tall[C:LANES, :] = jnp.zeros((LANES - C, WIDE), F32)
    for i, ref in enumerate((prev_ref, here_ref, next_ref)):
        tall[C + 4 * i : C + 4 * i + 4, :] = ref[...].astype(F32)
    out = tall[...].T.astype(BF16)
    out_ref[...] = out
    first_ref[...] = out[0:GAP]
    last_ref[...] = out[WIDE - GAP : WIDE]


def skip_of(tail, wpad_ref, lo, hi):
    n = tail.shape[0]
    left = pltpu.roll(tail, 1, 0)[lo:hi].astype(BF16)
    right = pltpu.roll(tail, n - 1, 0)[lo:hi].astype(BF16)
    mid = tail[lo:hi].astype(BF16)
    stacked = jnp.concatenate([left, mid, right], axis=1)
    return tap_dot(stacked, wpad_ref[...]).astype(BF16).astype(F32)


def join(cells, skip):
    lane = lax.broadcasted_iota(jnp.int32, (cells.shape[0], 128), 1)
    mixed = jnp.where(lane < 64, cells[:, 256:384], skip[:, 0:128])
    return jnp.concatenate([cells[:, 0:256], mixed, skip[:, 128:384]], axis=1)


def stats_kernel(cells_ref, left_ref, right_ref, wpad_ref, row_ref, stat_ref):
    sub = lax.broadcasted_iota(jnp.int32, (GAP, LANES), 0)
    gap = jnp.where(sub < 8, right_ref[...].astype(F32), left_ref[...].astype(F32))
    cells = jnp.concatenate([cells_ref[...].astype(F32), gap], axis=0)
    row_ref[...] = cells.astype(BF16)
    skip = skip_of(cells[:, 256:384], wpad_ref, 0, WIDE)
    joined = join(cells[0:WIDE], skip)
    sums = jnp.sum(joined, axis=0, keepdims=True)
    squares = jnp.sum(joined * joined, axis=0, keepdims=True)
    both = jnp.concatenate([sums, squares, jnp.zeros((6, 2 * C), F32)], axis=0)
    stat_ref[...] = exact_dot(both, same_group(2 * C, 128, 20, 1))


def keep_mask(r, first_row, first_col):
    i = lax.broadcasted_iota(jnp.int32, (SEG, 1), 0)
    here = first_row + r
    row = jnp.where(i < 8, here - 1, here)
    col = first_col + jnp.where(i < 8, i + WIDE, i - GAP)
    good = (row >= 0) & (row < 128) & (col >= 0) & (col < 1024)
    return good.astype(F32)


def shift_add(merged_ref, start, size):
    back = merged_ref[pl.ds(start - 1, size), :]
    mid = merged_ref[pl.ds(start, size), :]
    ahead = merged_ref[pl.ds(start + 1, size), :]
    low = back[:, 0:128] + mid[:, 128:256] + ahead[:, 256:384]
    high = (
        back[:, 384:512]
        + pltpu.roll(mid[:, 384:512], 96, 1)
        + pltpu.roll(ahead[:, 384:512], 64, 1)
    )
    return jnp.concatenate([low, high[:, 0:32]], axis=1)


def first_kernel(
    place_ref, rows_ref, stat_ref, wm_ref, wpad_ref, gain_ref, shift_ref,
    hidden_ref, joined_ref, sum_ref,
    raw, act, merged,
):
    first_row, first_col = place_ref[0], place_ref[1]
    order = ((0, 3), (0, 0), (1, 0), (0, 1), (1, 1), (0, 2), (1, 2), (1, 3))
    sub = lax.broadcasted_iota(jnp.int32, (GAP, LANES), 0)
    zeros = jnp.zeros((GAP, LANES), BF16)
    raw[0:GAP, :] = zeros
    raw[GAP + A_LEN : GAP + A_LEN + GAP, :] = zeros
    for r in range(IN_ROWS + 1):
        after = rows_ref[order[r]] if r < IN_ROWS else None
        gap_right = rows_ref[order[r - 1]][WIDE:SEG].astype(F32) if r else jnp.zeros((GAP, LANES), F32)
        gap_left = after[WIDE:SEG].astype(F32) if r < IN_ROWS else gap_right
        raw[GAP + r * SEG : 2 * GAP + r * SEG, :] = jnp.where(sub < 8, gap_right, gap_left).astype(BF16)
        if r < IN_ROWS:
            raw[2 * GAP + r * SEG : GAP + (r + 1) * SEG, :] = after[0:WIDE]

    totals = jnp.sum(stat_ref[...], axis=0, keepdims=True) / (20.0 * 131072.0)
    mean = totals[:, 0:32]
    var = totals[:, 32:64] - mean * mean
    pair = jnp.concatenate([lax.rsqrt(var + EPS), mean, jnp.zeros((6, 32), F32)[:, :]], axis=0)
    spread = exact_dot(pair, same_group(32, 2 * C, 1, 20))
    scale = spread[0:1] * gain_ref[...] * 0.5
    offset = -spread[1:2] * scale

    def one(r, size):
        base = r * SEG
        tail = raw[rows_at(base, size + 2 * GAP), 256:384].astype(F32)
        skip = skip_of(tail, wpad_ref, GAP, GAP + size)
        joined = join(raw[rows_at(base + GAP, size), :].astype(F32), skip)
        values = silu_half(joined * scale + offset) * keep_mask(r, first_row, first_col)[0:size]
        act[rows_at(base, size), :] = values.astype(BF16)
        return joined.astype(BF16)

    def build(r, carry):
        joined = one(r, SEG)

        @pl.when((r >= 2) & (r < 6))
        def _():
            joined_ref[rows_at((r - 2) * SEG, SEG), :] = joined

        @pl.when(r == 6)
        def _():
            joined_ref[4 * SEG : B_LEN, :] = joined[0:GAP]

        return carry

    lax.fori_loop(0, IN_ROWS, build, 0)
    one(IN_ROWS, GAP)

    def conv(start, size):
        taps = [act[rows_at(start + a * SEG, size), :] for a in range(3)]
        merged[rows_at(start + GAP, size), :] = tap_dot(jnp.concatenate(taps, axis=1), wm_ref[...])

    merged[0:GAP, :] = jnp.zeros((GAP, MERGED), F32)
    merged[GAP + H_LEN : GAP + H_LEN + GAP, :] = jnp.zeros((GAP, MERGED), F32)

    def convs(i, carry):
        conv(i * 2 * SEG, 2 * SEG)
        return carry

    lax.fori_loop(0, 3, convs, 0)
    conv(6 * SEG, GAP)

    sums = jnp.zeros((1, HALF), F32)
    squares = jnp.zeros((1, HALF), F32)
    for r in range(MID_ROWS):
        values = shift_add(merged, GAP + r * SEG, SEG) + shift_ref[...]
        hidden_ref[r * SEG : (r + 1) * SEG, :] = values
        if r in (2, 3):
            sums = sums + jnp.sum(values[GAP:], axis=0, keepdims=True)
            squares = squares + jnp.sum(values[GAP:] * values[GAP:], axis=0, keepdims=True)
    hidden_ref[6 * SEG : H_LEN, :] = shift_add(merged, GAP + 6 * SEG, GAP) + shift_ref[...]
    sum_ref[...] = jnp.concatenate([sums, squares], axis=0)


def affine(stat_ref, gain_ref, core):
    both = jnp.sum(stat_ref[...], axis=0)
    found = []
    for which in (0, 1):
        sums = both[2 * which : 2 * which + 2]
        padded = jnp.concatenate([sums, jnp.zeros((6, HALF), F32)], axis=0)
        totals = exact_dot(padded, same_group(HALF, HALF, 10, 10)) / (10.0 * 131072.0)
        mean = totals[0:1]
        scale = lax.rsqrt(totals[1:2] - mean * mean + EPS) * gain_ref[which : which + 1] * 0.5
        found.append((scale, -mean * scale))
    (scale_0, offset_0), (scale_1, offset_1) = found
    first = core == 0
    own = (jnp.where(first, scale_0, scale_1), jnp.where(first, offset_0, offset_1))
    other = (jnp.where(first, scale_1, scale_0), jnp.where(first, offset_1, offset_0))
    return own, other


def second_kernel(
    place_ref, own_ref, other_ref, stat_ref, gain_ref, wm_ref, wskip_ref, joined_ref,
    block_ref, sum_ref,
    act_own, act_other, merged,
):
    first_row, first_col, core = place_ref[0] + 1, place_ref[1], place_ref[2]
    own, other = affine(stat_ref, gain_ref, core)

    def one(r, size):
        mask = keep_mask(r, first_row, first_col)[0:size]
        where = rows_at(r * SEG, size)
        for source, target, (scale, offset) in ((own_ref, act_own, own), (other_ref, act_other, other)):
            target[where, :] = (silu_half(source[where, :] * scale + offset) * mask).astype(BF16)

    def build(r, carry):
        one(r, SEG)
        return carry

    lax.fori_loop(0, MID_ROWS, build, 0)
    one(MID_ROWS, GAP)

    def conv(start, size):
        total = None
        for source, weights in ((act_own, wm_ref[core]), (act_other, wm_ref[1 - core])):
            for a in range(3):
                part = tap_dot(source[rows_at(start + a * SEG, size), :], weights[a * HALF : (a + 1) * HALF])
                total = part if total is None else total + part
        merged[rows_at(start + GAP, size), :] = total

    merged[0:GAP, :] = jnp.zeros((GAP, MERGED), F32)
    merged[GAP + B_LEN : GAP + B_LEN + GAP, :] = jnp.zeros((GAP, MERGED), F32)

    def convs(i, carry):
        conv(i * 2 * SEG, 2 * SEG)
        return carry

    lax.fori_loop(0, 2, convs, 0)
    conv(4 * SEG, GAP)

    sums = jnp.zeros((1, HALF), F32)
    squares = jnp.zeros((1, HALF), F32)
    for r in range(OUT_ROWS + 1):
        size = SEG if r < OUT_ROWS else GAP
        where = slice(r * SEG, r * SEG + size)
        values = shift_add(merged, GAP + r * SEG, size) + tap_dot(joined_ref[where, :], wskip_ref[...])
        block_ref[where, :] = values
        if r in (1, 2):
            sums = sums + jnp.sum(values[GAP:], axis=0, keepdims=True)
            squares = squares + jnp.sum(values[GAP:] * values[GAP:], axis=0, keepdims=True)
    sum_ref[...] = jnp.concatenate([sums, squares], axis=0)


def third_kernel(place_ref, own_ref, other_ref, stat_ref, gain_ref, wout_ref, noise_ref):
    core = place_ref[2]
    first_row, first_col = place_ref[0] + 2 + core, place_ref[1]
    own, other = affine(stat_ref, gain_ref, core)
    parts = []
    for r in range(4):
        size = SEG if r < 3 else GAP
        mask = keep_mask(r, first_row, first_col)[0:size]
        where = rows_at(core * SEG + r * SEG, size)
        total = None
        for source, (scale, offset), which in ((own_ref, own, core), (other_ref, other, 1 - core)):
            act = (silu_half(source[where, :] * scale + offset) * mask).astype(BF16)
            part = tap_dot(act, wout_ref[which])
            total = part if total is None else total + part
        parts.append(total)
    parts.append(jnp.zeros((896 - 3 * SEG - GAP, 128), F32))
    turned = jnp.concatenate(parts, axis=0).T
    noise = None
    for a in range(3):
        for b in range(3):
            tap = 3 * a + b
            at = a * SEG + GAP + b - 1
            piece = turned[8 * tap : 8 * tap + 8, at : at + WIDE]
            noise = piece if noise is None else noise + piece
    noise_ref[...] = noise[0:4]


def place_merged(out_ref, at, size, b, piece):
    out_ref[at : at + size, 128 * b : 128 * (b + 1)] = piece[:, 0:128]
    out_ref[at : at + size, 384 + 32 * b : 384 + 32 * (b + 1)] = piece[:, 128:160]


def front_weight_kernel(found_ref, out_ref):
    out_ref[:, 480:512] = jnp.zeros((3 * 2 * C, 32), BF16)
    for chunk in range(5760 // CHUNK):
        plane, j = divmod(chunk, 15)
        s, q = divmod(plane, 4)
        row = chunk * CHUNK
        end = row + CHUNK
        while row < end:
            tap, channel = divmod(row, 2 * C)
            size = min(end - row, 2 * C - channel)
            a, b = divmod(tap, 3)
            i = row - chunk * CHUNK
            piece = found_ref[j, 48 * s + i : 48 * s + i + size, 160 * q : 160 * (q + 1)]
            place_merged(out_ref, a * 2 * C + channel, size, b, piece)
            row += size


def middle_weight_kernel(found_ref, out_ref, skip_ref):
    out_ref[:, :, 480:512] = jnp.zeros((2, 3 * HALF, 32), BF16)
    for tap in range(9):
        a, b = divmod(tap, 3)
        for half in (0, 1):
            for part in (0, 1):
                row = tap * C + half * HALF + part * 80
                x, i = divmod(row, 720)
                piece = found_ref[x, i : i + 80, :]
                place_merged(out_ref.at[half], a * HALF + part * 80, 80, b, piece)
    for x in range(4):
        skip_ref[x * HALF : (x + 1) * HALF, :] = found_ref[x, 720:880, :]


def from_everyone(x, axis):
    count = lax.axis_size(axis)
    return lax.all_to_all(jnp.broadcast_to(x[None], (count, *x.shape)), axis, 0, 0, tiled=True)


def shifted(x, axis, step):
    count = lax.axis_size(axis)
    return lax.ppermute(x, axis, [(i, i + step) for i in range(count) if 0 <= i + step < count])


def summed_halves(sums):
    near = from_everyone(sums, PLANE).reshape(4, 2, 4, 2, HALF).sum(axis=(0, 2))
    return from_everyone(near.reshape(4, HALF), DEPTH)


def shards(
    latent, deep, timestep, in_weight, front_weight, middle_weight, skip_weight, out_weight,
    time_weight, time_second, time_proj, input_gain, middle_gain, output_gain,
):
    core, x, y = lax.axis_index("core"), lax.axis_index("x"), lax.axis_index("y")
    chip_row = 2 * (lax.axis_index(("zp", "zl", "y")))
    place = jnp.stack([chip_row - 3, x * WIDE, core]).astype(jnp.int32)

    halves = front_weight.reshape(45, 2, HALF).transpose(1, 0, 2)
    spread = jnp.broadcast_to(halves[None], (8, 2, 45, HALF)).reshape(16, 45, HALF)
    planes = lax.all_to_all(spread, ("zl", "y", "core"), 0, 0, tiled=True).reshape(720, HALF)
    planes = jnp.pad(planes, ((0, CHUNK), (0, 0)))
    mine = lax.dynamic_slice_in_dim(planes, CHUNK * (4 * y + x), CHUNK, 0)
    deepest = from_everyone(mine, "zp")
    dense = deepest.reshape(2, 4, CHUNK, HALF).transpose(0, 2, 1, 3).reshape(2 * CHUNK, 4 * HALF)
    front_found = lax.all_gather(dense, ("y", "x"), axis=0)

    wpad = in_weight.reshape(3, 3, 4, C).transpose(1, 0, 2, 3).reshape(3, 12, C)
    wpad = jnp.pad(wpad, ((0, 0), (64, 52), (64, 0))).reshape(LANES, LANES)
    above, below = shifted(latent, ROWS, 1), shifted(latent, ROWS, -1)
    cells, first, last = call(
        pack_kernel,
        (sds((WIDE, LANES), BF16), sds((GAP, LANES), BF16), sds((GAP, LANES), BF16)),
        [VMEM] * 4,
        [pltpu.VMEM((LANES, WIDE), F32)],
    )(deep.reshape(C, WIDE), above.reshape(4, WIDE), latent.reshape(4, WIDE), below.reshape(4, WIDE))
    from_right, from_left = shifted(first, "x", -1), shifted(last, "x", 1)
    row, stats = call(stats_kernel, (sds((SEG, LANES), BF16), sds((8, 128), F32)), [VMEM] * 4)(
        cells, from_left, from_right, wpad
    )

    count = lax.axis_size(ROWS)
    crossed = [(i, i + 3) if i % 2 else (i, i - 3) for i in range(count)]
    crossed = [(i, j) for i, j in crossed if 0 <= j < count]
    around = jnp.stack([shifted(row, ROWS, 2), row, shifted(row, ROWS, -2), lax.ppermute(row, ROWS, crossed)])
    rows = lax.all_gather(around, "core", axis=0)

    half_width = time_weight.shape[0] // 2
    ratios = jnp.exp(-math.log(10000.0) * jnp.arange(half_width, dtype=F32) / half_width)
    angles = timestep[0].astype(F32) * ratios
    features = jnp.concatenate([jnp.cos(angles), jnp.sin(angles)])
    depth_here = time_second.shape[0]
    weight_here = lax.dynamic_slice_in_dim(time_weight, x * depth_here, depth_here, 1)
    hidden = jax.nn.silu(jnp.dot(features, weight_here.astype(F32), precision=HIGH))
    columns = lax.dynamic_slice_in_dim(time_second, (2 * y + core) * HALF, HALF, 1)
    partial = jnp.dot(hidden, columns.astype(F32), precision=HIGH)

    sent = jnp.concatenate([stats[0, 0:32], stats[1, 0:32], partial])
    near = from_everyone(sent[None], PLANE).reshape(8, 4, 224)
    embedded = jax.nn.silu(near[:, :, 64:].sum(axis=1).reshape(8 * HALF))
    proj = lax.dynamic_slice_in_dim(time_proj, core * HALF, HALF, 1)
    time_shift = jnp.dot(embedded, proj.astype(F32), precision=HIGH)
    wide = from_everyone(near[:, :, 0:64].sum(axis=(0, 1))[None], DEPTH).reshape(16, 64)

    front = call(front_weight_kernel, sds((3 * 2 * C, MERGED), BF16), [VMEM])(front_found)
    hidden_own, joined, sums = call(
        first_kernel,
        (sds((H_LEN, HALF), F32), sds((B_LEN, 2 * C), BF16), sds((2, HALF), F32)),
        [SMEM] + [VMEM] * 6,
        [
            pltpu.VMEM((A_LEN + 2 * GAP, LANES), BF16),
            pltpu.VMEM((A_LEN, 2 * C), BF16),
            pltpu.VMEM((H_LEN + 2 * GAP, MERGED), F32),
        ],
    )(place, rows, wide, front, wpad, input_gain[None], time_shift[None])

    both = jnp.concatenate([middle_weight, skip_weight], axis=0).reshape(880, 2, HALF)
    kept = lax.dynamic_slice_in_dim(both, core, 1, 1).reshape(880, HALF)
    kept, front_found = lax.optimization_barrier((kept, front_found))
    middle_found = lax.all_gather(kept, "x", axis=0)
    middle, shortcut = call(
        middle_weight_kernel,
        (sds((2, 3 * HALF, MERGED), BF16), sds((2 * C, HALF), BF16)),
        [VMEM],
    )(middle_found)

    swap = [(0, 1), (1, 0)]
    hidden_other = lax.ppermute(hidden_own, "core", swap)
    block_own, sums = call(
        second_kernel,
        (sds((B_LEN, HALF), F32), sds((2, HALF), F32)),
        [SMEM] + [VMEM] * 7,
        [
            pltpu.VMEM((H_LEN, HALF), BF16),
            pltpu.VMEM((H_LEN, HALF), BF16),
            pltpu.VMEM((B_LEN + 2 * GAP, MERGED), F32),
        ],
    )(place, hidden_own, hidden_other, summed_halves(sums), middle_gain.reshape(2, HALF), middle, shortcut, joined)

    wout = out_weight.reshape(9, 2, HALF, 4).transpose(1, 2, 0, 3)
    wout = jnp.pad(jnp.pad(wout, ((0, 0), (0, 0), (0, 0), (0, 4))).reshape(2, HALF, 72), ((0, 0), (0, 0), (0, 56)))
    block_other = lax.ppermute(block_own, "core", swap)
    noise = call(third_kernel, sds((4, WIDE), F32), [SMEM] + [VMEM] * 5)(
        place, block_own, block_other, summed_halves(sums), output_gain.reshape(2, HALF), wout
    )
    return noise.reshape(4, 1, WIDE)


def solution(mesh):
    finer = Mesh(
        mesh.devices.reshape(8, 2, 4, 2, mesh.shape["cols"]), ("zp", "zl", "y", "core", "x")
    )
    in_specs = (
        P(None, ROWS, "x"),
        P(None, ROWS, "x"),
        P(),
        P(),
        P(ROWS, None),
        P("x", None),
        P("x", None),
        P(),
        P(),
        P("x", None),
        P(),
        P(),
        P(),
        P(),
    )
    return jax.shard_map(
        shards, mesh=finer, in_specs=in_specs, out_specs=P(None, ROWS, "x"), check_vma=False
    )
```

time: 326 us -> 244 us (0.75)
  waiting for transfers between devices: 102 us -> 55.2 us
  blocking collectives: 71.8 us -> 48.7 us
  Pallas kernels: 0 us -> 17.9 us
  other arithmetic: 16.3 us -> 1.73 us
  matrix products: 14.4 us -> 1.89 us
    ppermute x16 -> x9, waiting for transfers between devices: 55 us -> 9.91 us  [the longest x6 9.9 us: shifted(): lax.ppermute(x, axis, [(i, i + step) for i in range(count) if 0 <= i + st...]
    all_to_all x5 -> x3, blocking collectives: 71.8 us -> 48.7 us  [from_everyone(): lax.all_to_all(jnp.broadcast_to(x[None], (count, *x.shape)), axis, 0, 0,...]
    all_gather x1 -> x3, waiting for transfers between devices: 24 us -> 5.07 us  [the longest x1 4.93 us: shards(): front_found = lax.all_gather(dense, ('y', 'x'), axis=0)]
    pallas_call x0 -> x7, Pallas kernels: none -> 17.9 us  [the longest x1 9.43 us: shards(): call(first_kernel, (sds((H_LEN, HALF), F32), sds((B_LEN, 2 * C), BF16), s...]
    ppermute x16 -> x9, starting transfers between devices: 46.3 us -> 31.2 us  [the longest x6 17.8 us: shifted(): lax.ppermute(x, axis, [(i, i + step) for i in range(count) if 0 <= i + st...]
    dot_general x8 -> x3, matrix products: 14.4 us -> 1.89 us  [the longest x1 1.17 us: shards(): partial = jnp.dot(hidden, columns.astype(F32), precision=HIGH)]
    unnamed x23 -> x0, other arithmetic: 10.4 us -> none
    all_to_all x0 -> x1, starting transfers between devices: none -> 10.2 us  [shards(): lax.all_to_all(spread, ('zl', 'y', 'core'), 0, 0, tiled=True)]
  transfers between devices with their start and end apart: 21 -> 17, of which waited for: 17 -> 10; matrix products, arithmetic and copies ran while one was open for 10% -> 6% of each run, Pallas kernels for 0% -> 5%
where the time goes in v1:
time: 244 us; the launch traced here: 243 us
  starting transfers between devices  76.8 us (31%)
  waiting for transfers between devices  55.2 us (23%)
  blocking collectives  48.7 us (20%)
  local copies, waits for them, and re-layouts  26.6 us (11%)
  Pallas kernels  17.9 us (7%)
  between operations  14.3 us (6%)
    all_to_all x3, blocking collectives, from_everyone(): lax.all_to_all(jnp.broadcast_to(x[None], (count, *x.shape)), axis, 0, 0,...  48.7 us
    all_to_all x4, starting transfers between devices, from_everyone(): lax.all_to_all(jnp.broadcast_to(x[None], (count, *x.shape)), axis, 0, 0,...  35.3 us
    all_to_all x4, waiting for transfers between devices, from_everyone(): lax.all_to_all(jnp.broadcast_to(x[None], (count, *x.shape)), axis, 0, 0,...  31.8 us
    ppermute x6, starting transfers between devices, shifted(): lax.ppermute(x, axis, [(i, i + step) for i in range(count) if 0 <= i + st...  17.8 us
    unnamed x42, local copies, waits for them, and re-layouts  12 us
    all_to_all x1, starting transfers between devices, shards(): lax.all_to_all(spread, ('zl', 'y', 'core'), 0, 0, tiled=True)  10.2 us
    ppermute x6, waiting for transfers between devices, shifted(): lax.ppermute(x, axis, [(i, i + step) for i in range(count) if 0 <= i + st...  9.9 us
    pallas_call x1, Pallas kernels, shards(): call(first_kernel, (sds((H_LEN, HALF), F32), sds((B_LEN, 2 * C), BF16), s...  9.43 us
  transfers between devices with their start and end apart: 17, of which 10 were waited for; matrix products, arithmetic and copies ran while one was open for 6% of the time, Pallas kernels for 5%

profile of v1, /device:TPU:1, one launch (start us, length us, event | category | flops | bytes accessed | tf_op | source)
XLA Modules:
  0.0 243.2 jit_solution(16419715515677662604)
XLA Ops:
  8.3 10.2 %all-to-all-start.2 = ((bf16[16,45,160]{2,1,0:T(8,128)(2,1)}), bf16[16,45,160]{2,1,0:T(8,128)(2,1)S(1)}, u32[]{:S(2)}, u32[]{:S(2)}) async-start(bf16[16,45,160]{2,1,0:T(8,128)(2,1)} %bitcast.20), calls=%async_computation.2 | async-start | bytes 786432 | tf_op jit(solution)/shard_map/all_to_all | solution.py:370
  18.6 8.4 %all-to-all-done.2 = bf16[16,45,160]{2,1,0:T(8,128)(2,1)S(1)} async-done(((bf16[16,45,160]{2,1,0:T(8,128)(2,1)}), bf16[16,45,160]{2,1,0:T(8,128)(2,1)S(1)}, u32[]{:S(2)}, u32[]{:S(2)}) %all-to-all-start.2) | async-done | bytes 230432 | tf_op jit(solution)/shard_map/all_to_all | solution.py:370
  27.2 25.6 %all_to_all.40 = bf16[8,48,160]{2,1,0:T(8,128)(2,1)S(1)} all-to-all(bf16[8,48,160]{2,1,0:T(8,128)(2,1)S(1)} %broadcast_in_dim.27), channel_id=1, replica_groups=mesh['zp'=8,'zl'=2,'y'=4,'core'=2,'x'=4] {'zp'}, dimensions={0} | all-to-all | bytes 245760 | tf_op jit(solution)/shard_map/all_to_all | solution.py:347
  53.9 5.6 %collective-permute-start = (bf16[4,1,256]{2,0,1:T(4,128)(2,1)S(1)}, bf16[4,1,256]{2,0,1:T(4,128)(2,1)S(1)}, u32[]{:S(2)}, u32[]{:S(2)}) collective-permute-start(bf16[4,1,256]{2,0,1:T(4,128)(2,1)S(1)} %copy-done.11), channel_id=1, source_target_pairs={{0,4},{4,8},{8,12},{12,16},{16,20},{20,24},{24,28},{28,32},{32,36}... | collective-permute-start | bytes 6152 | tf_op jit(solution)/shard_map/ppermute | solution.py:352
  59.4 2.5 %collective-permute-start.1 = (bf16[4,1,256]{2,0,1:T(4,128)(2,1)S(1)}, bf16[4,1,256]{2,0,1:T(4,128)(2,1)S(1)}, u32[]{:S(2)}, u32[]{:S(2)}) collective-permute-start(bf16[4,1,256]{2,0,1:T(4,128)(2,1)S(1)} %copy-done.11), channel_id=1, source_target_pairs={{4,0},{8,4},{12,8},{16,12},{20,16},{24,20},{28,24},{32,28},{36,32}... | collective-permute-start | bytes 6152 | tf_op jit(solution)/shard_map/ppermute | solution.py:352
  62.0 2.4 collective-permute-done.1
  64.5 3.1 %collective-permute-start.2 = (bf16[16,384]{1,0:T(8,128)(2,1)S(1)}, bf16[16,384]{1,0:T(8,128)(2,1)S(1)}, u32[]{:S(2)}, u32[]{:S(2)}) collective-permute-start(bf16[16,384]{1,0:T(8,128)(2,1)S(1)} %get-tuple-element.19), channel_id=1, source_target_pairs={{0,1},{1,2},{2,3},{4,5},{5,6},{6,7},{8,9},{9,10},{10,11},{12,13},{... | collective-permute-start | bytes 36872 | tf_op jit(solution)/shard_map/ppermute | solution.py:352
  69.1 3.0 %collective-permute-done.3.right_ref = bf16[16,384]{1,0:T(8,128)(2,1)S(1)} collective-permute-done((bf16[16,384]{1,0:T(8,128)(2,1)S(1)}, bf16[16,384]{1,0:T(8,128)(2,1)S(1)}, u32[]{:S(2)}, u32[]{:S(2)}) %collective-permute-start.3) | collective-permute-done | bytes 12320 | tf_op jit(solution)/shard_map/ppermute | solution.py:352
  72.6 4.7 %collective-permute-start.6 = (bf16[272,384]{1,0:T(8,128)(2,1)S(1)}, bf16[272,384]{1,0:T(8,128)(2,1)S(1)}, u32[]{:S(2)}, u32[]{:S(2)}) collective-permute-start(bf16[272,384]{1,0:T(8,128)(2,1)S(1)} %get-tuple-element.21), channel_id=1, source_target_pairs={{4,16},{12,24},{16,4},{20,32},{24,12},{28,40},{32,20},{36,48},{40,... | collective-permute-start | bytes 626696 | tf_op jit(solution)/shard_map/ppermute | solution.py:394
  78.6 4.0 %collective-permute-start.4 = (bf16[272,384]{1,0:T(8,128)(2,1)S(1)}, bf16[272,384]{1,0:T(8,128)(2,1)S(1)}, u32[]{:S(2)}, u32[]{:S(2)}) collective-permute-start(bf16[272,384]{1,0:T(8,128)(2,1)S(1)} %get-tuple-element.21), channel_id=1, source_target_pairs={{0,8},{4,12},{8,16},{12,20},{16,24},{20,28},{24,32},{28,36},{32,40... | collective-permute-start | bytes 626696 | tf_op jit(solution)/shard_map/ppermute | solution.py:352
  82.6 4.6 %collective-permute-done.5 = bf16[272,384]{1,0:T(8,128)(2,1)S(1)} collective-permute-done((bf16[272,384]{1,0:T(8,128)(2,1)S(1)}, bf16[272,384]{1,0:T(8,128)(2,1)S(1)}, u32[]{:S(2)}, u32[]{:S(2)}) %collective-permute-start.5) | collective-permute-done | bytes 208928 | tf_op jit(solution)/shard_map/ppermute | solution.py:352
  92.4 9.1 %all-to-all-start = ((f32[32,1,224]{2,1,0:T(1,128)}), f32[32,1,224]{2,1,0:T(1,128)S(1)}, u32[]{:S(2)}, u32[]{:S(2)}) async-start(f32[32,1,224]{2,1,0:T(1,128)} %broadcast_in_dim.24), calls=%async_computation | async-start | bytes 65536 | tf_op jit(solution)/shard_map/all_to_all | solution.py:347
  101.7 7.1 %all-to-all-done = f32[32,1,224]{2,1,0:T(1,128)S(1)} async-done(((f32[32,1,224]{2,1,0:T(1,128)}), f32[32,1,224]{2,1,0:T(1,128)S(1)}, u32[]{:S(2)}, u32[]{:S(2)}) %all-to-all-start) | async-done | bytes 28704 | tf_op jit(solution)/shard_map/all_to_all | solution.py:347
  108.9 4.9 %all-gather.7.cloned.1.call-done.found_ref = bf16[16,96,640]{2,1,0:T(8,128)(2,1)} async-done(((bf16[1,96,640]{2,1,0:T(8,128)(2,1)}), bf16[16,96,640]{2,1,0:T(8,128)(2,1)}) %all-gather.7.cloned.1.call-update) | async-done | bytes 1966096 | tf_op jit(solution)/shard_map/all_gather | solution.py:375
  114.7 11.9 %all-to-all-start.1 = ((f32[16,1,64]{2,1,0:T(1,128)}), f32[16,1,64]{2,1,0:T(1,128)S(1)}, u32[]{:S(2)}, u32[]{:S(2)}) async-start(f32[16,1,64]{2,1,0:T(1,128)} %broadcast_in_dim.25), calls=%async_computation.1 | async-start | bytes 16384 | tf_op jit(solution)/shard_map/all_to_all | solution.py:347
  127.0 1.6 copy-done.4
  129.7 8.1 %all-to-all-done.1 = f32[16,1,64]{2,1,0:T(1,128)S(1)} async-done(((f32[16,1,64]{2,1,0:T(1,128)}), f32[16,1,64]{2,1,0:T(1,128)S(1)}, u32[]{:S(2)}, u32[]{:S(2)}) %all-to-all-start.1) | async-done | bytes 4128 | tf_op jit(solution)/shard_map/all_to_all | solution.py:347
  139.4 9.4 %shard_map.139 = (f32[1648,160]{1,0:T(8,128)S(1)}, bf16[1104,640]{1,0:T(8,128)(2,1)S(1)}, f32[2,160]{1,0:T(2,128)S(1)}) custom-call(s32[3]{0:T(128)S(1)} %pad_add_fusion.place_ref, bf16[2,4,272,384]{3,2,1,0:T(8,128)(2,1)S(1)} %bitcast.44, f32[16,64]{1,0:T(8,128)S(1)} %bitcast.47, bf16[1920,512]{1,0:T(8,128)(2,1)S(1)} %shard_map.138.wm_ref, ...), custom_call_target="tpu_custom_call" | custom-call | tf_op jit(solution)/shard_map/pallas_call | solution.py:415
  151.2 1.9 copy.92
  153.1 4.7 %collective-permute-start.7 = (f32[1648,160]{0,1:T(8,128)S(1)}, f32[1648,160]{0,1:T(8,128)S(1)}, u32[]{:S(2)}, u32[]{:S(2)}) collective-permute-start(f32[1648,160]{0,1:T(8,128)S(1)} %copy.92), channel_id=1, source_target_pairs={{0,4},{4,0},{1,5},{5,1},{2,6},{6,2},{3,7},{7,3},{8,12},{12,8},{9,1... | collective-permute-start | bytes 3164168 | tf_op jit(solution)/shard_map/ppermute | solution.py:437
  157.8 12.4 %all_to_all.41 = f32[32,2,160]{2,1,0:T(2,128)S(1)} all-to-all(f32[32,2,160]{2,1,0:T(2,128)S(1)} %broadcast_in_dim.60), channel_id=1, replica_groups=mesh['zp'=8,'zl'=2,'y'=4,'core'=2,'x'=4] {'y','core','x'}, dimensions={0} | all-to-all | bytes 81920 | tf_op jit(solution)/shard_map/all_to_all | solution.py:347
  171.0 10.5 %all-to-all-start.5 = ((f32[16,4,160]{2,1,0:T(4,128)}), f32[16,4,160]{2,1,0:T(4,128)S(1)}, u32[]{:S(2)}, u32[]{:S(2)}) async-start(f32[16,4,160]{2,1,0:T(4,128)} %broadcast_in_dim.62), calls=%async_computation.5 | async-start | bytes 131072 | tf_op jit(solution)/shard_map/all_to_all | solution.py:347
  181.6 1.7 copy.96.other_ref
  183.3 1.7 copy.95.found_ref
  186.3 6.8 %all-to-all-done.5.stat_ref = f32[16,4,160]{2,1,0:T(4,128)S(1)} async-done(((f32[16,4,160]{2,1,0:T(4,128)}), f32[16,4,160]{2,1,0:T(4,128)S(1)}, u32[]{:S(2)}, u32[]{:S(2)}) %all-to-all-start.5) | async-done | bytes 40992 | tf_op jit(solution)/shard_map/all_to_all | solution.py:347
  198.6 4.7 %shard_map.141 = (f32[1104,160]{1,0:T(8,128)S(1)}, f32[2,160]{1,0:T(2,128)S(1)}) custom-call(s32[3]{0:T(128)S(1)} %pad_add_fusion.place_ref, f32[1648,160]{1,0:T(8,128)S(1)} %copy-done.2, f32[1648,160]{1,0:T(8,128)S(1)} %copy-done.3, f32[16,4,160]{2,1,0:T(4,128)S(1)} %all-to-all-done.5.stat_ref, f32[2,160]{1,0:T(2,128)S(1)} %reshape.97.gain_ref, ...), custom_call_target="tpu_custom_call" | custom-call | tf_op jit(solution)/shard_map/pallas_call | solution.py:438
  203.7 4.0 %collective-permute-start.8 = (f32[1104,160]{0,1:T(8,128)S(1)}, f32[1104,160]{0,1:T(8,128)}, u32[]{:S(2)}, u32[]{:S(2)}) collective-permute-start(f32[1104,160]{0,1:T(8,128)S(1)} %copy.97), channel_id=1, source_target_pairs={{0,4},{4,0},{1,5},{5,1},{2,6},{6,2},{3,7},{7,3},{8,12},{12,8},{9,1... | collective-permute-start | bytes 2119688 | tf_op jit(solution)/shard_map/ppermute | solution.py:451
  207.7 10.7 %all_to_all.42 = f32[32,2,160]{2,1,0:T(2,128)S(1)} all-to-all(f32[32,2,160]{2,1,0:T(2,128)S(1)} %broadcast_in_dim.63), channel_id=1, replica_groups=mesh['zp'=8,'zl'=2,'y'=4,'core'=2,'x'=4] {'y','core','x'}, dimensions={0} | all-to-all | bytes 81920 | tf_op jit(solution)/shard_map/all_to_all | solution.py:347
  219.1 3.7 %all-to-all-start.7 = ((f32[16,4,160]{2,1,0:T(4,128)}), f32[16,4,160]{2,1,0:T(4,128)S(1)}, u32[]{:S(2)}, u32[]{:S(2)}) async-start(f32[16,4,160]{2,1,0:T(4,128)} %broadcast_in_dim.65), calls=%async_computation.7 | async-start | bytes 131072 | tf_op jit(solution)/shard_map/all_to_all | solution.py:347
  223.3 1.5 copy.101.other_ref
  224.8 9.7 %all-to-all-done.7.stat_ref = f32[16,4,160]{2,1,0:T(4,128)S(1)} async-done(((f32[16,4,160]{2,1,0:T(4,128)}), f32[16,4,160]{2,1,0:T(4,128)S(1)}, u32[]{:S(2)}, u32[]{:S(2)}) %all-to-all-start.7) | async-done | bytes 40992 | tf_op jit(solution)/shard_map/all_to_all | solution.py:347
  234.5 1.6 shard_map.142
  (113 shorter events, 26.9 us)
Async XLA Ops:
  6.5 82.6 %copy-start = (bf16[320,1280]{1,0:T(8,128)(2,1)S(1)}, bf16[320,1280]{1,0:T(8,128)(2,1)}, u32[]{:S(2)}) copy-start(bf16[320,1280]{1,0:T(8,128)(2,1)} %param.22) | copy-start | bytes 2457604
  8.3 18.7 %all-to-all-start.2 = ((bf16[16,45,160]{2,1,0:T(8,128)(2,1)}), bf16[16,45,160]{2,1,0:T(8,128)(2,1)S(1)}, u32[]{:S(2)}, u32[]{:S(2)}) async-start(bf16[16,45,160]{2,1,0:T(8,128)(2,1)} %bitcast.20), calls=%async_computation.2 | async-start | bytes 786432 | tf_op jit(solution)/shard_map/all_to_all | solution.py:370
  18.5 95.3 %all-gather.7.cloned.1.call-start = ((), (), s32[]{:S(2)}) async-start(), calls=%async_computation.8 | async-start | bytes 2088960 | tf_op jit(solution)/shard_map/all_gather | solution.py:375
  18.6 35.3 %copy-start.11 = (bf16[4,1,256]{2,0,1:T(4,128)(2,1)S(1)}, bf16[4,1,256]{2,0,1:T(4,128)(2,1)}, u32[]{:S(2)}) copy-start(bf16[4,1,256]{2,0,1:T(4,128)(2,1)} %param.14) | copy-start | bytes 6148
  18.6 45.7 %copy-start.10 = (bf16[320,1,256]{2,0,1:T(8,128)(2,1)S(1)}, bf16[320,1,256]{2,0,1:T(8,128)(2,1)}, u32[]{:S(2)}) copy-start(bf16[320,1,256]{2,0,1:T(8,128)(2,1)} %param.15) | copy-start | bytes 491524
  27.2 41.7 %copy-start.15 = (bf16[36,320]{1,0:T(8,128)(2,1)S(1)}, bf16[36,320]{1,0:T(8,128)(2,1)}, u32[]{:S(2)}) copy-start(bf16[36,320]{1,0:T(8,128)(2,1)} %param.17) | copy-start | bytes 69124
  53.8 84.2 %all-gather.9.cloned.1.call-start = ((), (), s32[]{:S(2)}) async-start(), calls=%async_computation.9 | async-start | bytes 2506752 | tf_op jit(solution)/shard_map/all_gather | solution.py:395
  53.9 8.1 %collective-permute-start = (bf16[4,1,256]{2,0,1:T(4,128)(2,1)S(1)}, bf16[4,1,256]{2,0,1:T(4,128)(2,1)S(1)}, u32[]{:S(2)}, u32[]{:S(2)}) collective-permute-start(bf16[4,1,256]{2,0,1:T(4,128)(2,1)S(1)} %copy-done.11), channel_id=1, source_target_pairs={{0,4},{4,8},{8,12},{12,16},{16,20},{20,24},{24,28},{28,32},{32,36}... | collective-permute-start | bytes 6152 | tf_op jit(solution)/shard_map/ppermute | solution.py:352
  59.4 4.9 %collective-permute-start.1 = (bf16[4,1,256]{2,0,1:T(4,128)(2,1)S(1)}, bf16[4,1,256]{2,0,1:T(4,128)(2,1)S(1)}, u32[]{:S(2)}, u32[]{:S(2)}) collective-permute-start(bf16[4,1,256]{2,0,1:T(4,128)(2,1)S(1)} %copy-done.11), channel_id=1, source_target_pairs={{4,0},{8,4},{12,8},{16,12},{20,16},{24,20},{28,24},{32,28},{36,32}... | collective-permute-start | bytes 6152 | tf_op jit(solution)/shard_map/ppermute | solution.py:352
  64.5 4.6 %collective-permute-start.2 = (bf16[16,384]{1,0:T(8,128)(2,1)S(1)}, bf16[16,384]{1,0:T(8,128)(2,1)S(1)}, u32[]{:S(2)}, u32[]{:S(2)}) collective-permute-start(bf16[16,384]{1,0:T(8,128)(2,1)S(1)} %get-tuple-element.19), channel_id=1, source_target_pairs={{0,1},{1,2},{2,3},{4,5},{5,6},{6,7},{8,9},{9,10},{10,11},{12,13},{... | collective-permute-start | bytes 36872 | tf_op jit(solution)/shard_map/ppermute | solution.py:352
  67.6 4.4 %collective-permute-start.3 = (bf16[16,384]{1,0:T(8,128)(2,1)S(1)}, bf16[16,384]{1,0:T(8,128)(2,1)S(1)}, u32[]{:S(2)}, u32[]{:S(2)}) collective-permute-start(bf16[16,384]{1,0:T(8,128)(2,1)S(1)} %get-tuple-element.20), channel_id=1, source_target_pairs={{1,0},{2,1},{3,2},{5,4},{6,5},{7,6},{9,8},{10,9},{11,10},{13,12},{... | collective-permute-start | bytes 36872 | tf_op jit(solution)/shard_map/ppermute | solution.py:352
  72.6 10.0 %collective-permute-start.6 = (bf16[272,384]{1,0:T(8,128)(2,1)S(1)}, bf16[272,384]{1,0:T(8,128)(2,1)S(1)}, u32[]{:S(2)}, u32[]{:S(2)}) collective-permute-start(bf16[272,384]{1,0:T(8,128)(2,1)S(1)} %get-tuple-element.21), channel_id=1, source_target_pairs={{4,16},{12,24},{16,4},{20,32},{24,12},{28,40},{32,20},{36,48},{40,... | collective-permute-start | bytes 626696 | tf_op jit(solution)/shard_map/ppermute | solution.py:394
  77.3 9.9 %collective-permute-start.5 = (bf16[272,384]{1,0:T(8,128)(2,1)S(1)}, bf16[272,384]{1,0:T(8,128)(2,1)S(1)}, u32[]{:S(2)}, u32[]{:S(2)}) collective-permute-start(bf16[272,384]{1,0:T(8,128)(2,1)S(1)} %get-tuple-element.21), channel_id=1, source_target_pairs={{8,0},{12,4},{16,8},{20,12},{24,16},{28,20},{32,24},{36,28},{40,32... | collective-permute-start | bytes 626696 | tf_op jit(solution)/shard_map/ppermute | solution.py:352
  78.6 8.6 %collective-permute-start.4 = (bf16[272,384]{1,0:T(8,128)(2,1)S(1)}, bf16[272,384]{1,0:T(8,128)(2,1)S(1)}, u32[]{:S(2)}, u32[]{:S(2)}) collective-permute-start(bf16[272,384]{1,0:T(8,128)(2,1)S(1)} %get-tuple-element.21), channel_id=1, source_target_pairs={{0,8},{4,12},{8,16},{12,20},{16,24},{20,28},{24,32},{28,36},{32,40... | collective-permute-start | bytes 626696 | tf_op jit(solution)/shard_map/ppermute | solution.py:352
  87.2 2.3 copy-start.14
  88.2 1.4 copy-start.12
  89.5 12.2 %copy-start.17 = (f32[640]{0:T(1024)S(1)}, f32[640]{0:T(1024)}, u32[]{:S(2)}) copy-start(f32[640]{0:T(1024)} %param.25) | copy-start | bytes 7684
  89.7 36.9 %copy-start.13 = (bf16[1280,320]{0,1:T(8,128)(2,1)S(1)}, bf16[1280,320]{0,1:T(8,128)(2,1)}, u32[]{:S(2)}) copy-start(bf16[1280,320]{0,1:T(8,128)(2,1)} %param.24) | copy-start | bytes 2457604
  92.4 16.4 %all-to-all-start = ((f32[32,1,224]{2,1,0:T(1,128)}), f32[32,1,224]{2,1,0:T(1,128)S(1)}, u32[]{:S(2)}, u32[]{:S(2)}) async-start(f32[32,1,224]{2,1,0:T(1,128)} %broadcast_in_dim.24), calls=%async_computation | async-start | bytes 65536 | tf_op jit(solution)/shard_map/all_to_all | solution.py:347
  101.5 81.8 %all-gather.11.cloned.1.call-start = ((), (), s32[]{:S(2)}) async-start(), calls=%async_computation.10 | async-start | bytes 1433600 | tf_op jit(solution)/shard_map/all_gather | solution.py:429
  114.7 23.2 %all-to-all-start.1 = ((f32[16,1,64]{2,1,0:T(1,128)}), f32[16,1,64]{2,1,0:T(1,128)S(1)}, u32[]{:S(2)}, u32[]{:S(2)}) async-start(f32[16,1,64]{2,1,0:T(1,128)} %broadcast_in_dim.25), calls=%async_computation.1 | async-start | bytes 16384 | tf_op jit(solution)/shard_map/all_to_all | solution.py:347
  127.0 1.6 copy-start.4
  138.0 1.4 copy-start.5
  151.2 30.4 %copy-start.18 = (f32[320]{0:T(512)S(1)}, f32[320]{0:T(512)}, u32[]{:S(2)}) copy-start(f32[320]{0:T(512)} %param.26) | copy-start | bytes 3844
  153.1 28.5 %collective-permute-start.7 = (f32[1648,160]{0,1:T(8,128)S(1)}, f32[1648,160]{0,1:T(8,128)S(1)}, u32[]{:S(2)}, u32[]{:S(2)}) collective-permute-start(f32[1648,160]{0,1:T(8,128)S(1)} %copy.92), channel_id=1, source_target_pairs={{0,4},{4,0},{1,5},{5,1},{2,6},{6,2},{3,7},{7,3},{8,12},{12,8},{9,1... | collective-permute-start | bytes 3164168 | tf_op jit(solution)/shard_map/ppermute | solution.py:437
  171.0 22.2 %all-to-all-start.5 = ((f32[16,4,160]{2,1,0:T(4,128)}), f32[16,4,160]{2,1,0:T(4,128)S(1)}, u32[]{:S(2)}, u32[]{:S(2)}) async-start(f32[16,4,160]{2,1,0:T(4,128)} %broadcast_in_dim.62), calls=%async_computation.5 | async-start | bytes 131072 | tf_op jit(solution)/shard_map/all_to_all | solution.py:347
  193.2 1.4 copy-start.2
  194.6 1.4 copy-start.3
  203.4 19.5 %copy-start.19 = (f32[320]{0:T(512)S(1)}, f32[320]{0:T(512)}, u32[]{:S(2)}) copy-start(f32[320]{0:T(512)} %param.27) | copy-start | bytes 3844
  203.4 19.6 %copy-start.16 = (bf16[2880,4]{0,1:T(4,128)(2,1)S(1)}, bf16[2880,4]{0,1:T(4,128)(2,1)}, u32[]{:S(2)}) copy-start(bf16[2880,4]{0,1:T(4,128)(2,1)} %param.21) | copy-start | bytes 69124
  203.7 19.5 %collective-permute-start.8 = (f32[1104,160]{0,1:T(8,128)S(1)}, f32[1104,160]{0,1:T(8,128)}, u32[]{:S(2)}, u32[]{:S(2)}) collective-permute-start(f32[1104,160]{0,1:T(8,128)S(1)} %copy.97), channel_id=1, source_target_pairs={{0,4},{4,0},{1,5},{5,1},{2,6},{6,2},{3,7},{7,3},{8,12},{12,8},{9,1... | collective-permute-start | bytes 2119688 | tf_op jit(solution)/shard_map/ppermute | solution.py:451
  219.1 15.3 %all-to-all-start.7 = ((f32[16,4,160]{2,1,0:T(4,128)}), f32[16,4,160]{2,1,0:T(4,128)S(1)}, u32[]{:S(2)}, u32[]{:S(2)}) async-start(f32[16,4,160]{2,1,0:T(4,128)} %broadcast_in_dim.65), calls=%async_computation.7 | async-start | bytes 131072 | tf_op jit(solution)/shard_map/all_to_all | solution.py:347
  (5 other events, 5.8 us)
Sparse Core Ops, SparseCore 0:
  53.9 59.8 all-gather.6
  115.9 22.0 all-gather.8
  140.1 31.4 all-gather.10

commit v2 on v1

--- a/solution.py
+++ b/solution.py
@@ -29,19 +29,19 @@
 B_LEN = OUT_ROWS * SEG + GAP
 MERGED = 512
 LANES = 384
-CHUNK = 48
+SWAP = 256
 VMEM = pl.BlockSpec(memory_space=pltpu.VMEM)
 SMEM = pl.BlockSpec(memory_space=pltpu.SMEM)
 
 
-def call(kernel, out_shape, in_specs, scratch=()):
+def call(kernel, out_shape, in_specs, scratch=(), limit=16):
     return pl.pallas_call(
         kernel,
         out_shape=out_shape,
         in_specs=in_specs,
         out_specs=jax.tree.map(lambda _: VMEM, out_shape),
         scratch_shapes=list(scratch),
-        compiler_params=pltpu.CompilerParams(vmem_limit_bytes=40 * 1024 * 1024),
+        compiler_params=pltpu.CompilerParams(vmem_limit_bytes=limit * 1024 * 1024),
     )
 
 
@@ -132,81 +132,98 @@
     return jnp.concatenate([low, high[:, 0:32]], axis=1)
 
 
-def first_kernel(
-    place_ref, rows_ref, stat_ref, wm_ref, wpad_ref, gain_ref, shift_ref,
-    hidden_ref, joined_ref, sum_ref,
-    raw, act, merged,
-):
-    first_row, first_col = place_ref[0], place_ref[1]
+def join_kernel(place_ref, own_ref, other_ref, wpad_ref, joined_ref, raw):
     order = ((0, 3), (0, 0), (1, 0), (0, 1), (1, 1), (0, 2), (1, 2), (1, 3))
     sub = lax.broadcasted_iota(jnp.int32, (GAP, LANES), 0)
     zeros = jnp.zeros((GAP, LANES), BF16)
     raw[0:GAP, :] = zeros
     raw[GAP + A_LEN : GAP + A_LEN + GAP, :] = zeros
-    for r in range(IN_ROWS + 1):
-        after = rows_ref[order[r]] if r < IN_ROWS else None
-        gap_right = rows_ref[order[r - 1]][WIDE:SEG].astype(F32) if r else jnp.zeros((GAP, LANES), F32)
-        gap_left = after[WIDE:SEG].astype(F32) if r < IN_ROWS else gap_right
-        raw[GAP + r * SEG : 2 * GAP + r * SEG, :] = jnp.where(sub < 8, gap_right, gap_left).astype(BF16)
-        if r < IN_ROWS:
-            raw[2 * GAP + r * SEG : GAP + (r + 1) * SEG, :] = after[0:WIDE]
-
-    totals = jnp.sum(stat_ref[...], axis=0, keepdims=True) / (20.0 * 131072.0)
-    mean = totals[:, 0:32]
-    var = totals[:, 32:64] - mean * mean
-    pair = jnp.concatenate([lax.rsqrt(var + EPS), mean, jnp.zeros((6, 32), F32)[:, :]], axis=0)
-    spread = exact_dot(pair, same_group(32, 2 * C, 1, 20))
-    scale = spread[0:1] * gain_ref[...] * 0.5
-    offset = -spread[1:2] * scale
+
+    def lay_out(sources):
+        for r in range(IN_ROWS + 1):
+            before, after = None, None
+            if r:
+                which, at = order[r - 1]
+                before = sources[which][at, WIDE:SEG, :].astype(F32)
+            if r < IN_ROWS:
+                which, at = order[r]
+                after = sources[which][at, WIDE:SEG, :].astype(F32)
+                raw[2 * GAP + r * SEG : GAP + (r + 1) * SEG, :] = sources[which][at, 0:WIDE, :]
+            before = after if before is None else before
+            after = before if after is None else after
+            raw[GAP + r * SEG : 2 * GAP + r * SEG, :] = jnp.where(sub < 8, before, after).astype(BF16)
+
+    @pl.when(place_ref[2] == 0)
+    def _():
+        lay_out((own_ref, other_ref))
+
+    @pl.when(place_ref[2] == 1)
+    def _():
+        lay_out((other_ref, own_ref))
 
     def one(r, size):
         base = r * SEG
         tail = raw[rows_at(base, size + 2 * GAP), 256:384].astype(F32)
         skip = skip_of(tail, wpad_ref, GAP, GAP + size)
         joined = join(raw[rows_at(base + GAP, size), :].astype(F32), skip)
-        values = silu_half(joined * scale + offset) * keep_mask(r, first_row, first_col)[0:size]
-        act[rows_at(base, size), :] = values.astype(BF16)
-        return joined.astype(BF16)
+        joined_ref[rows_at(base, size), :] = joined.astype(BF16)
 
     def build(r, carry):
-        joined = one(r, SEG)
-
-        @pl.when((r >= 2) & (r < 6))
-        def _():
-            joined_ref[rows_at((r - 2) * SEG, SEG), :] = joined
-
-        @pl.when(r == 6)
-        def _():
-            joined_ref[4 * SEG : B_LEN, :] = joined[0:GAP]
-
+        one(r, SEG)
         return carry
 
     lax.fori_loop(0, IN_ROWS, build, 0)
     one(IN_ROWS, GAP)
 
+
+def first_kernel(
+    place_ref, joined_ref, stat_ref, wm_ref, gain_ref, shift_ref,
+    hidden_ref, sum_ref,
+    act, merged,
+):
+    first_row, first_col = place_ref[0], place_ref[1]
+    totals = jnp.sum(stat_ref[...], axis=0, keepdims=True) / (20.0 * 131072.0)
+    mean = totals[:, 0:32]
+    var = totals[:, 32:64] - mean * mean
+    pair = jnp.concatenate([lax.rsqrt(var + EPS), mean, jnp.zeros((6, 32), F32)], axis=0)
+    spread = exact_dot(pair, same_group(32, 2 * C, 1, 20))
+    scale = spread[0:1] * gain_ref[...] * 0.5
+    offset = -spread[1:2] * scale
+
+    def build(r):
+        where = slice(r * SEG, r * SEG + (SEG if r < IN_ROWS else GAP))
+        mask = keep_mask(r, first_row, first_col)[0 : where.stop - where.start]
+        for lane in range(0, 2 * C, 128):
+            at = slice(lane, lane + 128)
+            values = joined_ref[where, at].astype(F32) * scale[:, at] + offset[:, at]
+            act[where, at] = (silu_half(values) * mask).astype(BF16)
+
     def conv(start, size):
-        taps = [act[rows_at(start + a * SEG, size), :] for a in range(3)]
-        merged[rows_at(start + GAP, size), :] = tap_dot(jnp.concatenate(taps, axis=1), wm_ref[...])
+        taps = [act[start + a * SEG : start + a * SEG + size, :] for a in range(3)]
+        merged[start + GAP : start + GAP + size, :] = tap_dot(jnp.concatenate(taps, axis=1), wm_ref[...])
 
     merged[0:GAP, :] = jnp.zeros((GAP, MERGED), F32)
     merged[GAP + H_LEN : GAP + H_LEN + GAP, :] = jnp.zeros((GAP, MERGED), F32)
-
-    def convs(i, carry):
-        conv(i * 2 * SEG, 2 * SEG)
-        return carry
-
-    lax.fori_loop(0, 3, convs, 0)
-    conv(6 * SEG, GAP)
+    for r in range(4):
+        build(r)
+    conv(0, 2 * SEG)
+    build(4)
+    build(5)
+    conv(2 * SEG, 2 * SEG)
+    for r in range(6, 9):
+        build(r)
+    conv(4 * SEG, 2 * SEG + GAP)
 
     sums = jnp.zeros((1, HALF), F32)
     squares = jnp.zeros((1, HALF), F32)
-    for r in range(MID_ROWS):
-        values = shift_add(merged, GAP + r * SEG, SEG) + shift_ref[...]
-        hidden_ref[r * SEG : (r + 1) * SEG, :] = values
+    for r in range(MID_ROWS + 1):
+        size = SEG if r < MID_ROWS else GAP
+        values = shift_add(merged, GAP + r * SEG, size) + shift_ref[...]
+        hidden_ref[r * SEG : r * SEG + size, 0:HALF] = values
         if r in (2, 3):
             sums = sums + jnp.sum(values[GAP:], axis=0, keepdims=True)
             squares = squares + jnp.sum(values[GAP:] * values[GAP:], axis=0, keepdims=True)
-    hidden_ref[6 * SEG : H_LEN, :] = shift_add(merged, GAP + 6 * SEG, GAP) + shift_ref[...]
+    hidden_ref[:, HALF:SWAP] = jnp.zeros((H_LEN, SWAP - HALF), F32)
     sum_ref[...] = jnp.concatenate([sums, squares], axis=0)
 
 
@@ -239,7 +256,7 @@
         mask = keep_mask(r, first_row, first_col)[0:size]
         where = rows_at(r * SEG, size)
         for source, target, (scale, offset) in ((own_ref, act_own, own), (other_ref, act_other, other)):
-            target[where, :] = (silu_half(source[where, :] * scale + offset) * mask).astype(BF16)
+            target[where, :] = (silu_half(source[where, 0:HALF] * scale + offset) * mask).astype(BF16)
 
     def build(r, carry):
         one(r, SEG)
@@ -271,11 +288,14 @@
     for r in range(OUT_ROWS + 1):
         size = SEG if r < OUT_ROWS else GAP
         where = slice(r * SEG, r * SEG + size)
-        values = shift_add(merged, GAP + r * SEG, size) + tap_dot(joined_ref[where, :], wskip_ref[...])
-        block_ref[where, :] = values
+        values = shift_add(merged, GAP + r * SEG, size) + tap_dot(
+            joined_ref[2 * SEG + where.start : 2 * SEG + where.stop, :], wskip_ref[...]
+        )
+        block_ref[where, 0:HALF] = values
         if r in (1, 2):
             sums = sums + jnp.sum(values[GAP:], axis=0, keepdims=True)
             squares = squares + jnp.sum(values[GAP:] * values[GAP:], axis=0, keepdims=True)
+    block_ref[:, HALF:SWAP] = jnp.zeros((B_LEN, SWAP - HALF), F32)
     sum_ref[...] = jnp.concatenate([sums, squares], axis=0)
 
 
@@ -290,7 +310,7 @@
         where = rows_at(core * SEG + r * SEG, size)
         total = None
         for source, (scale, offset), which in ((own_ref, own, core), (other_ref, other, 1 - core)):
-            act = (silu_half(source[where, :] * scale + offset) * mask).astype(BF16)
+            act = (silu_half(source[where, 0:HALF] * scale + offset) * mask).astype(BF16)
             part = tap_dot(act, wout_ref[which])
             total = part if total is None else total + part
         parts.append(total)
@@ -311,35 +331,54 @@
     out_ref[at : at + size, 384 + 32 * b : 384 + 32 * (b + 1)] = piece[:, 128:160]
 
 
-def front_weight_kernel(found_ref, out_ref):
+def front_weight_kernel(found_ref, out_ref, rows):
     out_ref[:, 480:512] = jnp.zeros((3 * 2 * C, 32), BF16)
-    for chunk in range(5760 // CHUNK):
-        plane, j = divmod(chunk, 15)
-        s, q = divmod(plane, 4)
-        row = chunk * CHUNK
-        end = row + CHUNK
-        while row < end:
+    to = lax.broadcasted_iota(jnp.int32, (360, 384), 0)
+    source = lax.broadcasted_iota(jnp.int32, (360, 384), 1)
+    j, rest = source // 24, source % 24
+    part, i = rest // 12, rest % 12
+    at = 12 * (j % 4) + i
+    goal = 45 * (2 * (j // 4) + part) + at
+    picks = ((to == goal) & (at < 45)).astype(BF16)
+    for d in range(4):
+        found = [found_ref[j, 24 * d : 24 * (d + 1), :].astype(F32) for j in range(16)]
+        rows[360 * d : 360 * (d + 1), :] = tap_dot(picks, jnp.concatenate(found, axis=0).astype(BF16))
+    for q in range(4):
+        row = 1440 * q
+        while row < 1440 * (q + 1):
             tap, channel = divmod(row, 2 * C)
-            size = min(end - row, 2 * C - channel)
+            size = min(1440 * (q + 1) - row, 2 * C - channel)
             a, b = divmod(tap, 3)
-            i = row - chunk * CHUNK
-            piece = found_ref[j, 48 * s + i : 48 * s + i + size, 160 * q : 160 * (q + 1)]
+            k = row - 1440 * q
+            piece = rows[k : k + size, 160 * q : 160 * (q + 1)].astype(BF16)
             place_merged(out_ref, a * 2 * C + channel, size, b, piece)
             row += size
 
 
 def middle_weight_kernel(found_ref, out_ref, skip_ref):
     out_ref[:, :, 480:512] = jnp.zeros((2, 3 * HALF, 32), BF16)
+
+    def pieces(x, row, size):
+        while size:
+            q, i = divmod(row, 224)
+            some = min(size, 224 - i)
+            yield some, found_ref[x, i : i + some, 160 * q : 160 * (q + 1)]
+            row, size = row + some, size - some
+
     for tap in range(9):
         a, b = divmod(tap, 3)
         for half in (0, 1):
+            at = a * HALF
             for part in (0, 1):
-                row = tap * C + half * HALF + part * 80
-                x, i = divmod(row, 720)
-                piece = found_ref[x, i : i + 80, :]
-                place_merged(out_ref.at[half], a * HALF + part * 80, 80, b, piece)
+                x, i = divmod(tap * C + half * HALF + part * 80, 720)
+                for size, piece in pieces(x, i, 80):
+                    place_merged(out_ref.at[half], at, size, b, piece)
+                    at += size
+    at = 0
     for x in range(4):
-        skip_ref[x * HALF : (x + 1) * HALF, :] = found_ref[x, 720:880, :]
+        for size, piece in pieces(x, 720, HALF):
+            skip_ref[at : at + size, :] = piece
+            at += size
 
 
 def from_everyone(x, axis):
@@ -365,13 +404,15 @@
     chip_row = 2 * (lax.axis_index(("zp", "zl", "y")))
     place = jnp.stack([chip_row - 3, x * WIDE, core]).astype(jnp.int32)
 
-    halves = front_weight.reshape(45, 2, HALF).transpose(1, 0, 2)
-    spread = jnp.broadcast_to(halves[None], (8, 2, 45, HALF)).reshape(16, 45, HALF)
-    planes = lax.all_to_all(spread, ("zl", "y", "core"), 0, 0, tiled=True).reshape(720, HALF)
-    planes = jnp.pad(planes, ((0, CHUNK), (0, 0)))
-    mine = lax.dynamic_slice_in_dim(planes, CHUNK * (4 * y + x), CHUNK, 0)
-    deepest = from_everyone(mine, "zp")
-    dense = deepest.reshape(2, 4, CHUNK, HALF).transpose(0, 2, 1, 3).reshape(2 * CHUNK, 4 * HALF)
+    swap = [(0, 1), (1, 0)]
+    quarter = lax.dynamic_slice_in_dim(jnp.pad(front_weight, ((0, 3), (0, 0))), 12 * x, 12, 0)
+    kept = lax.dynamic_slice_in_dim(quarter, core * HALF, HALF, 1)
+    given = lax.dynamic_slice_in_dim(quarter, (1 - core) * HALF, HALF, 1)
+    taken = lax.ppermute(given, "core", swap)
+    first_core = core == 0
+    mine = jnp.concatenate([jnp.where(first_core, kept, taken), jnp.where(first_core, taken, kept)], axis=0)
+    deepest = from_everyone(mine, DEPTH)
+    dense = deepest.reshape(4, 4, 24, HALF).transpose(1, 2, 0, 3).reshape(96, 4 * HALF)
     front_found = lax.all_gather(dense, ("y", "x"), axis=0)
 
     wpad = in_weight.reshape(3, 3, 4, C).transpose(1, 0, 2, 3).reshape(3, 12, C)
@@ -392,7 +433,9 @@
     crossed = [(i, i + 3) if i % 2 else (i, i - 3) for i in range(count)]
     crossed = [(i, j) for i, j in crossed if 0 <= j < count]
     around = jnp.stack([shifted(row, ROWS, 2), row, shifted(row, ROWS, -2), lax.ppermute(row, ROWS, crossed)])
-    rows = lax.all_gather(around, "core", axis=0)
+    joined = call(
+        join_kernel, sds((A_LEN, 2 * C), BF16), [SMEM] + [VMEM] * 3, [pltpu.VMEM((A_LEN + 2 * GAP, LANES), BF16)]
+    )(place, around, lax.ppermute(around, "core", swap), wpad)
 
     half_width = time_weight.shape[0] // 2
     ratios = jnp.exp(-math.log(10000.0) * jnp.arange(half_width, dtype=F32) / half_width)
@@ -411,20 +454,20 @@
     time_shift = jnp.dot(embedded, proj.astype(F32), precision=HIGH)
     wide = from_everyone(near[:, :, 0:64].sum(axis=(0, 1))[None], DEPTH).reshape(16, 64)
 
-    front = call(front_weight_kernel, sds((3 * 2 * C, MERGED), BF16), [VMEM])(front_found)
-    hidden_own, joined, sums = call(
+    front = call(
+        front_weight_kernel, sds((3 * 2 * C, MERGED), BF16), [VMEM], [pltpu.VMEM((1440, 4 * HALF), F32)]
+    )(front_found)
+    hidden_own, sums = call(
         first_kernel,
-        (sds((H_LEN, HALF), F32), sds((B_LEN, 2 * C), BF16), sds((2, HALF), F32)),
-        [SMEM] + [VMEM] * 6,
-        [
-            pltpu.VMEM((A_LEN + 2 * GAP, LANES), BF16),
-            pltpu.VMEM((A_LEN, 2 * C), BF16),
-            pltpu.VMEM((H_LEN + 2 * GAP, MERGED), F32),
-        ],
-    )(place, rows, wide, front, wpad, input_gain[None], time_shift[None])
+        (sds((H_LEN, SWAP), F32), sds((2, HALF), F32)),
+        [SMEM] + [VMEM] * 5,
+        [pltpu.VMEM((A_LEN, 2 * C), BF16), pltpu.VMEM((H_LEN + 2 * GAP, MERGED), F32)],
+        24,
+    )(place, joined, wide, front, input_gain[None], time_shift[None])
 
     both = jnp.concatenate([middle_weight, skip_weight], axis=0).reshape(880, 2, HALF)
     kept = lax.dynamic_slice_in_dim(both, core, 1, 1).reshape(880, HALF)
+    kept = jnp.pad(kept, ((0, 16), (0, 0))).reshape(4, 224, HALF).transpose(1, 0, 2).reshape(224, 4 * HALF)
     kept, front_found = lax.optimization_barrier((kept, front_found))
     middle_found = lax.all_gather(kept, "x", axis=0)
     middle, shortcut = call(
@@ -433,11 +476,10 @@
         [VMEM],
     )(middle_found)
 
-    swap = [(0, 1), (1, 0)]
     hidden_other = lax.ppermute(hidden_own, "core", swap)
     block_own, sums = call(
         second_kernel,
-        (sds((B_LEN, HALF), F32), sds((2, HALF), F32)),
+        (sds((B_LEN, SWAP), F32), sds((2, HALF), F32)),
         [SMEM] + [VMEM] * 7,
         [
             pltpu.VMEM((H_LEN, HALF), BF16),

time: 244 us -> 217 us (0.89)
  waiting for transfers between devices: 55.2 us -> 37.1 us
  local copies, waits for them, and re-layouts: 26.6 us -> 19.3 us
  blocking collectives: 48.7 us -> 43.7 us
  Pallas kernels: 17.9 us -> 21.5 us
    ppermute x0 -> x2, starting transfers between devices: none -> 10.7 us  [the longest x1 8.76 us: shards(): taken = lax.ppermute(given, 'core', swap)]
    all_to_all x1 -> x0, starting transfers between devices: 10.2 us -> none  [shards(): lax.all_to_all(spread, ('zl', 'y', 'core'), 0, 0, tiled=True)]
    all_to_all x1 -> x0, waiting for transfers between devices: 8.39 us -> none  [shards(): lax.all_to_all(spread, ('zl', 'y', 'core'), 0, 0, tiled=True)]
    all_to_all x4, waiting for transfers between devices: 31.8 us -> 26.4 us  [from_everyone(): lax.all_to_all(jnp.broadcast_to(x[None], (count, *x.shape)), axis, 0, 0,...]
    all_to_all x3, blocking collectives: 48.7 us -> 43.7 us  [from_everyone(): lax.all_to_all(jnp.broadcast_to(x[None], (count, *x.shape)), axis, 0, 0,...]
    all_gather x1, waiting for transfers between devices: 4.93 us -> 0.83 us  [shards(): front_found = lax.all_gather(dense, ('y', 'x'), axis=0)]
    ppermute x2 -> x0, local copies, waits for them, and re-layouts: 3.15 us -> none  [the longest x1 1.68 us: shards(): hidden_other = lax.ppermute(hidden_own, 'core', swap)]
    all_to_all x4, starting transfers between devices: 35.3 us -> 32.2 us  [from_everyone(): lax.all_to_all(jnp.broadcast_to(x[None], (count, *x.shape)), axis, 0, 0,...]
  transfers between devices with their start and end apart: 17 -> 17, of which waited for: 10 -> 10; matrix products, arithmetic and copies ran while one was open for 6% -> 5% of each run, Pallas kernels for 5% -> 6%
where the time goes in v2:
time: 217 us; the launch traced here: 215 us
  starting transfers between devices  74.6 us (34%)
  blocking collectives  43.7 us (20%)
  waiting for transfers between devices  37.1 us (17%)
  Pallas kernels  21.5 us (10%)
  local copies, waits for them, and re-layouts  19.3 us (9%)
  between operations  14.6 us (7%)
  matrix products  2.9 us (1%)
    all_to_all x3, blocking collectives, from_everyone(): lax.all_to_all(jnp.broadcast_to(x[None], (count, *x.shape)), axis, 0, 0,...  43.7 us
    all_to_all x4, starting transfers between devices, from_everyone(): lax.all_to_all(jnp.broadcast_to(x[None], (count, *x.shape)), axis, 0, 0,...  32.2 us
    all_to_all x4, waiting for transfers between devices, from_everyone(): lax.all_to_all(jnp.broadcast_to(x[None], (count, *x.shape)), axis, 0, 0,...  26.4 us
    ppermute x6, starting transfers between devices, shifted(): lax.ppermute(x, axis, [(i, i + step) for i in range(count) if 0 <= i + st...  18.1 us
    unnamed x40, local copies, waits for them, and re-layouts  10.3 us
    ppermute x1, starting transfers between devices, shards(): taken = lax.ppermute(given, 'core', swap)  8.76 us
    ppermute x6, waiting for transfers between devices, shifted(): lax.ppermute(x, axis, [(i, i + step) for i in range(count) if 0 <= i + st...  8.32 us
    pallas_call x1, Pallas kernels, shards(): call(second_kernel, (sds((B_LEN, SWAP), F32), sds((2, HALF), F32)), [SMEM...  6.75 us
  transfers between devices with their start and end apart: 17, of which 10 were waited for; matrix products, arithmetic and copies ran while one was open for 5% of the time, Pallas kernels for 6%

profile of v2, /device:TPU:1, one launch (start us, length us, event | category | flops | bytes accessed | tf_op | source)
XLA Modules:
  0.0 215.3 jit_solution(17232476679698027016)
XLA Ops:
  7.5 8.8 %collective-permute-start.8 = (bf16[12,160]{1,0:T(8,128)(2,1)S(1)}, bf16[12,160]{1,0:T(8,128)(2,1)S(1)}, u32[]{:S(2)}, u32[]{:S(2)}) collective-permute-start(bf16[12,160]{1,0:T(8,128)(2,1)S(1)} %pad_dynamic-slice_fusion), channel_id=1, source_target_pairs={{0,4},{4,0},{1,5},{5,1},{2,6},{6,2},{3,7},{7,3},{8,12},{12,8},{9,1... | collective-permute-start | bytes 11528 | tf_op jit(solution)/shard_map/ppermute | solution.py:411
  17.9 22.3 %all_to_all.35 = bf16[16,24,160]{2,1,0:T(8,128)(2,1)S(1)} all-to-all(bf16[16,24,160]{2,1,0:T(8,128)(2,1)S(1)} %broadcast_in_dim.24), channel_id=1, replica_groups=mesh['zp'=8,'zl'=2,'y'=4,'core'=2,'x'=4] {'zp','zl'}, dimensions={0} | all-to-all | bytes 245760 | tf_op jit(solution)/shard_map/all_to_all | solution.py:386
  41.2 6.5 %collective-permute-start = (bf16[4,1,256]{2,0,1:T(4,128)(2,1)S(1)}, bf16[4,1,256]{2,0,1:T(4,128)(2,1)S(1)}, u32[]{:S(2)}, u32[]{:S(2)}) collective-permute-start(bf16[4,1,256]{2,0,1:T(4,128)(2,1)S(1)} %copy-done.13), channel_id=1, source_target_pairs={{0,4},{4,8},{8,12},{12,16},{16,20},{20,24},{24,28},{28,32},{32,36}... | collective-permute-start | bytes 6152 | tf_op jit(solution)/shard_map/ppermute | solution.py:391
  47.7 1.9 collective-permute-start.1
  52.7 3.1 %collective-permute-start.2 = (bf16[16,384]{1,0:T(8,128)(2,1)S(1)}, bf16[16,384]{1,0:T(8,128)(2,1)S(1)}, u32[]{:S(2)}, u32[]{:S(2)}) collective-permute-start(bf16[16,384]{1,0:T(8,128)(2,1)S(1)} %get-tuple-element.18), channel_id=1, source_target_pairs={{0,1},{1,2},{2,3},{4,5},{5,6},{6,7},{8,9},{9,10},{10,11},{12,13},{... | collective-permute-start | bytes 36872 | tf_op jit(solution)/shard_map/ppermute | solution.py:391
  55.8 1.3 collective-permute-start.3
  57.4 3.4 %collective-permute-done.3.right_ref = bf16[16,384]{1,0:T(8,128)(2,1)S(1)} collective-permute-done((bf16[16,384]{1,0:T(8,128)(2,1)S(1)}, bf16[16,384]{1,0:T(8,128)(2,1)S(1)}, u32[]{:S(2)}, u32[]{:S(2)}) %collective-permute-start.3) | collective-permute-done | bytes 12320 | tf_op jit(solution)/shard_map/ppermute | solution.py:391
  61.3 5.9 %collective-permute-start.6 = (bf16[272,384]{1,0:T(8,128)(2,1)S(1)}, bf16[272,384]{1,0:T(8,128)(2,1)S(1)}, u32[]{:S(2)}, u32[]{:S(2)}) collective-permute-start(bf16[272,384]{1,0:T(8,128)(2,1)S(1)} %get-tuple-element.20), channel_id=1, source_target_pairs={{4,16},{12,24},{16,4},{20,32},{24,12},{28,40},{32,20},{36,48},{40,... | collective-permute-start | bytes 626696 | tf_op jit(solution)/shard_map/ppermute | solution.py:435
  68.5 4.0 %collective-permute-start.4 = (bf16[272,384]{1,0:T(8,128)(2,1)S(1)}, bf16[272,384]{1,0:T(8,128)(2,1)S(1)}, u32[]{:S(2)}, u32[]{:S(2)}) collective-permute-start(bf16[272,384]{1,0:T(8,128)(2,1)S(1)} %get-tuple-element.20), channel_id=1, source_target_pairs={{0,8},{4,12},{8,16},{12,20},{16,24},{20,28},{24,32},{28,36},{32,40... | collective-permute-start | bytes 626696 | tf_op jit(solution)/shard_map/ppermute | solution.py:391
  73.3 4.6 %collective-permute-done.5 = bf16[272,384]{1,0:T(8,128)(2,1)S(1)} collective-permute-done((bf16[272,384]{1,0:T(8,128)(2,1)S(1)}, bf16[272,384]{1,0:T(8,128)(2,1)S(1)}, u32[]{:S(2)}, u32[]{:S(2)}) %collective-permute-start.5) | collective-permute-done | bytes 208928 | tf_op jit(solution)/shard_map/ppermute | solution.py:391
  78.1 1.9 collective-permute-start.7
  80.7 7.7 %all-to-all-start = ((f32[32,1,224]{2,1,0:T(1,128)}), f32[32,1,224]{2,1,0:T(1,128)S(1)}, u32[]{:S(2)}, u32[]{:S(2)}) async-start(f32[32,1,224]{2,1,0:T(1,128)} %broadcast_in_dim.22), calls=%async_computation | async-start | bytes 65536 | tf_op jit(solution)/shard_map/all_to_all | solution.py:386
  88.9 6.7 %all-to-all-done = f32[32,1,224]{2,1,0:T(1,128)S(1)} async-done(((f32[32,1,224]{2,1,0:T(1,128)}), f32[32,1,224]{2,1,0:T(1,128)S(1)}, u32[]{:S(2)}, u32[]{:S(2)}) %all-to-all-start) | async-done | bytes 28704 | tf_op jit(solution)/shard_map/all_to_all | solution.py:386
  96.6 9.1 %all-to-all-start.1 = ((f32[16,1,64]{2,1,0:T(1,128)}), f32[16,1,64]{2,1,0:T(1,128)S(1)}, u32[]{:S(2)}, u32[]{:S(2)}) async-start(f32[16,1,64]{2,1,0:T(1,128)} %broadcast_in_dim.23), calls=%async_computation.1 | async-start | bytes 16384 | tf_op jit(solution)/shard_map/all_to_all | solution.py:386
  107.4 1.4 fusion.shift_ref
  108.9 3.4 %shard_map.138.joined_ref = bf16[2192,640]{1,0:T(8,128)(2,1)S(1)} custom-call(s32[3]{0:T(128)S(1)} %pad_add_fusion.place_ref, bf16[4,272,384]{2,1,0:T(8,128)(2,1)S(1)} %pad_maximum_fusion.own_ref, bf16[4,272,384]{2,1,0:T(8,128)(2,1)S(1)} %collective-permute-done.7.other_ref, bf16[384,384]{1,0:T(8,128)(2,1)S(1)} %bitcast.44), custom_call_target="tpu_custom_call" | custom-call | tf_op jit(solution)/shard_map/pallas_call | solution.py:436
  112.3 1.6 copy-done.1
  113.9 1.6 shard_map.139.wm_ref
  115.5 1.4 all-to-all-done.1
  117.0 1.8 copy-done.2
  118.7 6.1 %shard_map.140 = (f32[1648,256]{1,0:T(8,128)}, f32[2,160]{1,0:T(2,128)S(1)}) custom-call(s32[3]{0:T(128)S(1)} %pad_add_fusion.place_ref, bf16[2192,640]{1,0:T(8,128)(2,1)S(1)} %copy-done.2, f32[16,64]{1,0:T(8,128)S(1)} %bitcast.48, bf16[1920,512]{1,0:T(8,128)(2,1)S(1)} %shard_map.139.wm_ref, f32[1,640]{1,0:T(1,128)S(1)} %broadcast_in_dim.25.gain_ref, ...), custom_call_target="tpu_custom_call" | custom-call | tf_op jit(solution)/shard_map/pallas_call | solution.py:460
  124.8 3.7 %collective-permute-start.9 = (f32[1648,256]{1,0:T(8,128)}, f32[1648,256]{1,0:T(8,128)S(1)}, u32[]{:S(2)}, u32[]{:S(2)}) collective-permute-start(f32[1648,256]{1,0:T(8,128)} %get-tuple-element.22.own_ref), channel_id=1, source_target_pairs={{0,4},{4,0},{1,5},{5,1},{2,6},{6,2},{3,7},{7,3},{8,12},{12,8},{9,1... | collective-permute-start | bytes 5062664 | tf_op jit(solution)/shard_map/ppermute | solution.py:479
  128.5 10.9 %all_to_all.36 = f32[32,2,160]{2,1,0:T(2,128)S(1)} all-to-all(f32[32,2,160]{2,1,0:T(2,128)S(1)} %broadcast_in_dim.53), channel_id=1, replica_groups=mesh['zp'=8,'zl'=2,'y'=4,'core'=2,'x'=4] {'y','core','x'}, dimensions={0} | all-to-all | bytes 81920 | tf_op jit(solution)/shard_map/all_to_all | solution.py:386
  140.1 11.9 %all-to-all-start.4 = ((f32[16,4,160]{2,1,0:T(4,128)}), f32[16,4,160]{2,1,0:T(4,128)S(1)}, u32[]{:S(2)}, u32[]{:S(2)}) async-start(f32[16,4,160]{2,1,0:T(4,128)} %broadcast_in_dim.55), calls=%async_computation.4 | async-start | bytes 131072 | tf_op jit(solution)/shard_map/all_to_all | solution.py:386
  155.3 8.4 %all-to-all-done.4.stat_ref = f32[16,4,160]{2,1,0:T(4,128)S(1)} async-done(((f32[16,4,160]{2,1,0:T(4,128)}), f32[16,4,160]{2,1,0:T(4,128)S(1)}, u32[]{:S(2)}, u32[]{:S(2)}) %all-to-all-start.4) | async-done | bytes 40992 | tf_op jit(solution)/shard_map/all_to_all | solution.py:386
  163.7 1.8 copy-done.3
  167.8 6.7 %shard_map.142 = (f32[1104,256]{1,0:T(8,128)}, f32[2,160]{1,0:T(2,128)S(1)}) custom-call(s32[3]{0:T(128)S(1)} %copy-done.10, f32[1648,256]{1,0:T(8,128)} %get-tuple-element.22.own_ref, f32[1648,256]{1,0:T(8,128)S(1)} %collective-permute-done.9.other_ref, f32[16,4,160]{2,1,0:T(4,128)S(1)} %all-to-all-done.4.stat_ref, f32[2,160]{1,0:T(2,128)S(1)} %copy-done.12, ...), custom_call_target="tpu_custom_call" | custom-call | tf_op jit(solution)/shard_map/pallas_call | solution.py:480
  174.5 4.0 %collective-permute-start.10 = (f32[1104,256]{1,0:T(8,128)}, f32[1104,256]{1,0:T(8,128)S(1)}, u32[]{:S(2)}, u32[]{:S(2)}) collective-permute-start(f32[1104,256]{1,0:T(8,128)} %get-tuple-element.27.own_ref), channel_id=1, source_target_pairs={{0,4},{4,0},{1,5},{5,1},{2,6},{6,2},{3,7},{7,3},{8,12},{12,8},{9,1... | collective-permute-start | bytes 3391496 | tf_op jit(solution)/shard_map/ppermute | solution.py:493
  178.5 10.6 %all_to_all.37 = f32[32,2,160]{2,1,0:T(2,128)S(1)} all-to-all(f32[32,2,160]{2,1,0:T(2,128)S(1)} %broadcast_in_dim.56), channel_id=1, replica_groups=mesh['zp'=8,'zl'=2,'y'=4,'core'=2,'x'=4] {'y','core','x'}, dimensions={0} | all-to-all | bytes 81920 | tf_op jit(solution)/shard_map/all_to_all | solution.py:386
  189.8 3.5 %all-to-all-start.6 = ((f32[16,4,160]{2,1,0:T(4,128)}), f32[16,4,160]{2,1,0:T(4,128)S(1)}, u32[]{:S(2)}, u32[]{:S(2)}) async-start(f32[16,4,160]{2,1,0:T(4,128)} %broadcast_in_dim.58), calls=%async_computation.6 | async-start | bytes 131072 | tf_op jit(solution)/shard_map/all_to_all | solution.py:386
  195.1 9.8 %all-to-all-done.6.stat_ref = f32[16,4,160]{2,1,0:T(4,128)S(1)} async-done(((f32[16,4,160]{2,1,0:T(4,128)}), f32[16,4,160]{2,1,0:T(4,128)S(1)}, u32[]{:S(2)}, u32[]{:S(2)}) %all-to-all-start.6) | async-done | bytes 40992 | tf_op jit(solution)/shard_map/all_to_all | solution.py:386
  205.6 2.3 %shard_map.143 = f32[4,256]{1,0:T(4,128)S(1)} custom-call(s32[3]{0:T(128)S(1)} %copy-done.11, f32[1104,256]{1,0:T(8,128)} %get-tuple-element.27.own_ref, f32[1104,256]{1,0:T(8,128)S(1)} %collective-permute-done.10.other_ref, f32[16,4,160]{2,1,0:T(4,128)S(1)} %all-to-all-done.6.stat_ref, f32[2,160]{1,0:T(2,128)S(1)} %reshape.96.gain_ref, ...), custom_call_target="tpu_custom_call" | custom-call | tf_op jit(solution)/shard_map/pallas_call | solution.py:494
  (108 shorter events, 22.8 us)
Async XLA Ops:
  6.5 43.9 %copy-start = (bf16[320,1280]{1,0:T(8,128)(2,1)S(1)}, bf16[320,1280]{1,0:T(8,128)(2,1)}, u32[]{:S(2)}) copy-start(bf16[320,1280]{1,0:T(8,128)(2,1)} %param.22) | copy-start | bytes 2457604
  6.5 34.7 %copy-start.13 = (bf16[4,1,256]{2,0,1:T(4,128)(2,1)S(1)}, bf16[4,1,256]{2,0,1:T(4,128)(2,1)}, u32[]{:S(2)}) copy-start(bf16[4,1,256]{2,0,1:T(4,128)(2,1)} %param.14) | copy-start | bytes 6148
  6.5 44.2 %copy-start.15 = (bf16[160,320]{1,0:T(8,128)(2,1)S(1)}, bf16[160,320]{1,0:T(8,128)(2,1)}, u32[]{:S(2)}) copy-start(bf16[160,320]{1,0:T(8,128)(2,1)} %param.20) | copy-start | bytes 307204
  6.5 100.0 %all-gather.4.cloned.1.call-start = ((), (), s32[]{:S(2)}) async-start(), calls=%async_computation.7 | async-start | bytes 2088960 | tf_op jit(solution)/shard_map/all_gather | solution.py:416
  7.5 9.6 %collective-permute-start.8 = (bf16[12,160]{1,0:T(8,128)(2,1)S(1)}, bf16[12,160]{1,0:T(8,128)(2,1)S(1)}, u32[]{:S(2)}, u32[]{:S(2)}) collective-permute-start(bf16[12,160]{1,0:T(8,128)(2,1)S(1)} %pad_dynamic-slice_fusion), channel_id=1, source_target_pairs={{0,4},{4,0},{1,5},{5,1},{2,6},{6,2},{3,7},{7,3},{8,12},{12,8},{9,1... | collective-permute-start | bytes 11528 | tf_op jit(solution)/shard_map/ppermute | solution.py:411
  16.2 35.9 %copy-start.14 = (bf16[720,320]{0,1:T(8,128)(2,1)S(1)}, bf16[720,320]{0,1:T(8,128)(2,1)}, u32[]{:S(2)}) copy-start(bf16[720,320]{0,1:T(8,128)(2,1)} %param.19) | copy-start | bytes 1382404
  40.4 12.2 %copy-start.8 = (bf16[320,1,256]{2,0,1:T(8,128)(2,1)S(1)}, bf16[320,1,256]{2,0,1:T(8,128)(2,1)}, u32[]{:S(2)}) copy-start(bf16[320,1,256]{2,0,1:T(8,128)(2,1)} %param.15) | copy-start | bytes 491524
  41.2 11.1 %collective-permute-start = (bf16[4,1,256]{2,0,1:T(4,128)(2,1)S(1)}, bf16[4,1,256]{2,0,1:T(4,128)(2,1)S(1)}, u32[]{:S(2)}, u32[]{:S(2)}) collective-permute-start(bf16[4,1,256]{2,0,1:T(4,128)(2,1)S(1)} %copy-done.13), channel_id=1, source_target_pairs={{0,4},{4,8},{8,12},{12,16},{16,20},{20,24},{24,28},{28,32},{32,36}... | collective-permute-start | bytes 6152 | tf_op jit(solution)/shard_map/ppermute | solution.py:391
  47.7 4.9 %collective-permute-start.1 = (bf16[4,1,256]{2,0,1:T(4,128)(2,1)S(1)}, bf16[4,1,256]{2,0,1:T(4,128)(2,1)S(1)}, u32[]{:S(2)}, u32[]{:S(2)}) collective-permute-start(bf16[4,1,256]{2,0,1:T(4,128)(2,1)S(1)} %copy-done.13), channel_id=1, source_target_pairs={{4,0},{8,4},{12,8},{16,12},{20,16},{24,20},{28,24},{32,28},{36,32}... | collective-permute-start | bytes 6152 | tf_op jit(solution)/shard_map/ppermute | solution.py:391
  50.9 6.3 %copy-start.16 = (bf16[36,320]{1,0:T(8,128)(2,1)S(1)}, bf16[36,320]{1,0:T(8,128)(2,1)}, u32[]{:S(2)}) copy-start(bf16[36,320]{1,0:T(8,128)(2,1)} %param.17) | copy-start | bytes 69124
  52.7 4.6 %collective-permute-start.2 = (bf16[16,384]{1,0:T(8,128)(2,1)S(1)}, bf16[16,384]{1,0:T(8,128)(2,1)S(1)}, u32[]{:S(2)}, u32[]{:S(2)}) collective-permute-start(bf16[16,384]{1,0:T(8,128)(2,1)S(1)} %get-tuple-element.18), channel_id=1, source_target_pairs={{0,1},{1,2},{2,3},{4,5},{5,6},{6,7},{8,9},{9,10},{10,11},{12,13},{... | collective-permute-start | bytes 36872 | tf_op jit(solution)/shard_map/ppermute | solution.py:391
  55.8 4.9 %collective-permute-start.3 = (bf16[16,384]{1,0:T(8,128)(2,1)S(1)}, bf16[16,384]{1,0:T(8,128)(2,1)S(1)}, u32[]{:S(2)}, u32[]{:S(2)}) collective-permute-start(bf16[16,384]{1,0:T(8,128)(2,1)S(1)} %get-tuple-element.19), channel_id=1, source_target_pairs={{1,0},{2,1},{3,2},{5,4},{6,5},{7,6},{9,8},{10,9},{11,10},{13,12},{... | collective-permute-start | bytes 36872 | tf_op jit(solution)/shard_map/ppermute | solution.py:391
  60.7 27.8 %copy-start.17 = (f32[640]{0:T(1024)S(1)}, f32[640]{0:T(1024)}, u32[]{:S(2)}) copy-start(f32[640]{0:T(1024)} %param.25) | copy-start | bytes 7684
  61.3 12.0 %collective-permute-start.6 = (bf16[272,384]{1,0:T(8,128)(2,1)S(1)}, bf16[272,384]{1,0:T(8,128)(2,1)S(1)}, u32[]{:S(2)}, u32[]{:S(2)}) collective-permute-start(bf16[272,384]{1,0:T(8,128)(2,1)S(1)} %get-tuple-element.20), channel_id=1, source_target_pairs={{4,16},{12,24},{16,4},{20,32},{24,12},{28,40},{32,20},{36,48},{40,... | collective-permute-start | bytes 626696 | tf_op jit(solution)/shard_map/ppermute | solution.py:435
  67.2 10.7 %collective-permute-start.5 = (bf16[272,384]{1,0:T(8,128)(2,1)S(1)}, bf16[272,384]{1,0:T(8,128)(2,1)S(1)}, u32[]{:S(2)}, u32[]{:S(2)}) collective-permute-start(bf16[272,384]{1,0:T(8,128)(2,1)S(1)} %get-tuple-element.20), channel_id=1, source_target_pairs={{8,0},{12,4},{16,8},{20,12},{24,16},{28,20},{32,24},{36,28},{40,32... | collective-permute-start | bytes 626696 | tf_op jit(solution)/shard_map/ppermute | solution.py:391
  68.5 9.4 %collective-permute-start.4 = (bf16[272,384]{1,0:T(8,128)(2,1)S(1)}, bf16[272,384]{1,0:T(8,128)(2,1)S(1)}, u32[]{:S(2)}, u32[]{:S(2)}) collective-permute-start(bf16[272,384]{1,0:T(8,128)(2,1)S(1)} %get-tuple-element.20), channel_id=1, source_target_pairs={{0,8},{4,12},{8,16},{12,20},{16,24},{20,28},{24,32},{28,36},{32,40... | collective-permute-start | bytes 626696 | tf_op jit(solution)/shard_map/ppermute | solution.py:391
  78.1 30.7 %collective-permute-start.7 = (bf16[4,272,384]{2,1,0:T(8,128)(2,1)S(1)}, bf16[4,272,384]{2,1,0:T(8,128)(2,1)S(1)}, u32[]{:S(2)}, u32[]{:S(2)}) collective-permute-start(bf16[4,272,384]{2,1,0:T(8,128)(2,1)S(1)} %pad_maximum_fusion.own_ref), channel_id=1, source_target_pairs={{0,4},{4,0},{1,5},{5,1},{2,6},{6,2},{3,7},{7,3},{8,12},{12,8},{9,1... | collective-permute-start | bytes 2506760 | tf_op jit(solution)/shard_map/ppermute | solution.py:438
  80.7 14.9 %all-to-all-start = ((f32[32,1,224]{2,1,0:T(1,128)}), f32[32,1,224]{2,1,0:T(1,128)S(1)}, u32[]{:S(2)}, u32[]{:S(2)}) async-start(f32[32,1,224]{2,1,0:T(1,128)} %broadcast_in_dim.22), calls=%async_computation | async-start | bytes 65536 | tf_op jit(solution)/shard_map/all_to_all | solution.py:386
  88.5 28.4 %copy-start.9 = (s32[3]{0:T(128)}, s32[3]{0:T(128)S(1)}, u32[]{:S(2)}) copy-start(s32[3]{0:T(128)S(1)} %pad_add_fusion.place_ref) | copy-start | bytes 40
  96.6 20.4 %all-to-all-start.1 = ((f32[16,1,64]{2,1,0:T(1,128)}), f32[16,1,64]{2,1,0:T(1,128)S(1)}, u32[]{:S(2)}, u32[]{:S(2)}) async-start(f32[16,1,64]{2,1,0:T(1,128)} %broadcast_in_dim.23), calls=%async_computation.1 | async-start | bytes 16384 | tf_op jit(solution)/shard_map/all_to_all | solution.py:386
  105.7 47.1 %all-gather.6.cloned.1.call-start = ((), (), s32[]{:S(2)}) async-start(), calls=%async_computation.8 | async-start | bytes 1433600 | tf_op jit(solution)/shard_map/all_gather | solution.py:472
  108.9 5.0 %copy-start.4 = (bf16[16,96,640]{2,1,0:T(8,128)(2,1)S(1)}, bf16[16,96,640]{2,1,0:T(8,128)(2,1)}, u32[]{:S(2)}) copy-start(bf16[16,96,640]{2,1,0:T(8,128)(2,1)} %all-gather.4.cloned.1.call-done.found_ref) | copy-start | bytes 5898244
  112.3 1.6 copy-start.1
  117.0 1.8 copy-start.2
  118.7 33.3 %copy-start.18 = (f32[320]{0:T(512)S(1)}, f32[320]{0:T(512)}, u32[]{:S(2)}) copy-start(f32[320]{0:T(512)} %param.26) | copy-start | bytes 3844
  124.8 38.9 %collective-permute-start.9 = (f32[1648,256]{1,0:T(8,128)}, f32[1648,256]{1,0:T(8,128)S(1)}, u32[]{:S(2)}, u32[]{:S(2)}) collective-permute-start(f32[1648,256]{1,0:T(8,128)} %get-tuple-element.22.own_ref), channel_id=1, source_target_pairs={{0,4},{4,0},{1,5},{5,1},{2,6},{6,2},{3,7},{7,3},{8,12},{12,8},{9,1... | collective-permute-start | bytes 5062664 | tf_op jit(solution)/shard_map/ppermute | solution.py:479
  140.1 23.6 %all-to-all-start.4 = ((f32[16,4,160]{2,1,0:T(4,128)}), f32[16,4,160]{2,1,0:T(4,128)S(1)}, u32[]{:S(2)}, u32[]{:S(2)}) async-start(f32[16,4,160]{2,1,0:T(4,128)} %broadcast_in_dim.55), calls=%async_computation.4 | async-start | bytes 131072 | tf_op jit(solution)/shard_map/all_to_all | solution.py:386
  152.7 1.3 copy-start.5
  163.7 1.8 copy-start.3
  165.5 1.0 copy-start.7
  174.5 30.4 %collective-permute-start.10 = (f32[1104,256]{1,0:T(8,128)}, f32[1104,256]{1,0:T(8,128)S(1)}, u32[]{:S(2)}, u32[]{:S(2)}) collective-permute-start(f32[1104,256]{1,0:T(8,128)} %get-tuple-element.27.own_ref), channel_id=1, source_target_pairs={{0,4},{4,0},{1,5},{5,1},{2,6},{6,2},{3,7},{7,3},{8,12},{12,8},{9,1... | collective-permute-start | bytes 3391496 | tf_op jit(solution)/shard_map/ppermute | solution.py:493
  189.8 15.1 %all-to-all-start.6 = ((f32[16,4,160]{2,1,0:T(4,128)}), f32[16,4,160]{2,1,0:T(4,128)S(1)}, u32[]{:S(2)}, u32[]{:S(2)}) async-start(f32[16,4,160]{2,1,0:T(4,128)} %broadcast_in_dim.58), calls=%async_computation.6 | async-start | bytes 131072 | tf_op jit(solution)/shard_map/all_to_all | solution.py:386
  (4 other events, 2.7 us)
Sparse Core Ops, SparseCore 0:
  41.3 65.1 all-gather.3
  108.6 31.4 all-gather.5

commit v3 on v2

v3 whole, which is shorter than its diff:
```python
import math

import jax
import jax.numpy as jnp
from jax import lax
from jax.experimental import pallas as pl
from jax.experimental.pallas import tpu as pltpu
from jax.sharding import Mesh
from jax.sharding import PartitionSpec as P

ROWS = ("zp", "zl", "y", "core")
DEPTH = ("zp", "zl")
PLANE = ("y", "core", "x")
EPS = 1e-05
F32 = jnp.float32
BF16 = jnp.bfloat16
HIGH = lax.Precision.HIGHEST

C = 320
HALF = 160
WIDE = 256
GAP = 16
SEG = WIDE + GAP
IN_ROWS = 8
MID_ROWS = 6
OUT_ROWS = 4
A_LEN = IN_ROWS * SEG + GAP
H_LEN = MID_ROWS * SEG + GAP
B_LEN = OUT_ROWS * SEG + GAP
MERGED = 512
LANES = 384
SWAP = 256
VMEM = pl.BlockSpec(memory_space=pltpu.VMEM)


def call(kernel, out_shape, in_specs, scratch=(), limit=16):
    return pl.pallas_call(
        kernel,
        out_shape=out_shape,
        in_specs=in_specs,
        out_specs=jax.tree.map(lambda _: VMEM, out_shape),
        scratch_shapes=list(scratch),
        compiler_params=pltpu.CompilerParams(vmem_limit_bytes=limit * 1024 * 1024),
    )


def sds(shape, dtype):
    return jax.ShapeDtypeStruct(shape, dtype)


def rows_at(start, size):
    return pl.ds(pl.multiple_of(start, 16), size)


def place():
    return 2 * lax.axis_index(("zp", "zl", "y")), lax.axis_index("x") * WIDE, lax.axis_index("core")


def same_group(n, m, size_n, size_m):
    i = lax.broadcasted_iota(jnp.int32, (n, m), 0)
    j = lax.broadcasted_iota(jnp.int32, (n, m), 1)
    return ((i // size_n) == (j // size_m)).astype(F32)


def exact_dot(a, b):
    return jnp.dot(a, b, preferred_element_type=F32, precision=HIGH)


def tap_dot(a, b):
    return jnp.dot(a, b, preferred_element_type=F32)


def silu_half(h):
    return h + h * jnp.tanh(h)


def pack_kernel(deep_ref, prev_ref, here_ref, next_ref, out_ref, first_ref, last_ref, tall):
    tall[0:C, :] = deep_ref[...].astype(F32)
    tall[C:LANES, :] = jnp.zeros((LANES - C, WIDE), F32)
    for i, ref in enumerate((prev_ref, here_ref, next_ref)):
        tall[C + 4 * i : C + 4 * i + 4, :] = ref[...].astype(F32)
    out = tall[...].T.astype(BF16)
    out_ref[...] = out
    first_ref[...] = out[0:GAP]
    last_ref[...] = out[WIDE - GAP : WIDE]


def skip_of(tail, wpad_ref, lo, hi):
    n = tail.shape[0]
    left = pltpu.roll(tail, 1, 0)[lo:hi].astype(BF16)
    right = pltpu.roll(tail, n - 1, 0)[lo:hi].astype(BF16)
    mid = tail[lo:hi].astype(BF16)
    stacked = jnp.concatenate([left, mid, right], axis=1)
    return tap_dot(stacked, wpad_ref[...]).astype(BF16).astype(F32)


def join(cells, skip):
    lane = lax.broadcasted_iota(jnp.int32, (cells.shape[0], 128), 1)
    mixed = jnp.where(lane < 64, cells[:, 256:384], skip[:, 0:128])
    return jnp.concatenate([cells[:, 0:256], mixed, skip[:, 128:384]], axis=1)


def three_terms(values):
    high = values.astype(BF16).astype(F32)
    middle = (values - high).astype(BF16).astype(F32)
    return high, middle, values - high - middle


def stats_kernel(cells_ref, left_ref, right_ref, wpad_ref, quarter_ref, row_ref, sent_ref):
    sub = lax.broadcasted_iota(jnp.int32, (GAP, LANES), 0)
    gap = jnp.where(sub < 8, right_ref[...].astype(F32), left_ref[...].astype(F32))
    cells = jnp.concatenate([cells_ref[...].astype(F32), gap], axis=0)
    row_ref[...] = cells.astype(BF16)
    skip = skip_of(cells[:, 256:384], wpad_ref, 0, WIDE)
    joined = join(cells[0:WIDE], skip)
    sums = jnp.sum(joined, axis=0, keepdims=True)
    squares = jnp.sum(joined * joined, axis=0, keepdims=True)
    both = jnp.concatenate([sums, squares, jnp.zeros((6, 2 * C), F32)], axis=0)
    grouped = exact_dot(both, same_group(2 * C, 32, 20, 1))
    terms = three_terms(jnp.concatenate([grouped[0:1], grouped[1:2]], axis=1))
    line = jnp.concatenate([*terms, jnp.zeros((1, C - 192), F32)], axis=1)
    message = jnp.concatenate([quarter_ref[...].astype(F32), line, jnp.zeros((3, C), F32)], axis=0).astype(BF16)
    for z in range(sent_ref.shape[0]):
        sent_ref[z] = message


def plane_kernel(got_ref, part_ref, sent_ref, rows):
    total = jnp.zeros((1, 64), F32)
    for z in range(16):
        got = got_ref[z].astype(F32)
        q, d = divmod(z, 4)
        for half in (0, 1):
            rows[half, 12 * d : 12 * d + 12, 160 * q : 160 * (q + 1)] = got[0:12, 160 * half : 160 * (half + 1)]
        total = total + got[12:13, 0:64] + got[12:13, 64:128] + got[12:13, 128:192]
    first = jnp.concatenate([*three_terms(total), jnp.zeros((1, 4 * HALF - 192), F32)], axis=1)
    second = jnp.concatenate([*three_terms(part_ref[...]), jnp.zeros((1, HALF), F32)], axis=1)
    tail = jnp.concatenate([first, second, jnp.zeros((6, 4 * HALF), F32)], axis=0).astype(BF16)
    for half in (0, 1):
        block = rows[half].astype(BF16)
        for y in range(4):
            for x in range(4):
                sent_ref[8 * y + 4 * half + x, 0:48, :] = block
                sent_ref[8 * y + 4 * half + x, 48:56, :] = tail


def keep_mask(r, first_row, first_col):
    i = lax.broadcasted_iota(jnp.int32, (SEG, 1), 0)
    here = first_row + r
    row = jnp.where(i < 8, here - 1, here)
    col = first_col + jnp.where(i < 8, i + WIDE, i - GAP)
    good = (row >= 0) & (row < 128) & (col >= 0) & (col < 1024)
    return good.astype(F32)


def shift_add(merged_ref, start, size):
    back = merged_ref[pl.ds(start - 1, size), :]
    mid = merged_ref[pl.ds(start, size), :]
    ahead = merged_ref[pl.ds(start + 1, size), :]
    low = back[:, 0:128] + mid[:, 128:256] + ahead[:, 256:384]
    high = (
        back[:, 384:512]
        + pltpu.roll(mid[:, 384:512], 96, 1)
        + pltpu.roll(ahead[:, 384:512], 64, 1)
    )
    return jnp.concatenate([low, high[:, 0:32]], axis=1)


def join_kernel(own_ref, other_ref, wpad_ref, joined_ref, raw):
    order = ((0, 3), (0, 0), (1, 0), (0, 1), (1, 1), (0, 2), (1, 2), (1, 3))
    sub = lax.broadcasted_iota(jnp.int32, (GAP, LANES), 0)
    zeros = jnp.zeros((GAP, LANES), BF16)
    raw[0:GAP, :] = zeros
    raw[GAP + A_LEN : GAP + A_LEN + GAP, :] = zeros

    def lay_out(sources):
        for r in range(IN_ROWS + 1):
            before, after = None, None
            if r:
                which, at = order[r - 1]
                before = sources[which][at, WIDE:SEG, :].astype(F32)
            if r < IN_ROWS:
                which, at = order[r]
                after = sources[which][at, WIDE:SEG, :].astype(F32)
                raw[2 * GAP + r * SEG : GAP + (r + 1) * SEG, :] = sources[which][at, 0:WIDE, :]
            before = after if before is None else before
            after = before if after is None else after
            raw[GAP + r * SEG : 2 * GAP + r * SEG, :] = jnp.where(sub < 8, before, after).astype(BF16)

    core = lax.axis_index("core")

    @pl.when(core == 0)
    def _():
        lay_out((own_ref, other_ref))

    @pl.when(core == 1)
    def _():
        lay_out((other_ref, own_ref))

    def one(r, size):
        base = r * SEG
        tail = raw[rows_at(base, size + 2 * GAP), 256:384].astype(F32)
        skip = skip_of(tail, wpad_ref, GAP, GAP + size)
        joined = join(raw[rows_at(base + GAP, size), :].astype(F32), skip)
        joined_ref[rows_at(base, size), :] = joined.astype(BF16)

    def build(r, carry):
        one(r, SEG)
        return carry

    lax.fori_loop(0, IN_ROWS, build, 0)
    one(IN_ROWS, GAP)


def first_kernel(
    joined_ref, stat_ref, wm_ref, gain_ref, shift_ref,
    hidden_ref, sum_ref,
    act, merged,
):
    chip_row, first_col, _ = place()
    first_row = chip_row - 3
    totals = stat_ref[...] / (20.0 * 131072.0)
    mean = totals[:, 0:32]
    var = totals[:, 32:64] - mean * mean
    pair = jnp.concatenate([lax.rsqrt(var + EPS), mean, jnp.zeros((6, 32), F32)], axis=0)
    spread = exact_dot(pair, same_group(32, 2 * C, 1, 20))
    scale = spread[0:1] * gain_ref[...] * 0.5
    offset = -spread[1:2] * scale

    def build(r):
        where = slice(r * SEG, r * SEG + (SEG if r < IN_ROWS else GAP))
        mask = keep_mask(r, first_row, first_col)[0 : where.stop - where.start]
        for lane in range(0, 2 * C, 128):
            at = slice(lane, lane + 128)
            values = joined_ref[where, at].astype(F32) * scale[:, at] + offset[:, at]
            act[where, at] = (silu_half(values) * mask).astype(BF16)

    def conv(start, size):
        taps = [act[start + a * SEG : start + a * SEG + size, :] for a in range(3)]
        merged[start + GAP : start + GAP + size, :] = tap_dot(jnp.concatenate(taps, axis=1), wm_ref[...])

    merged[0:GAP, :] = jnp.zeros((GAP, MERGED), F32)
    merged[GAP + H_LEN : GAP + H_LEN + GAP, :] = jnp.zeros((GAP, MERGED), F32)
    for r in range(4):
        build(r)
    conv(0, 2 * SEG)
    build(4)
    build(5)
    conv(2 * SEG, 2 * SEG)
    for r in range(6, 9):
        build(r)
    conv(4 * SEG, 2 * SEG + GAP)

    sums = jnp.zeros((1, HALF), F32)
    squares = jnp.zeros((1, HALF), F32)
    for r in range(MID_ROWS + 1):
        size = SEG if r < MID_ROWS else GAP
        values = shift_add(merged, GAP + r * SEG, size) + shift_ref[...]
        hidden_ref[r * SEG : r * SEG + size, 0:HALF] = values
        if r in (2, 3):
            sums = sums + jnp.sum(values[GAP:], axis=0, keepdims=True)
            squares = squares + jnp.sum(values[GAP:] * values[GAP:], axis=0, keepdims=True)
    hidden_ref[:, HALF:SWAP] = jnp.zeros((H_LEN, SWAP - HALF), F32)
    sum_ref[...] = jnp.concatenate([sums, squares], axis=0)


def affine(stat_ref, gain_ref):
    both = jnp.sum(stat_ref[...], axis=0)
    found = []
    for which in (0, 1):
        sums = both[2 * which : 2 * which + 2]
        padded = jnp.concatenate([sums, jnp.zeros((6, HALF), F32)], axis=0)
        totals = exact_dot(padded, same_group(HALF, HALF, 10, 10)) / (10.0 * 131072.0)
        mean = totals[0:1]
        scale = lax.rsqrt(totals[1:2] - mean * mean + EPS) * gain_ref[which : which + 1] * 0.5
        found.append((scale, -mean * scale))
    return found


def second_kernel(own_ref, other_ref, stat_ref, gain_ref, wm_ref, short_ref, block_ref, sum_ref, act, merged):
    chip_row, first_col, core = place()
    first_row = chip_row - 2
    affines = affine(stat_ref, gain_ref)
    first = core == 0

    def build(r):
        where = slice(r * SEG, r * SEG + (SEG if r < MID_ROWS else GAP))
        mask = keep_mask(r, first_row, first_col)[0 : where.stop - where.start]
        own, other = own_ref[where, 0:HALF], other_ref[where, 0:HALF]
        parts = []
        for which, (scale, offset) in enumerate(affines):
            values = jnp.where(first, own, other) if which == 0 else jnp.where(first, other, own)
            parts.append(silu_half(values * scale + offset) * mask)
        parts.append(jnp.zeros((where.stop - where.start, LANES - C), F32))
        act[where, :] = jnp.concatenate(parts, axis=1).astype(BF16)

    def conv(start, size):
        taps = [act[start + a * SEG : start + a * SEG + size, :] for a in range(3)]
        merged[start + GAP : start + GAP + size, :] = tap_dot(jnp.concatenate(taps, axis=1), wm_ref[...])

    merged[0:GAP, :] = jnp.zeros((GAP, MERGED), F32)
    merged[GAP + B_LEN : GAP + B_LEN + GAP, :] = jnp.zeros((GAP, MERGED), F32)
    for r in range(4):
        build(r)
    conv(0, 2 * SEG)
    for r in range(4, 7):
        build(r)
    conv(2 * SEG, 2 * SEG + GAP)

    sums = jnp.zeros((1, HALF), F32)
    squares = jnp.zeros((1, HALF), F32)
    for r in range(OUT_ROWS + 1):
        size = SEG if r < OUT_ROWS else GAP
        where = slice(r * SEG, r * SEG + size)
        values = shift_add(merged, GAP + r * SEG, size) + short_ref[where, :]
        block_ref[where, 0:HALF] = values
        if r in (1, 2):
            sums = sums + jnp.sum(values[GAP:], axis=0, keepdims=True)
            squares = squares + jnp.sum(values[GAP:] * values[GAP:], axis=0, keepdims=True)
    block_ref[:, HALF:SWAP] = jnp.zeros((B_LEN, SWAP - HALF), F32)
    sum_ref[...] = jnp.concatenate([sums, squares], axis=0)


def third_kernel(own_ref, other_ref, stat_ref, gain_ref, wout_ref, noise_ref):
    chip_row, first_col, core = place()
    first_row = chip_row - 1 + core
    affines = affine(stat_ref, gain_ref)
    first = core == 0
    parts = []
    for r in range(4):
        size = SEG if r < 3 else GAP
        mask = keep_mask(r, first_row, first_col)[0:size]
        where = rows_at(core * SEG + r * SEG, size)
        total = None
        own, other = own_ref[where, 0:HALF], other_ref[where, 0:HALF]
        for which, (scale, offset) in enumerate(affines):
            values = jnp.where(first, own, other) if which == 0 else jnp.where(first, other, own)
            act = (silu_half(values * scale + offset) * mask).astype(BF16)
            part = tap_dot(act, wout_ref[which])
            total = part if total is None else total + part
        parts.append(total)
    parts.append(jnp.zeros((896 - 3 * SEG - GAP, 128), F32))
    turned = jnp.concatenate(parts, axis=0).T
    noise = None
    for a in range(3):
        for b in range(3):
            tap = 3 * a + b
            at = a * SEG + GAP + b - 1
            piece = turned[8 * tap : 8 * tap + 8, at : at + WIDE]
            noise = piece if noise is None else noise + piece
    for o in range(4):
        noise_ref[o] = noise[o : o + 1]


def place_merged(out_ref, at, size, b, piece):
    out_ref[at : at + size, 128 * b : 128 * (b + 1)] = piece[:, 0:128]
    out_ref[at : at + size, 384 + 32 * b : 384 + 32 * (b + 1)] = piece[:, 128:160]


def front_weight_kernel(found_ref, proj_ref, out_ref, stat_ref, shift_ref, rows):
    out_ref[:, 480:512] = jnp.zeros((3 * 2 * C, 32), BF16)
    sums = jnp.zeros((1, 64), F32)
    embedded = []
    for shard in range(8):
        part = jnp.zeros((1, HALF), F32)
        for x in range(4):
            j = 4 * shard + x
            found = found_ref[j].astype(F32)
            size = 12 if x < 3 else 9
            for d in range(4):
                at = 360 * d + 45 * shard + 12 * x
                rows[at : at + size, :] = found[12 * d : 12 * d + size]
            for term in range(3):
                sums = sums + found[48:49, 64 * term : 64 * (term + 1)]
                part = part + found[49:50, HALF * term : HALF * (term + 1)]
        embedded.append(part)
    stat_ref[...] = jnp.concatenate([sums, jnp.zeros((1, 64), F32)], axis=1)
    values = jnp.concatenate(embedded, axis=0)
    values = jnp.concatenate([values / (1.0 + jnp.exp(-values)), jnp.zeros((8, WIDE - HALF), F32)], axis=1)
    turned = jnp.concatenate([values, jnp.zeros((120, WIDE), F32)], axis=0).T[0:HALF]
    shift = jnp.zeros((HALF, HALF), F32)
    for shard in range(8):
        shift = shift + turned[:, shard : shard + 1] * proj_ref[shard].astype(F32)
    shift_ref[...] = jnp.sum(shift, axis=0, keepdims=True)
    for q in range(4):
        row = 1440 * q
        while row < 1440 * (q + 1):
            tap, channel = divmod(row, 2 * C)
            size = min(1440 * (q + 1) - row, 2 * C - channel)
            a, b = divmod(tap, 3)
            k = row - 1440 * q
            piece = rows[k : k + size, 160 * q : 160 * (q + 1)].astype(BF16)
            place_merged(out_ref, a * 2 * C + channel, size, b, piece)
            row += size


def middle_weight_kernel(found_ref, joined_ref, out_ref, short_ref, skip):
    out_ref[:, 480:512] = jnp.zeros((3 * LANES, 32), BF16)

    def pieces(x, row, size):
        while size:
            q, i = divmod(row, 224)
            some = min(size, 224 - i)
            yield some, found_ref[x, i : i + some, 160 * q : 160 * (q + 1)]
            row, size = row + some, size - some

    for a in range(3):
        out_ref[a * LANES + C : (a + 1) * LANES, :] = jnp.zeros((LANES - C, MERGED), BF16)
    for tap in range(9):
        a, b = divmod(tap, 3)
        at = a * LANES
        for part in range(4):
            x, i = divmod(tap * C + part * 80, 720)
            for size, piece in pieces(x, i, 80):
                place_merged(out_ref, at, size, b, piece)
                at += size
    at = 0
    for x in range(4):
        for size, piece in pieces(x, 720, HALF):
            skip[at : at + size, :] = piece
            at += size
    short_ref[...] = tap_dot(joined_ref[2 * SEG : 2 * SEG + B_LEN, :], skip[...])


def from_everyone(x, axis):
    count = lax.axis_size(axis)
    return lax.all_to_all(jnp.broadcast_to(x[None], (count, *x.shape)), axis, 0, 0, tiled=True)


def shifted(x, axis, step):
    count = lax.axis_size(axis)
    return lax.ppermute(x, axis, [(i, i + step) for i in range(count) if 0 <= i + step < count])


def summed_halves(sums, kept):
    near = from_everyone(sums, PLANE).reshape(4, 2, 4, 2, HALF).sum(axis=(0, 2))
    near, kept = lax.optimization_barrier((near, kept))
    return from_everyone(near.reshape(4, HALF), DEPTH), kept


def shards(
    latent, deep, timestep, in_weight, front_weight, middle_weight, skip_weight, out_weight,
    time_weight, time_second, time_proj, input_gain, middle_gain, output_gain,
):
    core, x, y = lax.axis_index("core"), lax.axis_index("x"), lax.axis_index("y")
    depths = lax.axis_size(DEPTH)

    above, below = shifted(latent, ROWS, 1), shifted(latent, ROWS, -1)
    cells, first, last = call(
        pack_kernel,
        (sds((WIDE, LANES), BF16), sds((GAP, LANES), BF16), sds((GAP, LANES), BF16)),
        [VMEM] * 4,
        [pltpu.VMEM((LANES, WIDE), F32)],
    )(deep.reshape(C, WIDE), above.reshape(4, WIDE), latent.reshape(4, WIDE), below.reshape(4, WIDE))
    from_right, from_left = shifted(first, "x", -1), shifted(last, "x", 1)
    wpad = in_weight.reshape(3, 3, 4, C).transpose(1, 0, 2, 3).reshape(3, 12, C)
    wpad = jnp.pad(wpad, ((0, 0), (64, 52), (64, 0))).reshape(LANES, LANES)
    quarter = lax.dynamic_slice_in_dim(jnp.pad(front_weight, ((0, 3), (0, 0))), 12 * x, 12, 0)
    row, sent = call(stats_kernel, (sds((SEG, LANES), BF16), sds((depths, 16, C), BF16)), [VMEM] * 5)(
        cells, from_left, from_right, wpad, quarter
    )

    half_width = time_weight.shape[0] // 2
    ratios = jnp.exp(-math.log(10000.0) * jnp.arange(half_width, dtype=F32) / half_width)
    angles = timestep[0].astype(F32) * ratios
    features = jnp.concatenate([jnp.cos(angles), jnp.sin(angles)])
    depth_here = time_second.shape[0]
    weight_here = lax.dynamic_slice_in_dim(time_weight, x * depth_here, depth_here, 1)
    hidden = jax.nn.silu(jnp.dot(features, weight_here.astype(F32), precision=HIGH))
    columns = lax.dynamic_slice_in_dim(time_second, (2 * y + core) * HALF, HALF, 1)
    part = jnp.dot(hidden, columns.astype(F32), precision=HIGH)
    proj = lax.dynamic_slice_in_dim(time_proj, core * HALF, HALF, 1).reshape(8, HALF, HALF)

    got = lax.all_to_all(sent, DEPTH, 0, 0, tiled=True)
    sent = call(plane_kernel, sds((32, 56, 4 * HALF), BF16), [VMEM] * 2, [pltpu.VMEM((2, 48, 4 * HALF), F32)])(
        got, part[None]
    )
    found = lax.all_to_all(sent, PLANE, 0, 0, tiled=True)

    count = lax.axis_size(ROWS)
    crossed = [(i, i + 3) if i % 2 else (i, i - 3) for i in range(count)]
    crossed = [(i, j) for i, j in crossed if 0 <= j < count]
    around = jnp.stack([shifted(row, ROWS, 2), row, shifted(row, ROWS, -2), lax.ppermute(row, ROWS, crossed)])
    swap = [(0, 1), (1, 0)]
    joined = call(
        join_kernel, sds((A_LEN, 2 * C), BF16), [VMEM] * 3, [pltpu.VMEM((A_LEN + 2 * GAP, LANES), BF16)]
    )(around, lax.ppermute(around, "core", swap), wpad)

    both = jnp.concatenate([middle_weight, skip_weight], axis=0).reshape(880, 2, HALF)
    kept = lax.dynamic_slice_in_dim(both, core, 1, 1).reshape(880, HALF)
    kept = jnp.pad(kept, ((0, 16), (0, 0))).reshape(4, 224, HALF).transpose(1, 0, 2).reshape(224, 4 * HALF)
    kept, found = lax.optimization_barrier((kept, found))
    middle_found = lax.all_gather(kept, "x", axis=0)

    front, wide, time_shift = call(
        front_weight_kernel,
        (sds((3 * 2 * C, MERGED), BF16), sds((1, 128), F32), sds((1, HALF), F32)),
        [VMEM] * 2,
        [pltpu.VMEM((1440, 4 * HALF), F32)],
    )(found, proj)
    hidden_own, sums = call(
        first_kernel,
        (sds((H_LEN, SWAP), F32), sds((2, HALF), F32)),
        [VMEM] * 5,
        [pltpu.VMEM((A_LEN, 2 * C), BF16), pltpu.VMEM((H_LEN + 2 * GAP, MERGED), F32)],
        24,
    )(joined, wide, front, input_gain[None], time_shift)

    middle, shortcut = call(
        middle_weight_kernel,
        (sds((3 * LANES, MERGED), BF16), sds((B_LEN, HALF), F32)),
        [VMEM] * 2,
        [pltpu.VMEM((2 * C, HALF), BF16)],
    )(middle_found, joined)

    totals, hidden_own = summed_halves(sums, hidden_own)
    hidden_other = lax.ppermute(hidden_own, "core", swap)
    block_own, sums = call(
        second_kernel,
        (sds((B_LEN, SWAP), F32), sds((2, HALF), F32)),
        [VMEM] * 6,
        [pltpu.VMEM((H_LEN, LANES), BF16), pltpu.VMEM((B_LEN + 2 * GAP, MERGED), F32)],
    )(hidden_own, hidden_other, totals, middle_gain.reshape(2, HALF), middle, shortcut)

    wout = out_weight.reshape(9, 2, HALF, 4).transpose(1, 2, 0, 3)
    wout = jnp.pad(jnp.pad(wout, ((0, 0), (0, 0), (0, 0), (0, 4))).reshape(2, HALF, 72), ((0, 0), (0, 0), (0, 56)))
    totals, block_own = summed_halves(sums, block_own)
    block_other = lax.ppermute(block_own, "core", swap)
    return call(third_kernel, sds((4, 1, WIDE), F32), [VMEM] * 5)(
        block_own, block_other, totals, output_gain.reshape(2, HALF), wout
    )


def solution(mesh):
    finer = Mesh(
        mesh.devices.reshape(8, 2, 4, 2, mesh.shape["cols"]), ("zp", "zl", "y", "core", "x")
    )
    in_specs = (
        P(None, ROWS, "x"),
        P(None, ROWS, "x"),
        P(),
        P(),
        P(ROWS, None),
        P("x", None),
        P("x", None),
        P(),
        P(),
        P("x", None),
        P(),
        P(),
        P(),
        P(),
    )
    return jax.shard_map(
        shards, mesh=finer, in_specs=in_specs, out_specs=P(None, ROWS, "x"), check_vma=False
    )
```

time: 217 us -> 238 us (1.097)
  waiting for transfers between devices: 37.1 us -> 72.5 us
  blocking collectives: 43.7 us -> 14.8 us
  local copies, waits for them, and re-layouts: 19.3 us -> 29.3 us
  starting transfers between devices: 74.6 us -> 80 us
    all_to_all x3 -> x1, blocking collectives: 43.7 us -> 14.8 us  [from_everyone(): lax.all_to_all(jnp.broadcast_to(x[None], (count, *x.shape)), axis, 0, 0,...]
    all_to_all x0 -> x2, starting transfers between devices: none -> 25.9 us  [the longest x1 14.9 us: shards(): got = lax.all_to_all(sent, DEPTH, 0, 0, tiled=True)]
    ppermute x1, waiting for transfers between devices: 0.75 us -> 22.5 us  [shards(): lax.ppermute(row, ROWS, crossed)]
    all_gather x1, waiting for transfers between devices: 0.01 us -> 12.8 us  [shards(): middle_found = lax.all_gather(kept, 'x', axis=0)]
    all_to_all x0 -> x2, waiting for transfers between devices: none -> 9.75 us  [the longest x1 9.75 us: shards(): got = lax.all_to_all(sent, DEPTH, 0, 0, tiled=True)]
    all_to_all x4 -> x3, waiting for transfers between devices: 26.4 us -> 17.5 us  [from_everyone(): lax.all_to_all(jnp.broadcast_to(x[None], (count, *x.shape)), axis, 0, 0,...]
    ppermute x1 -> x0, starting transfers between devices: 8.76 us -> none  [shards(): taken = lax.ppermute(given, 'core', swap)]
    all_to_all x4 -> x3, starting transfers between devices: 32.2 us -> 24.3 us  [from_everyone(): lax.all_to_all(jnp.broadcast_to(x[None], (count, *x.shape)), axis, 0, 0,...]
  transfers between devices with their start and end apart: 17 -> 16, of which waited for: 10 -> 7; matrix products, arithmetic and copies ran while one was open for 5% -> 8% of each run, Pallas kernels for 6% -> 2%
where the time goes in v3:
time: 238 us; the launch traced here: 236 us
  starting transfers between devices  80 us (34%)
  waiting for transfers between devices  72.5 us (30%)
  local copies, waits for them, and re-layouts  29.3 us (12%)
  Pallas kernels  19.5 us (8%)
  blocking collectives  14.8 us (6%)
  between operations  14.4 us (6%)
  other arithmetic  3.41 us (1%)
  matrix products  2.48 us (1%)
    all_to_all x3, starting transfers between devices, from_everyone(): lax.all_to_all(jnp.broadcast_to(x[None], (count, *x.shape)), axis, 0, 0,...  24.3 us
    ppermute x1, waiting for transfers between devices, shards(): lax.ppermute(row, ROWS, crossed)  22.5 us
    ppermute x6, starting transfers between devices, shifted(): lax.ppermute(x, axis, [(i, i + step) for i in range(count) if 0 <= i + st...  18.1 us
    all_to_all x3, waiting for transfers between devices, from_everyone(): lax.all_to_all(jnp.broadcast_to(x[None], (count, *x.shape)), axis, 0, 0,...  17.5 us
    unnamed x46, local copies, waits for them, and re-layouts  17.1 us
    all_to_all x1, starting transfers between devices, shards(): got = lax.all_to_all(sent, DEPTH, 0, 0, tiled=True)  14.9 us
    all_to_all x1, blocking collectives, from_everyone(): lax.all_to_all(jnp.broadcast_to(x[None], (count, *x.shape)), axis, 0, 0,...  14.8 us
    all_gather x1, waiting for transfers between devices, shards(): middle_found = lax.all_gather(kept, 'x', axis=0)  12.8 us
  transfers between devices with their start and end apart: 16, of which 7 were waited for; matrix products, arithmetic and copies ran while one was open for 8% of the time, Pallas kernels for 2%

profile of v3, /device:TPU:1, one launch (start us, length us, event | category | flops | bytes accessed | tf_op | source)
XLA Modules:
  0.0 236.5 jit_solution(10794862780918396517)
XLA Ops:
  6.5 4.7 %collective-permute-start = (bf16[4,1,256]{2,0,1:T(4,128)(2,1)}, bf16[4,1,256]{2,0,1:T(4,128)(2,1)S(1)}, u32[]{:S(2)}, u32[]{:S(2)}) collective-permute-start(bf16[4,1,256]{2,0,1:T(4,128)(2,1)} %param.14), channel_id=1, source_target_pairs={{0,4},{4,8},{8,12},{12,16},{16,20},{20,24},{24,28},{28,32},{32,36}... | collective-permute-start | bytes 6152 | tf_op jit(solution)/shard_map/ppermute | solution.py:431
  11.3 5.5 %collective-permute-start.1 = (bf16[4,1,256]{2,0,1:T(4,128)(2,1)}, bf16[4,1,256]{2,0,1:T(4,128)(2,1)S(1)}, u32[]{:S(2)}, u32[]{:S(2)}) collective-permute-start(bf16[4,1,256]{2,0,1:T(4,128)(2,1)} %param.14), channel_id=1, source_target_pairs={{4,0},{8,4},{12,8},{16,12},{20,16},{24,20},{28,24},{32,28},{36,32}... | collective-permute-start | bytes 6152 | tf_op jit(solution)/shard_map/ppermute | solution.py:431
  23.5 2.2 collective-permute-done.3.right_ref
  27.8 14.9 %all-to-all-start = ((bf16[16,16,320]{2,1,0:T(8,128)(2,1)}), bf16[16,16,320]{2,1,0:T(8,128)(2,1)S(1)}, u32[]{:S(2)}, u32[]{:S(2)}) async-start(bf16[16,16,320]{2,1,0:T(8,128)(2,1)} %get-tuple-element.29), calls=%async_computation | async-start | bytes 393216 | tf_op jit(solution)/shard_map/all_to_all | solution.py:473
  45.3 9.7 %all-to-all-done.got_ref = bf16[16,16,320]{2,1,0:T(8,128)(2,1)S(1)} async-done(((bf16[16,16,320]{2,1,0:T(8,128)(2,1)}), bf16[16,16,320]{2,1,0:T(8,128)(2,1)S(1)}, u32[]{:S(2)}, u32[]{:S(2)}) %all-to-all-start) | async-done | bytes 163872 | tf_op jit(solution)/shard_map/all_to_all | solution.py:473
  55.3 1.4 copy-done.4
  56.8 10.9 %all-to-all-start.1 = ((bf16[32,56,640]{2,1,0:T(8,128)(2,1)}), bf16[32,56,640]{2,1,0:T(8,128)(2,1)S(1)}, u32[]{:S(2)}, u32[]{:S(2)}) async-start(bf16[32,56,640]{2,1,0:T(8,128)(2,1)} %copy-done.4), calls=%async_computation.1 | async-start | bytes 4587520 | tf_op jit(solution)/shard_map/all_to_all | solution.py:477
  67.7 5.2 %collective-permute-start.6 = (bf16[272,384]{1,0:T(8,128)(2,1)}, bf16[272,384]{1,0:T(8,128)(2,1)S(1)}, u32[]{:S(2)}, u32[]{:S(2)}) collective-permute-start(bf16[272,384]{1,0:T(8,128)(2,1)} %copy-done.13), channel_id=1, source_target_pairs={{4,16},{12,24},{16,4},{20,32},{24,12},{28,40},{32,20},{36,48},{40,... | collective-permute-start | bytes 626696 | tf_op jit(solution)/shard_map/ppermute | solution.py:482
  74.2 4.0 %collective-permute-start.4 = (bf16[272,384]{1,0:T(8,128)(2,1)}, bf16[272,384]{1,0:T(8,128)(2,1)S(1)}, u32[]{:S(2)}, u32[]{:S(2)}) collective-permute-start(bf16[272,384]{1,0:T(8,128)(2,1)} %copy-done.13), channel_id=1, source_target_pairs={{0,8},{4,12},{8,16},{12,20},{16,24},{20,28},{24,32},{28,36},{32,40... | collective-permute-start | bytes 626696 | tf_op jit(solution)/shard_map/ppermute | solution.py:431
  78.2 22.5 %collective-permute-done.6 = bf16[272,384]{1,0:T(8,128)(2,1)S(1)} collective-permute-done((bf16[272,384]{1,0:T(8,128)(2,1)}, bf16[272,384]{1,0:T(8,128)(2,1)S(1)}, u32[]{:S(2)}, u32[]{:S(2)}) %collective-permute-start.6) | collective-permute-done | bytes 208928 | tf_op jit(solution)/shard_map/ppermute | solution.py:482
  100.7 7.7 %collective-permute-done.5 = bf16[272,384]{1,0:T(8,128)(2,1)S(1)} collective-permute-done((bf16[272,384]{1,0:T(8,128)(2,1)}, bf16[272,384]{1,0:T(8,128)(2,1)S(1)}, u32[]{:S(2)}, u32[]{:S(2)}) %collective-permute-start.5) | collective-permute-done | bytes 208928 | tf_op jit(solution)/shard_map/ppermute | solution.py:431
  108.4 2.0 pad_maximum_fusion.own_ref
  110.4 1.9 collective-permute-start.7
  113.9 2.1 copy.49
  118.0 2.0 reshape.68
  120.0 1.7 copy.48
  121.8 4.2 %shard_map.138.joined_ref = bf16[2192,640]{1,0:T(8,128)(2,1)S(1)} custom-call(bf16[4,272,384]{2,1,0:T(8,128)(2,1)} %pad_maximum_fusion.own_ref, bf16[4,272,384]{2,1,0:T(8,128)(2,1)} %collective-permute-done.7.other_ref, bf16[384,384]{1,0:T(8,128)(2,1)S(1)} %bitcast.31), custom_call_target="tpu_custom_call" | custom-call | tf_op jit(solution)/shard_map/pallas_call | solution.py:484
  126.0 1.6 copy-done.1
  128.6 2.0 shard_map.140
  130.6 4.4 %shard_map.141 = (f32[1648,256]{1,0:T(8,128)S(1)}, f32[2,160]{1,0:T(2,128)S(1)}) custom-call(bf16[2192,640]{1,0:T(8,128)(2,1)S(1)} %copy-done.2, f32[1,128]{1,0:T(1,128)S(1)} %get-tuple-element.31.stat_ref, bf16[1920,512]{1,0:T(8,128)(2,1)S(1)} %get-tuple-element.32.wm_ref, f32[1,640]{1,0:T(1,128)S(1)} %broadcast_in_dim.33.gain_ref, ...), custom_call_target="tpu_custom_call" | custom-call | tf_op jit(solution)/shard_map/pallas_call | solution.py:500
  135.7 4.1 %all-to-all-start.2 = ((f32[32,2,160]{2,1,0:T(2,128)}), f32[32,2,160]{2,1,0:T(2,128)S(1)}, u32[]{:S(2)}, u32[]{:S(2)}) async-start(f32[32,2,160]{2,1,0:T(2,128)} %broadcast_in_dim.34), calls=%async_computation.2 | async-start | bytes 131072 | tf_op jit(solution)/shard_map/all_to_all | solution.py:426
  140.8 6.3 %all-to-all-done.2 = f32[32,2,160]{2,1,0:T(2,128)S(1)} async-done(((f32[32,2,160]{2,1,0:T(2,128)}), f32[32,2,160]{2,1,0:T(2,128)S(1)}, u32[]{:S(2)}, u32[]{:S(2)}) %all-to-all-start.2) | async-done | bytes 40992 | tf_op jit(solution)/shard_map/all_to_all | solution.py:426
  147.1 2.3 collective-permute-start.8
  150.1 8.2 %all-to-all-start.3 = ((f32[16,4,160]{2,1,0:T(4,128)}), f32[16,4,160]{2,1,0:T(4,128)S(1)}, u32[]{:S(2)}, u32[]{:S(2)}) async-start(f32[16,4,160]{2,1,0:T(4,128)} %broadcast_in_dim.36), calls=%async_computation.3 | async-start | bytes 131072 | tf_op jit(solution)/shard_map/all_to_all | solution.py:426
  158.4 12.8 %all-gather.3.cloned.1.call-done = bf16[896,640]{1,0:T(8,128)(2,1)} async-done(((bf16[224,640]{1,0:T(8,128)(2,1)}), bf16[896,640]{1,0:T(8,128)(2,1)}) %all-gather.3.cloned.1.call-update) | async-done | bytes 1146896 | tf_op jit(solution)/shard_map/all_gather | solution.py:492
  171.1 1.8 copy-done.3
  179.6 4.5 %shard_map.143 = (f32[1104,256]{1,0:T(8,128)S(1)}, f32[2,160]{1,0:T(2,128)S(1)}) custom-call(f32[1648,256]{1,0:T(8,128)S(1)} %get-tuple-element.36.own_ref, f32[1648,256]{1,0:T(8,128)} %collective-permute-done.8.other_ref, f32[16,4,160]{2,1,0:T(4,128)S(1)} %all-to-all-done.3.stat_ref, f32[2,160]{1,0:T(2,128)S(1)} %reshape.72.gain_ref, ...), custom_call_target="tpu_custom_call" | custom-call | tf_op jit(solution)/shard_map/pallas_call | solution.py:517
  185.2 14.8 %all_to_all.30 = f32[32,2,160]{2,1,0:T(2,128)S(1)} all-to-all(f32[32,2,160]{2,1,0:T(2,128)S(1)} %broadcast_in_dim.37), channel_id=1, replica_groups=mesh['zp'=8,'zl'=2,'y'=4,'core'=2,'x'=4] {'y','core','x'}, dimensions={0} | all-to-all | bytes 81920 | tf_op jit(solution)/shard_map/all_to_all | solution.py:426
  200.1 2.3 collective-permute-start.9
  203.0 12.0 %all-to-all-start.5 = ((f32[16,4,160]{2,1,0:T(4,128)}), f32[16,4,160]{2,1,0:T(4,128)S(1)}, u32[]{:S(2)}, u32[]{:S(2)}) async-start(f32[16,4,160]{2,1,0:T(4,128)} %broadcast_in_dim.39), calls=%async_computation.5 | async-start | bytes 131072 | tf_op jit(solution)/shard_map/all_to_all | solution.py:426
  215.4 11.2 %all-to-all-done.5.stat_ref = f32[16,4,160]{2,1,0:T(4,128)S(1)} async-done(((f32[16,4,160]{2,1,0:T(4,128)}), f32[16,4,160]{2,1,0:T(4,128)S(1)}, u32[]{:S(2)}, u32[]{:S(2)}) %all-to-all-start.5) | async-done | bytes 40992 | tf_op jit(solution)/shard_map/all_to_all | solution.py:426
  227.9 1.7 shard_map.144
  (93 shorter events, 29.3 us)
Async XLA Ops:
  6.5 106.6 %copy-start = (bf16[1280,320]{0,1:T(8,128)(2,1)S(1)}, bf16[1280,320]{0,1:T(8,128)(2,1)}, u32[]{:S(2)}) copy-start(bf16[1280,320]{0,1:T(8,128)(2,1)} %param.24) | copy-start | bytes 2457604
  6.5 11.6 %collective-permute-start = (bf16[4,1,256]{2,0,1:T(4,128)(2,1)}, bf16[4,1,256]{2,0,1:T(4,128)(2,1)S(1)}, u32[]{:S(2)}, u32[]{:S(2)}) collective-permute-start(bf16[4,1,256]{2,0,1:T(4,128)(2,1)} %param.14), channel_id=1, source_target_pairs={{0,4},{4,8},{8,12},{12,16},{16,20},{20,24},{24,28},{28,32},{32,36}... | collective-permute-start | bytes 6152 | tf_op jit(solution)/shard_map/ppermute | solution.py:431
  11.3 6.9 %collective-permute-start.1 = (bf16[4,1,256]{2,0,1:T(4,128)(2,1)}, bf16[4,1,256]{2,0,1:T(4,128)(2,1)S(1)}, u32[]{:S(2)}, u32[]{:S(2)}) collective-permute-start(bf16[4,1,256]{2,0,1:T(4,128)(2,1)} %param.14), channel_id=1, source_target_pairs={{4,0},{8,4},{12,8},{16,12},{20,16},{24,20},{28,24},{32,28},{36,32}... | collective-permute-start | bytes 6152 | tf_op jit(solution)/shard_map/ppermute | solution.py:431
  19.9 3.6 %collective-permute-start.2 = (bf16[16,384]{1,0:T(8,128)(2,1)S(1)}, bf16[16,384]{1,0:T(8,128)(2,1)S(1)}, u32[]{:S(2)}, u32[]{:S(2)}) collective-permute-start(bf16[16,384]{1,0:T(8,128)(2,1)S(1)} %get-tuple-element.26), channel_id=1, source_target_pairs={{0,1},{1,2},{2,3},{4,5},{5,6},{6,7},{8,9},{9,10},{10,11},{12,13},{... | collective-permute-start | bytes 36872 | tf_op jit(solution)/shard_map/ppermute | solution.py:431
  21.2 4.4 %collective-permute-start.3 = (bf16[16,384]{1,0:T(8,128)(2,1)S(1)}, bf16[16,384]{1,0:T(8,128)(2,1)S(1)}, u32[]{:S(2)}, u32[]{:S(2)}) collective-permute-start(bf16[16,384]{1,0:T(8,128)(2,1)S(1)} %get-tuple-element.27), channel_id=1, source_target_pairs={{1,0},{2,1},{3,2},{5,4},{6,5},{7,6},{9,8},{10,9},{11,10},{13,12},{... | collective-permute-start | bytes 36872 | tf_op jit(solution)/shard_map/ppermute | solution.py:431
  27.8 27.3 %all-to-all-start = ((bf16[16,16,320]{2,1,0:T(8,128)(2,1)}), bf16[16,16,320]{2,1,0:T(8,128)(2,1)S(1)}, u32[]{:S(2)}, u32[]{:S(2)}) async-start(bf16[16,16,320]{2,1,0:T(8,128)(2,1)} %get-tuple-element.29), calls=%async_computation | async-start | bytes 393216 | tf_op jit(solution)/shard_map/all_to_all | solution.py:473
  55.3 1.4 copy-start.4
  56.8 70.8 %all-to-all-start.1 = ((bf16[32,56,640]{2,1,0:T(8,128)(2,1)}), bf16[32,56,640]{2,1,0:T(8,128)(2,1)S(1)}, u32[]{:S(2)}, u32[]{:S(2)}) async-start(bf16[32,56,640]{2,1,0:T(8,128)(2,1)} %copy-done.4), calls=%async_computation.1 | async-start | bytes 4587520 | tf_op jit(solution)/shard_map/all_to_all | solution.py:477
  67.7 44.6 %copy-start.19 = (f32[640]{0:T(1024)S(1)}, f32[640]{0:T(1024)}, u32[]{:S(2)}) copy-start(f32[640]{0:T(1024)} %param.25) | copy-start | bytes 7684
  67.7 44.6 %copy-start.17 = (bf16[160,320]{1,0:T(8,128)(2,1)S(1)}, bf16[160,320]{1,0:T(8,128)(2,1)}, u32[]{:S(2)}) copy-start(bf16[160,320]{1,0:T(8,128)(2,1)} %param.20) | copy-start | bytes 307204
  67.7 33.0 %collective-permute-start.6 = (bf16[272,384]{1,0:T(8,128)(2,1)}, bf16[272,384]{1,0:T(8,128)(2,1)S(1)}, u32[]{:S(2)}, u32[]{:S(2)}) collective-permute-start(bf16[272,384]{1,0:T(8,128)(2,1)} %copy-done.13), channel_id=1, source_target_pairs={{4,16},{12,24},{16,4},{20,32},{24,12},{28,40},{32,20},{36,48},{40,... | collective-permute-start | bytes 626696 | tf_op jit(solution)/shard_map/ppermute | solution.py:482
  72.9 35.5 %collective-permute-start.5 = (bf16[272,384]{1,0:T(8,128)(2,1)}, bf16[272,384]{1,0:T(8,128)(2,1)S(1)}, u32[]{:S(2)}, u32[]{:S(2)}) collective-permute-start(bf16[272,384]{1,0:T(8,128)(2,1)} %copy-done.13), channel_id=1, source_target_pairs={{8,0},{12,4},{16,8},{20,12},{24,16},{28,20},{32,24},{36,28},{40,32... | collective-permute-start | bytes 626696 | tf_op jit(solution)/shard_map/ppermute | solution.py:431
  74.2 34.2 %collective-permute-start.4 = (bf16[272,384]{1,0:T(8,128)(2,1)}, bf16[272,384]{1,0:T(8,128)(2,1)S(1)}, u32[]{:S(2)}, u32[]{:S(2)}) collective-permute-start(bf16[272,384]{1,0:T(8,128)(2,1)} %copy-done.13), channel_id=1, source_target_pairs={{0,8},{4,12},{8,16},{12,20},{16,24},{20,28},{24,32},{28,36},{32,40... | collective-permute-start | bytes 626696 | tf_op jit(solution)/shard_map/ppermute | solution.py:431
  110.4 11.3 %collective-permute-start.7 = (bf16[4,272,384]{2,1,0:T(8,128)(2,1)}, bf16[4,272,384]{2,1,0:T(8,128)(2,1)}, u32[]{:S(2)}, u32[]{:S(2)}) collective-permute-start(bf16[4,272,384]{2,1,0:T(8,128)(2,1)} %pad_maximum_fusion.own_ref), channel_id=1, source_target_pairs={{0,4},{4,0},{1,5},{5,1},{2,6},{6,2},{3,7},{7,3},{8,12},{12,8},{9,1... | collective-permute-start | bytes 2506760 | tf_op jit(solution)/shard_map/ppermute | solution.py:486
  126.0 1.6 copy-start.1
  127.5 1.1 copy-start.5
  128.6 2.0 copy-start.2
  130.6 9.3 %copy-start.16 = (bf16[224,4,160]{0,2,1:T(8,128)(2,1)S(1)}, bf16[224,4,160]{0,2,1:T(8,128)(2,1)}, u32[]{:S(2)}) copy-start(bf16[224,4,160]{0,2,1:T(8,128)(2,1)} %copy.48) | copy-start | bytes 860164
  135.0 23.2 %copy-start.20 = (f32[320]{0:T(512)S(1)}, f32[320]{0:T(512)}, u32[]{:S(2)}) copy-start(f32[320]{0:T(512)} %param.26) | copy-start | bytes 3844
  135.7 11.4 %all-to-all-start.2 = ((f32[32,2,160]{2,1,0:T(2,128)}), f32[32,2,160]{2,1,0:T(2,128)S(1)}, u32[]{:S(2)}, u32[]{:S(2)}) async-start(f32[32,2,160]{2,1,0:T(2,128)} %broadcast_in_dim.34), calls=%async_computation.2 | async-start | bytes 131072 | tf_op jit(solution)/shard_map/all_to_all | solution.py:426
  139.8 31.3 %all-gather.3.cloned.1.call-start = ((), (), s32[]{:S(2)}) async-start(), calls=%async_computation.6 | async-start | bytes 1433600 | tf_op jit(solution)/shard_map/all_gather | solution.py:492
  147.1 29.9 %collective-permute-start.8 = (f32[1648,256]{1,0:T(8,128)S(1)}, f32[1648,256]{1,0:T(8,128)}, u32[]{:S(2)}, u32[]{:S(2)}) collective-permute-start(f32[1648,256]{1,0:T(8,128)S(1)} %get-tuple-element.36.own_ref), channel_id=1, source_target_pairs={{0,4},{4,0},{1,5},{5,1},{2,6},{6,2},{3,7},{7,3},{8,12},{12,8},{9,1... | collective-permute-start | bytes 5062664 | tf_op jit(solution)/shard_map/ppermute | solution.py:516
  150.1 27.0 %all-to-all-start.3 = ((f32[16,4,160]{2,1,0:T(4,128)}), f32[16,4,160]{2,1,0:T(4,128)S(1)}, u32[]{:S(2)}, u32[]{:S(2)}) async-start(f32[16,4,160]{2,1,0:T(4,128)} %broadcast_in_dim.36), calls=%async_computation.3 | async-start | bytes 131072 | tf_op jit(solution)/shard_map/all_to_all | solution.py:426
  171.1 1.8 copy-start.3
  172.9 1.3 copy-start.8
  177.0 1.3 copy-start.7
  178.3 1.3 copy-start.10
  179.6 35.5 %copy-start.21 = (f32[320]{0:T(512)S(1)}, f32[320]{0:T(512)}, u32[]{:S(2)}) copy-start(f32[320]{0:T(512)} %param.27) | copy-start | bytes 3844
  179.6 35.6 %copy-start.18 = (bf16[2880,4]{0,1:T(4,128)(2,1)S(1)}, bf16[2880,4]{0,1:T(4,128)(2,1)}, u32[]{:S(2)}) copy-start(bf16[2880,4]{0,1:T(4,128)(2,1)} %param.21) | copy-start | bytes 69124
  200.1 26.6 %collective-permute-start.9 = (f32[1104,256]{1,0:T(8,128)}, f32[1104,256]{1,0:T(8,128)S(1)}, u32[]{:S(2)}, u32[]{:S(2)}) collective-permute-start(f32[1104,256]{1,0:T(8,128)} %copy-done.11), channel_id=1, source_target_pairs={{0,4},{4,0},{1,5},{5,1},{2,6},{6,2},{3,7},{7,3},{8,12},{12,8},{9,1... | collective-permute-start | bytes 3391496 | tf_op jit(solution)/shard_map/ppermute | solution.py:527
  203.0 23.7 %all-to-all-start.5 = ((f32[16,4,160]{2,1,0:T(4,128)}), f32[16,4,160]{2,1,0:T(4,128)S(1)}, u32[]{:S(2)}, u32[]{:S(2)}) async-start(f32[16,4,160]{2,1,0:T(4,128)} %broadcast_in_dim.39), calls=%async_computation.5 | async-start | bytes 131072 | tf_op jit(solution)/shard_map/all_to_all | solution.py:426
  226.7 1.3 copy-start.12
  (6 other events, 5.3 us)
Sparse Core Ops, SparseCore 0:
  142.8 28.3 all-gather.2

commit v4 on v3

--- a/solution.py
+++ b/solution.py
@@ -31,14 +31,15 @@
 LANES = 384
 SWAP = 256
 VMEM = pl.BlockSpec(memory_space=pltpu.VMEM)
-
-
-def call(kernel, out_shape, in_specs, scratch=(), limit=16):
+ANY = pl.BlockSpec(memory_space=pltpu.HBM)
+
+
+def call(kernel, out_shape, in_specs, scratch=(), limit=16, out_spec=VMEM):
     return pl.pallas_call(
         kernel,
         out_shape=out_shape,
         in_specs=in_specs,
-        out_specs=jax.tree.map(lambda _: VMEM, out_shape),
+        out_specs=jax.tree.map(lambda _: out_spec, out_shape),
         scratch_shapes=list(scratch),
         compiler_params=pltpu.CompilerParams(vmem_limit_bytes=limit * 1024 * 1024),
     )
@@ -74,7 +75,7 @@
     return h + h * jnp.tanh(h)
 
 
-def pack_kernel(deep_ref, prev_ref, here_ref, next_ref, out_ref, first_ref, last_ref, tall):
+def pack_kernel(deep_ref, prev_ref, here_ref, next_ref, weight_ref, out_ref, first_ref, last_ref, wpad_ref, tall, wide):
     tall[0:C, :] = deep_ref[...].astype(F32)
     tall[C:LANES, :] = jnp.zeros((LANES - C, WIDE), F32)
     for i, ref in enumerate((prev_ref, here_ref, next_ref)):
@@ -83,6 +84,13 @@
     out_ref[...] = out
     first_ref[...] = out[0:GAP]
     last_ref[...] = out[WIDE - GAP : WIDE]
+    wide[...] = jnp.zeros((LANES, LANES), F32)
+    weight = weight_ref[...].astype(F32)
+    for tap in range(9):
+        a, b = divmod(tap, 3)
+        at = 128 * b + 64 + 4 * a
+        wide[at : at + 4, 64:LANES] = weight[4 * tap : 4 * tap + 4]
+    wpad_ref[...] = wide[...].astype(BF16)
 
 
 def skip_of(tail, wpad_ref, lo, hi):
@@ -124,7 +132,7 @@
         sent_ref[z] = message
 
 
-def plane_kernel(got_ref, part_ref, sent_ref, rows):
+def plane_kernel(got_ref, part_ref, sent_hbm, rows, blocks, sems):
     total = jnp.zeros((1, 64), F32)
     for z in range(16):
         got = got_ref[z].astype(F32)
@@ -135,12 +143,16 @@
     first = jnp.concatenate([*three_terms(total), jnp.zeros((1, 4 * HALF - 192), F32)], axis=1)
     second = jnp.concatenate([*three_terms(part_ref[...]), jnp.zeros((1, HALF), F32)], axis=1)
     tail = jnp.concatenate([first, second, jnp.zeros((6, 4 * HALF), F32)], axis=0).astype(BF16)
+    copies = []
     for half in (0, 1):
-        block = rows[half].astype(BF16)
-        for y in range(4):
-            for x in range(4):
-                sent_ref[8 * y + 4 * half + x, 0:48, :] = block
-                sent_ref[8 * y + 4 * half + x, 48:56, :] = tail
+        blocks[half, 0:48, :] = rows[half].astype(BF16)
+        blocks[half, 48:56, :] = tail
+        for i in range(16):
+            goal = 8 * (i // 4) + 4 * half + i % 4
+            copies.append(pltpu.make_async_copy(blocks.at[half], sent_hbm.at[goal], sems.at[goal]))
+            copies[-1].start()
+    for copy in copies:
+        copy.wait()
 
 
 def keep_mask(r, first_row, first_col):
@@ -212,13 +224,20 @@
 
 
 def first_kernel(
-    joined_ref, stat_ref, wm_ref, gain_ref, shift_ref,
+    joined_hbm, found_hbm, proj_ref, gain_ref,
     hidden_ref, sum_ref,
-    act, merged,
+    joined_ref, found_ref, rows, wm_ref, act, merged, sems,
 ):
+    copies = [pltpu.make_async_copy(found_hbm, found_ref, sems.at[0])]
+    for i, part in enumerate((slice(0, 4 * SEG), slice(4 * SEG, A_LEN))):
+        copies.append(pltpu.make_async_copy(joined_hbm.at[part], joined_ref.at[part], sems.at[i + 1]))
+    for copy in copies:
+        copy.start()
+    copies[0].wait()
     chip_row, first_col, _ = place()
     first_row = chip_row - 3
-    totals = stat_ref[...] / (20.0 * 131072.0)
+    sums, shift = front_weight(found_ref, proj_ref, wm_ref, rows)
+    totals = sums / (20.0 * 131072.0)
     mean = totals[:, 0:32]
     var = totals[:, 32:64] - mean * mean
     pair = jnp.concatenate([lax.rsqrt(var + EPS), mean, jnp.zeros((6, 32), F32)], axis=0)
@@ -240,8 +259,10 @@
 
     merged[0:GAP, :] = jnp.zeros((GAP, MERGED), F32)
     merged[GAP + H_LEN : GAP + H_LEN + GAP, :] = jnp.zeros((GAP, MERGED), F32)
+    copies[1].wait()
     for r in range(4):
         build(r)
+    copies[2].wait()
     conv(0, 2 * SEG)
     build(4)
     build(5)
@@ -254,29 +275,64 @@
     squares = jnp.zeros((1, HALF), F32)
     for r in range(MID_ROWS + 1):
         size = SEG if r < MID_ROWS else GAP
-        values = shift_add(merged, GAP + r * SEG, size) + shift_ref[...]
+        values = shift_add(merged, GAP + r * SEG, size) + shift
         hidden_ref[r * SEG : r * SEG + size, 0:HALF] = values
         if r in (2, 3):
             sums = sums + jnp.sum(values[GAP:], axis=0, keepdims=True)
             squares = squares + jnp.sum(values[GAP:] * values[GAP:], axis=0, keepdims=True)
     hidden_ref[:, HALF:SWAP] = jnp.zeros((H_LEN, SWAP - HALF), F32)
-    sum_ref[...] = jnp.concatenate([sums, squares], axis=0)
+    send_sums(sums, squares, sum_ref)
+
+
+def send_sums(sums, squares, sent_ref):
+    both = jnp.concatenate([sums, squares, jnp.zeros((6, HALF), F32)], axis=0)
+    grouped = exact_dot(both, same_group(HALF, 16, 10, 1))
+    line = jnp.concatenate([grouped[0:1], grouped[1:2], jnp.zeros((1, 96), F32)], axis=1)
+    for i in range(32):
+        sent_ref[i] = line
+
+
+def plane_sums_kernel(got_ref, sent_ref):
+    cores = [jnp.zeros((1, 32), F32), jnp.zeros((1, 32), F32)]
+    for i in range(32):
+        half = (i // 4) % 2
+        cores[half] = cores[half] + got_ref[i][:, 0:32]
+    line = jnp.concatenate([*cores, jnp.zeros((1, 64), F32)], axis=1)
+    for i in range(sent_ref.shape[0]):
+        sent_ref[i] = line
 
 
 def affine(stat_ref, gain_ref):
-    both = jnp.sum(stat_ref[...], axis=0)
+    both = stat_ref[0]
+    for i in range(1, stat_ref.shape[0]):
+        both = both + stat_ref[i]
     found = []
     for which in (0, 1):
-        sums = both[2 * which : 2 * which + 2]
-        padded = jnp.concatenate([sums, jnp.zeros((6, HALF), F32)], axis=0)
-        totals = exact_dot(padded, same_group(HALF, HALF, 10, 10)) / (10.0 * 131072.0)
+        at = 32 * which
+        padded = jnp.concatenate([both[:, at : at + 16], both[:, at + 16 : at + 32], jnp.zeros((6, 16), F32)], axis=0)
+        totals = exact_dot(padded, same_group(16, HALF, 1, 10)) / (10.0 * 131072.0)
         mean = totals[0:1]
         scale = lax.rsqrt(totals[1:2] - mean * mean + EPS) * gain_ref[which : which + 1] * 0.5
         found.append((scale, -mean * scale))
     return found
 
 
-def second_kernel(own_ref, other_ref, stat_ref, gain_ref, wm_ref, short_ref, block_ref, sum_ref, act, merged):
+def second_kernel(
+    own_hbm, other_hbm, stat_ref, gain_ref, found_hbm, joined_hbm,
+    block_ref, sum_ref,
+    own_ref, other_ref, found_ref, joined_ref, wm_ref, skip, act, merged, sems,
+):
+    early, late = slice(0, 4 * SEG), slice(4 * SEG, H_LEN)
+    copies = [
+        pltpu.make_async_copy(own_hbm.at[early], own_ref.at[early], sems.at[0]),
+        pltpu.make_async_copy(other_hbm.at[early], other_ref.at[early], sems.at[1]),
+        pltpu.make_async_copy(found_hbm, found_ref, sems.at[2]),
+        pltpu.make_async_copy(own_hbm.at[late], own_ref.at[late], sems.at[3]),
+        pltpu.make_async_copy(other_hbm.at[late], other_ref.at[late], sems.at[4]),
+        pltpu.make_async_copy(joined_hbm.at[2 * SEG : 2 * SEG + B_LEN], joined_ref, sems.at[5]),
+    ]
+    for copy in copies:
+        copy.start()
     chip_row, first_col, core = place()
     first_row = chip_row - 2
     affines = affine(stat_ref, gain_ref)
@@ -299,37 +355,53 @@
 
     merged[0:GAP, :] = jnp.zeros((GAP, MERGED), F32)
     merged[GAP + B_LEN : GAP + B_LEN + GAP, :] = jnp.zeros((GAP, MERGED), F32)
+    copies[0].wait()
+    copies[1].wait()
     for r in range(4):
         build(r)
+    copies[2].wait()
+    middle_weight(found_ref, wm_ref, skip)
+    copies[3].wait()
+    copies[4].wait()
     conv(0, 2 * SEG)
     for r in range(4, 7):
         build(r)
     conv(2 * SEG, 2 * SEG + GAP)
+    copies[5].wait()
 
     sums = jnp.zeros((1, HALF), F32)
     squares = jnp.zeros((1, HALF), F32)
     for r in range(OUT_ROWS + 1):
         size = SEG if r < OUT_ROWS else GAP
         where = slice(r * SEG, r * SEG + size)
-        values = shift_add(merged, GAP + r * SEG, size) + short_ref[where, :]
+        values = shift_add(merged, GAP + r * SEG, size) + tap_dot(joined_ref[where, :], skip[...])
         block_ref[where, 0:HALF] = values
         if r in (1, 2):
             sums = sums + jnp.sum(values[GAP:], axis=0, keepdims=True)
             squares = squares + jnp.sum(values[GAP:] * values[GAP:], axis=0, keepdims=True)
     block_ref[:, HALF:SWAP] = jnp.zeros((B_LEN, SWAP - HALF), F32)
-    sum_ref[...] = jnp.concatenate([sums, squares], axis=0)
-
-
-def third_kernel(own_ref, other_ref, stat_ref, gain_ref, wout_ref, noise_ref):
+    send_sums(sums, squares, sum_ref)
+
+
+def third_kernel(own_hbm, other_hbm, stat_ref, gain_ref, wout_ref, noise_ref, own_ref, other_ref, sems):
     chip_row, first_col, core = place()
+    needed = pl.ds(pl.multiple_of(core * SEG, 16), 3 * SEG + GAP)
+    copies = [
+        pltpu.make_async_copy(own_hbm.at[needed], own_ref, sems.at[0]),
+        pltpu.make_async_copy(other_hbm.at[needed], other_ref, sems.at[1]),
+    ]
+    for copy in copies:
+        copy.start()
     first_row = chip_row - 1 + core
     affines = affine(stat_ref, gain_ref)
     first = core == 0
+    for copy in copies:
+        copy.wait()
     parts = []
     for r in range(4):
         size = SEG if r < 3 else GAP
         mask = keep_mask(r, first_row, first_col)[0:size]
-        where = rows_at(core * SEG + r * SEG, size)
+        where = slice(r * SEG, r * SEG + size)
         total = None
         own, other = own_ref[where, 0:HALF], other_ref[where, 0:HALF]
         for which, (scale, offset) in enumerate(affines):
@@ -356,7 +428,7 @@
     out_ref[at : at + size, 384 + 32 * b : 384 + 32 * (b + 1)] = piece[:, 128:160]
 
 
-def front_weight_kernel(found_ref, proj_ref, out_ref, stat_ref, shift_ref, rows):
+def front_weight(found_ref, proj_ref, out_ref, rows):
     out_ref[:, 480:512] = jnp.zeros((3 * 2 * C, 32), BF16)
     sums = jnp.zeros((1, 64), F32)
     embedded = []
@@ -373,14 +445,12 @@
                 sums = sums + found[48:49, 64 * term : 64 * (term + 1)]
                 part = part + found[49:50, HALF * term : HALF * (term + 1)]
         embedded.append(part)
-    stat_ref[...] = jnp.concatenate([sums, jnp.zeros((1, 64), F32)], axis=1)
-    values = jnp.concatenate(embedded, axis=0)
-    values = jnp.concatenate([values / (1.0 + jnp.exp(-values)), jnp.zeros((8, WIDE - HALF), F32)], axis=1)
-    turned = jnp.concatenate([values, jnp.zeros((120, WIDE), F32)], axis=0).T[0:HALF]
-    shift = jnp.zeros((HALF, HALF), F32)
-    for shard in range(8):
-        shift = shift + turned[:, shard : shard + 1] * proj_ref[shard].astype(F32)
-    shift_ref[...] = jnp.sum(shift, axis=0, keepdims=True)
+    values = jnp.concatenate(embedded, axis=1)
+    values = values / (1.0 + jnp.exp(-values))
+    proj = proj_ref[rows_at(lax.axis_index("core") * HALF, HALF), :].astype(F32)
+    shift = jnp.sum(proj * values, axis=1, keepdims=True)
+    shift = jnp.concatenate([jnp.broadcast_to(shift, (HALF, 128)), jnp.zeros((WIDE - HALF, 128), F32)], axis=0)
+    shift = shift.T[0:1, 0:HALF]
     for q in range(4):
         row = 1440 * q
         while row < 1440 * (q + 1):
@@ -391,9 +461,20 @@
             piece = rows[k : k + size, 160 * q : 160 * (q + 1)].astype(BF16)
             place_merged(out_ref, a * 2 * C + channel, size, b, piece)
             row += size
-
-
-def middle_weight_kernel(found_ref, joined_ref, out_ref, short_ref, skip):
+    return sums, shift
+
+
+def share_kernel(middle_ref, skip_ref, out_ref):
+    core = lax.axis_index("core")
+    middle = middle_ref[rows_at(core * HALF, HALF), :].astype(F32).T
+    wide = skip_ref[...].astype(F32)
+    skip = jnp.where(core == 0, wide[:, 0:HALF], wide[:, HALF:C])
+    whole = jnp.concatenate([middle, skip, jnp.zeros((16, HALF), F32)], axis=0)
+    parts = [whole[224 * q : 224 * (q + 1)] for q in range(4)]
+    out_ref[...] = jnp.concatenate(parts, axis=1).astype(BF16)
+
+
+def middle_weight(found_ref, out_ref, skip_ref):
     out_ref[:, 480:512] = jnp.zeros((3 * LANES, 32), BF16)
 
     def pieces(x, row, size):
@@ -416,14 +497,8 @@
     at = 0
     for x in range(4):
         for size, piece in pieces(x, 720, HALF):
-            skip[at : at + size, :] = piece
+            skip_ref[at : at + size, :] = piece
             at += size
-    short_ref[...] = tap_dot(joined_ref[2 * SEG : 2 * SEG + B_LEN, :], skip[...])
-
-
-def from_everyone(x, axis):
-    count = lax.axis_size(axis)
-    return lax.all_to_all(jnp.broadcast_to(x[None], (count, *x.shape)), axis, 0, 0, tiled=True)
 
 
 def shifted(x, axis, step):
@@ -431,10 +506,11 @@
     return lax.ppermute(x, axis, [(i, i + step) for i in range(count) if 0 <= i + step < count])
 
 
-def summed_halves(sums, kept):
-    near = from_everyone(sums, PLANE).reshape(4, 2, 4, 2, HALF).sum(axis=(0, 2))
+def summed(sums, kept):
+    near = lax.all_to_all(sums, PLANE, 0, 0, tiled=True)
+    near = call(plane_sums_kernel, sds((lax.axis_size(DEPTH), 1, 128), F32), [VMEM])(near)
     near, kept = lax.optimization_barrier((near, kept))
-    return from_everyone(near.reshape(4, HALF), DEPTH), kept
+    return lax.all_to_all(near, DEPTH, 0, 0, tiled=True), kept
 
 
 def shards(
@@ -444,20 +520,28 @@
     core, x, y = lax.axis_index("core"), lax.axis_index("x"), lax.axis_index("y")
     depths = lax.axis_size(DEPTH)
 
+    packed = call(share_kernel, sds((224, 4 * HALF), BF16), [VMEM] * 2)(middle_weight.T, skip_weight)
+
     above, below = shifted(latent, ROWS, 1), shifted(latent, ROWS, -1)
-    cells, first, last = call(
+    quarter = lax.dynamic_slice_in_dim(jnp.pad(front_weight, ((0, 3), (0, 0))), 12 * x, 12, 0)
+    above, packed, quarter = lax.optimization_barrier((above, packed, quarter))
+    cells, first, last, wpad = call(
         pack_kernel,
-        (sds((WIDE, LANES), BF16), sds((GAP, LANES), BF16), sds((GAP, LANES), BF16)),
-        [VMEM] * 4,
-        [pltpu.VMEM((LANES, WIDE), F32)],
-    )(deep.reshape(C, WIDE), above.reshape(4, WIDE), latent.reshape(4, WIDE), below.reshape(4, WIDE))
+        (sds((WIDE, LANES), BF16), sds((GAP, LANES), BF16), sds((GAP, LANES), BF16), sds((LANES, LANES), BF16)),
+        [VMEM] * 5,
+        [pltpu.VMEM((LANES, WIDE), F32), pltpu.VMEM((LANES, LANES), F32)],
+    )(deep.reshape(C, WIDE), above.reshape(4, WIDE), latent.reshape(4, WIDE), below.reshape(4, WIDE), in_weight)
     from_right, from_left = shifted(first, "x", -1), shifted(last, "x", 1)
-    wpad = in_weight.reshape(3, 3, 4, C).transpose(1, 0, 2, 3).reshape(3, 12, C)
-    wpad = jnp.pad(wpad, ((0, 0), (64, 52), (64, 0))).reshape(LANES, LANES)
-    quarter = lax.dynamic_slice_in_dim(jnp.pad(front_weight, ((0, 3), (0, 0))), 12 * x, 12, 0)
+    packed, from_right, from_left = lax.optimization_barrier((packed, from_right, from_left))
+    middle_found = lax.all_gather(packed, "x", axis=0)
     row, sent = call(stats_kernel, (sds((SEG, LANES), BF16), sds((depths, 16, C), BF16)), [VMEM] * 5)(
         cells, from_left, from_right, wpad, quarter
     )
+
+    count = lax.axis_size(ROWS)
+    crossed = [(i, i + 3) if i % 2 else (i, i - 3) for i in range(count)]
+    crossed = [(i, j) for i, j in crossed if 0 <= j < count]
+    before, after, across = shifted(row, ROWS, 2), shifted(row, ROWS, -2), lax.ppermute(row, ROWS, crossed)
 
     half_width = time_weight.shape[0] // 2
     ratios = jnp.exp(-math.log(10000.0) * jnp.arange(half_width, dtype=F32) / half_width)
@@ -468,64 +552,67 @@
     hidden = jax.nn.silu(jnp.dot(features, weight_here.astype(F32), precision=HIGH))
     columns = lax.dynamic_slice_in_dim(time_second, (2 * y + core) * HALF, HALF, 1)
     part = jnp.dot(hidden, columns.astype(F32), precision=HIGH)
-    proj = lax.dynamic_slice_in_dim(time_proj, core * HALF, HALF, 1).reshape(8, HALF, HALF)
 
     got = lax.all_to_all(sent, DEPTH, 0, 0, tiled=True)
-    sent = call(plane_kernel, sds((32, 56, 4 * HALF), BF16), [VMEM] * 2, [pltpu.VMEM((2, 48, 4 * HALF), F32)])(
-        got, part[None]
-    )
+    scratch = [
+        pltpu.VMEM((2, 48, 4 * HALF), F32),
+        pltpu.VMEM((2, 56, 4 * HALF), BF16),
+        pltpu.SemaphoreType.DMA((32,)),
+    ]
+    sent = call(plane_kernel, sds((32, 56, 4 * HALF), BF16), [VMEM] * 2, scratch, 52, ANY)(got, part[None])
+    around = jnp.stack([before, row, after, across])
+    sent, around, middle_found = lax.optimization_barrier((sent, around, middle_found))
     found = lax.all_to_all(sent, PLANE, 0, 0, tiled=True)
-
-    count = lax.axis_size(ROWS)
-    crossed = [(i, i + 3) if i % 2 else (i, i - 3) for i in range(count)]
-    crossed = [(i, j) for i, j in crossed if 0 <= j < count]
-    around = jnp.stack([shifted(row, ROWS, 2), row, shifted(row, ROWS, -2), lax.ppermute(row, ROWS, crossed)])
     swap = [(0, 1), (1, 0)]
     joined = call(
-        join_kernel, sds((A_LEN, 2 * C), BF16), [VMEM] * 3, [pltpu.VMEM((A_LEN + 2 * GAP, LANES), BF16)]
+        join_kernel, sds((A_LEN, 2 * C), BF16), [VMEM] * 3, [pltpu.VMEM((A_LEN + 2 * GAP, LANES), BF16)], 60
     )(around, lax.ppermute(around, "core", swap), wpad)
-
-    both = jnp.concatenate([middle_weight, skip_weight], axis=0).reshape(880, 2, HALF)
-    kept = lax.dynamic_slice_in_dim(both, core, 1, 1).reshape(880, HALF)
-    kept = jnp.pad(kept, ((0, 16), (0, 0))).reshape(4, 224, HALF).transpose(1, 0, 2).reshape(224, 4 * HALF)
-    kept, found = lax.optimization_barrier((kept, found))
-    middle_found = lax.all_gather(kept, "x", axis=0)
-
-    front, wide, time_shift = call(
-        front_weight_kernel,
-        (sds((3 * 2 * C, MERGED), BF16), sds((1, 128), F32), sds((1, HALF), F32)),
-        [VMEM] * 2,
-        [pltpu.VMEM((1440, 4 * HALF), F32)],
-    )(found, proj)
     hidden_own, sums = call(
         first_kernel,
-        (sds((H_LEN, SWAP), F32), sds((2, HALF), F32)),
-        [VMEM] * 5,
-        [pltpu.VMEM((A_LEN, 2 * C), BF16), pltpu.VMEM((H_LEN + 2 * GAP, MERGED), F32)],
-        24,
-    )(joined, wide, front, input_gain[None], time_shift)
-
-    middle, shortcut = call(
-        middle_weight_kernel,
-        (sds((3 * LANES, MERGED), BF16), sds((B_LEN, HALF), F32)),
-        [VMEM] * 2,
-        [pltpu.VMEM((2 * C, HALF), BF16)],
-    )(middle_found, joined)
-
-    totals, hidden_own = summed_halves(sums, hidden_own)
+        (sds((H_LEN, SWAP), F32), sds((32, 1, 128), F32)),
+        [ANY, ANY, VMEM, VMEM],
+        [
+            pltpu.VMEM((A_LEN, 2 * C), BF16),
+            pltpu.VMEM((32, 56, 4 * HALF), BF16),
+            pltpu.VMEM((1440, 4 * HALF), F32),
+            pltpu.VMEM((3 * 2 * C, MERGED), BF16),
+            pltpu.VMEM((A_LEN, 2 * C), BF16),
+            pltpu.VMEM((H_LEN + 2 * GAP, MERGED), F32),
+            pltpu.SemaphoreType.DMA((3,)),
+        ],
+        52,
+    )(joined, found, time_proj.T, input_gain[None])
+
+    totals, hidden_own = summed(sums, hidden_own)
     hidden_other = lax.ppermute(hidden_own, "core", swap)
     block_own, sums = call(
         second_kernel,
-        (sds((B_LEN, SWAP), F32), sds((2, HALF), F32)),
-        [VMEM] * 6,
-        [pltpu.VMEM((H_LEN, LANES), BF16), pltpu.VMEM((B_LEN + 2 * GAP, MERGED), F32)],
-    )(hidden_own, hidden_other, totals, middle_gain.reshape(2, HALF), middle, shortcut)
+        (sds((B_LEN, SWAP), F32), sds((32, 1, 128), F32)),
+        [ANY, ANY, VMEM, VMEM, ANY, ANY],
+        [
+            pltpu.VMEM((H_LEN, SWAP), F32),
+            pltpu.VMEM((H_LEN, SWAP), F32),
+            pltpu.VMEM((4, 224, 4 * HALF), BF16),
+            pltpu.VMEM((B_LEN, 2 * C), BF16),
+            pltpu.VMEM((3 * LANES, MERGED), BF16),
+            pltpu.VMEM((2 * C, HALF), BF16),
+            pltpu.VMEM((H_LEN, LANES), BF16),
+            pltpu.VMEM((B_LEN + 2 * GAP, MERGED), F32),
+            pltpu.SemaphoreType.DMA((6,)),
+        ],
+        52,
+    )(hidden_own, hidden_other, totals, middle_gain.reshape(2, HALF), middle_found, joined)
 
     wout = out_weight.reshape(9, 2, HALF, 4).transpose(1, 2, 0, 3)
     wout = jnp.pad(jnp.pad(wout, ((0, 0), (0, 0), (0, 0), (0, 4))).reshape(2, HALF, 72), ((0, 0), (0, 0), (0, 56)))
-    totals, block_own = summed_halves(sums, block_own)
+    totals, block_own = summed(sums, block_own)
     block_other = lax.ppermute(block_own, "core", swap)
-    return call(third_kernel, sds((4, 1, WIDE), F32), [VMEM] * 5)(
+    scratch = [
+        pltpu.VMEM((3 * SEG + GAP, SWAP), F32),
+        pltpu.VMEM((3 * SEG + GAP, SWAP), F32),
+        pltpu.SemaphoreType.DMA((2,)),
+    ]
+    return call(third_kernel, sds((4, 1, WIDE), F32), [ANY, ANY, VMEM, VMEM, VMEM], scratch, 30)(
         block_own, block_other, totals, output_gain.reshape(2, HALF), wout
     )
 

time: 238 us -> 197 us (0.83)
  local copies, waits for them, and re-layouts: 29.3 us -> 6.42 us
  waiting for transfers between devices: 72.5 us -> 50 us
  starting transfers between devices: 80 us -> 70.2 us
  Pallas kernels: 19.5 us -> 29.1 us
  blocking collectives: 14.8 us -> 23.6 us
  other arithmetic: 3.41 us -> 0.26 us
    ppermute x1, waiting for transfers between devices: 22.5 us -> 0.19 us  [shards(): lax.ppermute(row, ROWS, crossed)]
    all_to_all x1, waiting for transfers between devices: 0.01 us -> 18 us  [shards(): found = lax.all_to_all(sent, PLANE, 0, 0, tiled=True)]
    all_gather x1, waiting for transfers between devices: 12.8 us -> 0.07 us  [shards(): middle_found = lax.all_gather(packed, 'x', axis=0)]
    unnamed x46 -> x29, local copies, waits for them, and re-layouts: 17.1 us -> 5.24 us
    all_to_all x1, waiting for transfers between devices: 9.75 us -> 0.01 us  [shards(): got = lax.all_to_all(sent, DEPTH, 0, 0, tiled=True)]
    all_to_all x3 -> x2, starting transfers between devices: 24.3 us -> 15.1 us  [summed(): return (lax.all_to_all(near, DEPTH, 0, 0, tiled=True), kept)]
    all_to_all x1 -> x2, blocking collectives: 14.8 us -> 23.6 us  [summed(): near = lax.all_to_all(sums, PLANE, 0, 0, tiled=True)]
    pallas_call x6 -> x7, Pallas kernels: 13.8 us -> 21.8 us  [the longest x1 9.51 us: shards(): call(first_kernel, (sds((H_LEN, SWAP), F32), sds((32, 1, 128), F32)), [AN...]
  transfers between devices with their start and end apart: 16 -> 15, of which waited for: 7 -> 9; matrix products, arithmetic and copies ran while one was open for 8% -> 2% of each run, Pallas kernels for 2% -> 5%
where the time goes in v4:
time: 197 us; the launch traced here: 196 us
  starting transfers between devices  70.2 us (36%)
  waiting for transfers between devices  50 us (25%)
  Pallas kernels  29.1 us (15%)
  blocking collectives  23.6 us (12%)
  between operations  14.4 us (7%)
  local copies, waits for them, and re-layouts  6.42 us (3%)
    all_to_all x2, blocking collectives, summed(): near = lax.all_to_all(sums, PLANE, 0, 0, tiled=True)  23.6 us
    all_to_all x2, waiting for transfers between devices, summed(): return (lax.all_to_all(near, DEPTH, 0, 0, tiled=True), kept)  22.1 us
    ppermute x6, starting transfers between devices, shifted(): lax.ppermute(x, axis, [(i, i + step) for i in range(count) if 0 <= i + st...  19.1 us
    all_to_all x1, waiting for transfers between devices, shards(): found = lax.all_to_all(sent, PLANE, 0, 0, tiled=True)  18 us
    all_to_all x2, starting transfers between devices, summed(): return (lax.all_to_all(near, DEPTH, 0, 0, tiled=True), kept)  15.1 us
    all_to_all x1, starting transfers between devices, shards(): got = lax.all_to_all(sent, DEPTH, 0, 0, tiled=True)  11.4 us
    all_to_all x1, starting transfers between devices, shards(): found = lax.all_to_all(sent, PLANE, 0, 0, tiled=True)  10.7 us
    pallas_call x1, Pallas kernels, shards(): call(first_kernel, (sds((H_LEN, SWAP), F32), sds((32, 1, 128), F32)), [AN...  9.51 us
  transfers between devices with their start and end apart: 15, of which 9 were waited for; matrix products, arithmetic and copies ran while one was open for 2% of the time, Pallas kernels for 5%

profile of v4, /device:TPU:1, one launch (start us, length us, event | category | flops | bytes accessed | tf_op | source)
XLA Modules:
  0.0 195.6 jit_solution(16913503074492523073)
XLA Ops:
  6.5 4.7 %collective-permute-start = (bf16[4,1,256]{2,0,1:T(4,128)(2,1)}, bf16[4,1,256]{2,0,1:T(4,128)(2,1)S(1)}, u32[]{:S(2)}, u32[]{:S(2)}) collective-permute-start(bf16[4,1,256]{2,0,1:T(4,128)(2,1)} %param.14), channel_id=1, source_target_pairs={{0,4},{4,8},{8,12},{12,16},{16,20},{20,24},{24,28},{28,32},{32,36}... | collective-permute-start | bytes 6152 | tf_op jit(solution)/shard_map/ppermute | solution.py:506
  11.3 5.5 %collective-permute-start.1 = (bf16[4,1,256]{2,0,1:T(4,128)(2,1)}, bf16[4,1,256]{2,0,1:T(4,128)(2,1)S(1)}, u32[]{:S(2)}, u32[]{:S(2)}) collective-permute-start(bf16[4,1,256]{2,0,1:T(4,128)(2,1)} %param.14), channel_id=1, source_target_pairs={{4,0},{8,4},{12,8},{16,12},{20,16},{24,20},{28,24},{32,28},{36,32}... | collective-permute-start | bytes 6152 | tf_op jit(solution)/shard_map/ppermute | solution.py:506
  17.5 1.0 copy-done.3
  19.4 1.0 shard_map.136
  20.5 0.9 copy-done.4
  23.0 1.3 collective-permute-start.2
  24.3 4.0 %collective-permute-start.3 = (bf16[16,384]{1,0:T(8,128)(2,1)S(1)}, bf16[16,384]{1,0:T(8,128)(2,1)S(1)}, u32[]{:S(2)}, u32[]{:S(2)}) collective-permute-start(bf16[16,384]{1,0:T(8,128)(2,1)S(1)} %get-tuple-element.32), channel_id=1, source_target_pairs={{0,1},{1,2},{2,3},{4,5},{5,6},{6,7},{8,9},{9,10},{10,11},{12,13},{... | collective-permute-start | bytes 36872 | tf_op jit(solution)/shard_map/ppermute | solution.py:506
  29.9 1.4 shard_map.138
  31.3 11.4 %all-to-all-start = ((bf16[16,16,320]{2,1,0:T(8,128)(2,1)}), bf16[16,16,320]{2,1,0:T(8,128)(2,1)S(1)}, u32[]{:S(2)}, u32[]{:S(2)}) async-start(bf16[16,16,320]{2,1,0:T(8,128)(2,1)} %get-tuple-element.37), calls=%async_computation | async-start | bytes 393216 | tf_op jit(solution)/shard_map/all_to_all | solution.py:556
  43.1 6.7 %collective-permute-start.6 = (bf16[272,384]{1,0:T(8,128)(2,1)S(1)}, bf16[272,384]{1,0:T(8,128)(2,1)S(1)}, u32[]{:S(2)}, u32[]{:S(2)}) collective-permute-start(bf16[272,384]{1,0:T(8,128)(2,1)S(1)} %get-tuple-element.38), channel_id=1, source_target_pairs={{4,16},{12,24},{16,4},{20,32},{24,12},{28,40},{32,20},{36,48},{40,... | collective-permute-start | bytes 626696 | tf_op jit(solution)/shard_map/ppermute | solution.py:544
  49.8 2.3 %collective-permute-start.4 = (bf16[272,384]{1,0:T(8,128)(2,1)S(1)}, bf16[272,384]{1,0:T(8,128)(2,1)S(1)}, u32[]{:S(2)}, u32[]{:S(2)}) collective-permute-start(bf16[272,384]{1,0:T(8,128)(2,1)S(1)} %get-tuple-element.38), channel_id=1, source_target_pairs={{0,8},{4,12},{8,16},{12,20},{16,24},{20,28},{24,32},{28,36},{32,40... | collective-permute-start | bytes 626696 | tf_op jit(solution)/shard_map/ppermute | solution.py:506
  52.1 1.3 collective-permute-start.5
  53.4 1.2 fusion.1.part_ref
  54.8 4.4 %collective-permute-done.4 = bf16[272,384]{1,0:T(8,128)(2,1)S(1)} collective-permute-done((bf16[272,384]{1,0:T(8,128)(2,1)S(1)}, bf16[272,384]{1,0:T(8,128)(2,1)S(1)}, u32[]{:S(2)}, u32[]{:S(2)}) %collective-permute-start.4) | collective-permute-done | bytes 208928 | tf_op jit(solution)/shard_map/ppermute | solution.py:506
  59.2 2.4 %collective-permute-done.5 = bf16[272,384]{1,0:T(8,128)(2,1)S(1)} collective-permute-done((bf16[272,384]{1,0:T(8,128)(2,1)S(1)}, bf16[272,384]{1,0:T(8,128)(2,1)S(1)}, u32[]{:S(2)}, u32[]{:S(2)}) %collective-permute-start.5) | collective-permute-done | bytes 208928 | tf_op jit(solution)/shard_map/ppermute | solution.py:506
  61.7 1.9 shard_map.139
  63.8 10.7 %all-to-all-start.1 = ((bf16[32,56,640]{2,1,0:T(8,128)(2,1)}), bf16[32,56,640]{2,1,0:T(8,128)(2,1)}, u32[]{:S(2)}, u32[]{:S(2)}) async-start(bf16[32,56,640]{2,1,0:T(8,128)(2,1)} %shard_map.139), calls=%async_computation.1 | async-start | bytes 4587520 | tf_op jit(solution)/shard_map/all_to_all | solution.py:565
  74.5 2.2 %collective-permute-start.7 = (bf16[4,272,384]{2,1,0:T(8,128)(2,1)S(1)}, bf16[4,272,384]{2,1,0:T(8,128)(2,1)S(1)}, u32[]{:S(2)}, u32[]{:S(2)}) collective-permute-start(bf16[4,272,384]{2,1,0:T(8,128)(2,1)S(1)} %pad_maximum_fusion.own_ref), channel_id=1, source_target_pairs={{0,4},{4,0},{1,5},{5,1},{2,6},{6,2},{3,7},{7,3},{8,12},{12,8},{9,1... | collective-permute-start | bytes 2506760 | tf_op jit(solution)/shard_map/ppermute | solution.py:569
  76.8 2.0 %collective-permute-done.7.other_ref = bf16[4,272,384]{2,1,0:T(8,128)(2,1)S(1)} collective-permute-done((bf16[4,272,384]{2,1,0:T(8,128)(2,1)S(1)}, bf16[4,272,384]{2,1,0:T(8,128)(2,1)S(1)}, u32[]{:S(2)}, u32[]{:S(2)}) %collective-permute-start.7) | collective-permute-done | bytes 835616 | tf_op jit(solution)/shard_map/ppermute | solution.py:569
  79.7 5.8 %shard_map.140.joined_hbm = bf16[2192,640]{1,0:T(8,128)(2,1)} custom-call(bf16[4,272,384]{2,1,0:T(8,128)(2,1)} %copy-done.8, bf16[4,272,384]{2,1,0:T(8,128)(2,1)} %copy-done.9, bf16[384,384]{1,0:T(8,128)(2,1)} %copy-done.1), custom_call_target="tpu_custom_call" | custom-call | tf_op jit(solution)/shard_map/pallas_call | solution.py:567
  85.5 18.0 %all-to-all-done.1.found_hbm = bf16[32,56,640]{2,1,0:T(8,128)(2,1)} async-done(((bf16[32,56,640]{2,1,0:T(8,128)(2,1)}), bf16[32,56,640]{2,1,0:T(8,128)(2,1)}, u32[]{:S(2)}, u32[]{:S(2)}) %all-to-all-start.1) | async-done | bytes 2293792 | tf_op jit(solution)/shard_map/all_to_all | solution.py:565
  103.5 9.5 %shard_map.141 = (f32[1648,256]{1,0:T(8,128)}, f32[32,1,128]{2,1,0:T(1,128)S(1)}) custom-call(bf16[2192,640]{1,0:T(8,128)(2,1)} %shard_map.140.joined_hbm, bf16[32,56,640]{2,1,0:T(8,128)(2,1)} %all-to-all-done.1.found_hbm, bf16[320,1280]{1,0:T(8,128)(2,1)S(1)} %bitcast.20, f32[1,640]{1,0:T(1,128)S(1)} %broadcast_in_dim.7.gain_ref), custom_call_target="tpu_custom_call" | custom-call | tf_op jit(solution)/shard_map/pallas_call | solution.py:570
  113.0 12.2 %all_to_all.30.got_ref = f32[32,1,128]{2,1,0:T(1,128)S(1)} all-to-all(f32[32,1,128]{2,1,0:T(1,128)S(1)} %get-tuple-element.42), channel_id=1, replica_groups=mesh['zp'=8,'zl'=2,'y'=4,'core'=2,'x'=4] {'y','core','x'}, dimensions={0} | all-to-all | bytes 32768 | tf_op jit(solution)/shard_map/all_to_all | solution.py:510
  125.9 2.5 %collective-permute-start.8 = (f32[1648,256]{1,0:T(8,128)}, f32[1648,256]{1,0:T(8,128)}, u32[]{:S(2)}, u32[]{:S(2)}) collective-permute-start(f32[1648,256]{1,0:T(8,128)} %get-tuple-element.44.own_hbm), channel_id=1, source_target_pairs={{0,4},{4,0},{1,5},{5,1},{2,6},{6,2},{3,7},{7,3},{8,12},{12,8},{9,1... | collective-permute-start | bytes 5062664 | tf_op jit(solution)/shard_map/ppermute | solution.py:587
  128.5 11.6 %all-to-all-start.3 = ((f32[16,1,128]{2,1,0:T(1,128)}), f32[16,1,128]{2,1,0:T(1,128)S(1)}, u32[]{:S(2)}, u32[]{:S(2)}) async-start(f32[16,1,128]{2,1,0:T(1,128)} %shard_map.142), calls=%async_computation.3 | async-start | bytes 16384 | tf_op jit(solution)/shard_map/all_to_all | solution.py:513
  140.2 11.2 %all-to-all-done.3.stat_ref = f32[16,1,128]{2,1,0:T(1,128)S(1)} async-done(((f32[16,1,128]{2,1,0:T(1,128)}), f32[16,1,128]{2,1,0:T(1,128)S(1)}, u32[]{:S(2)}, u32[]{:S(2)}) %all-to-all-start.3) | async-done | bytes 8224 | tf_op jit(solution)/shard_map/all_to_all | solution.py:513
  151.4 5.9 %shard_map.143 = (f32[1104,256]{1,0:T(8,128)S(1)}, f32[32,1,128]{2,1,0:T(1,128)S(1)}) custom-call(f32[1648,256]{1,0:T(8,128)} %get-tuple-element.44.own_hbm, f32[1648,256]{1,0:T(8,128)} %collective-permute-done.8.other_hbm, f32[16,1,128]{2,1,0:T(1,128)S(1)} %all-to-all-done.3.stat_ref, f32[2,160]{1,0:T(2,128)S(1)} %reshape.29.gain_ref, ...), custom_call_target="tpu_custom_call" | custom-call | tf_op jit(solution)/shard_map/pallas_call | solution.py:588
  157.3 11.4 %all_to_all.31.got_ref = f32[32,1,128]{2,1,0:T(1,128)S(1)} all-to-all(f32[32,1,128]{2,1,0:T(1,128)S(1)} %get-tuple-element.47), channel_id=1, replica_groups=mesh['zp'=8,'zl'=2,'y'=4,'core'=2,'x'=4] {'y','core','x'}, dimensions={0} | all-to-all | bytes 32768 | tf_op jit(solution)/shard_map/all_to_all | solution.py:510
  169.3 2.5 %collective-permute-start.9 = (f32[1104,256]{1,0:T(8,128)S(1)}, f32[1104,256]{1,0:T(8,128)S(1)}, u32[]{:S(2)}, u32[]{:S(2)}) collective-permute-start(f32[1104,256]{1,0:T(8,128)S(1)} %get-tuple-element.49.own_hbm), channel_id=1, source_target_pairs={{0,4},{4,0},{1,5},{5,1},{2,6},{6,2},{3,7},{7,3},{8,12},{12,8},{9,1... | collective-permute-start | bytes 3391496 | tf_op jit(solution)/shard_map/ppermute | solution.py:609
  172.0 3.5 %all-to-all-start.5 = ((f32[16,1,128]{2,1,0:T(1,128)}), f32[16,1,128]{2,1,0:T(1,128)S(1)}, u32[]{:S(2)}, u32[]{:S(2)}) async-start(f32[16,1,128]{2,1,0:T(1,128)} %shard_map.144), calls=%async_computation.5 | async-start | bytes 16384 | tf_op jit(solution)/shard_map/all_to_all | solution.py:513
  175.8 10.9 %all-to-all-done.5.stat_ref = f32[16,1,128]{2,1,0:T(1,128)S(1)} async-done(((f32[16,1,128]{2,1,0:T(1,128)}), f32[16,1,128]{2,1,0:T(1,128)S(1)}, u32[]{:S(2)}, u32[]{:S(2)}) %all-to-all-start.5) | async-done | bytes 8224 | tf_op jit(solution)/shard_map/all_to_all | solution.py:513
  186.7 2.0 %shard_map.145 = f32[4,1,256]{2,1,0:T(1,128)} custom-call(f32[1104,256]{1,0:T(8,128)S(1)} %get-tuple-element.49.own_hbm, f32[1104,256]{1,0:T(8,128)S(1)} %collective-permute-done.9.other_hbm, f32[16,1,128]{2,1,0:T(1,128)S(1)} %all-to-all-done.5.stat_ref, f32[2,160]{1,0:T(2,128)S(1)} %reshape.30.gain_ref, bf16[2,160,128]{2,1,0:T(8,128)(2,1)S(1)} %pad.14.wout_ref), custom_call_target="tpu_custom_call" | custom-call | tf_op jit(solution)/shard_map/pallas_call | solution.py:615
  (56 shorter events, 7.7 us)
Async XLA Ops:
  6.5 36.2 %copy-start = (bf16[320,1280]{1,0:T(8,128)(2,1)S(1)}, bf16[320,1280]{1,0:T(8,128)(2,1)}, u32[]{:S(2)}) copy-start(bf16[320,1280]{1,0:T(8,128)(2,1)} %param.22) | copy-start | bytes 2457604
  6.5 57.2 %all-gather.3.cloned.1.call-start = ((), (), s32[]{:S(2)}) async-start(), calls=%async_computation.6 | async-start | bytes 1433600 | tf_op jit(solution)/shard_map/all_gather | solution.py:536
  6.5 13.9 %collective-permute-start = (bf16[4,1,256]{2,0,1:T(4,128)(2,1)}, bf16[4,1,256]{2,0,1:T(4,128)(2,1)S(1)}, u32[]{:S(2)}, u32[]{:S(2)}) collective-permute-start(bf16[4,1,256]{2,0,1:T(4,128)(2,1)} %param.14), channel_id=1, source_target_pairs={{0,4},{4,8},{8,12},{12,16},{16,20},{20,24},{24,28},{28,32},{32,36}... | collective-permute-start | bytes 6152 | tf_op jit(solution)/shard_map/ppermute | solution.py:506
  11.3 9.2 %collective-permute-start.1 = (bf16[4,1,256]{2,0,1:T(4,128)(2,1)}, bf16[4,1,256]{2,0,1:T(4,128)(2,1)S(1)}, u32[]{:S(2)}, u32[]{:S(2)}) collective-permute-start(bf16[4,1,256]{2,0,1:T(4,128)(2,1)} %param.14), channel_id=1, source_target_pairs={{4,0},{8,4},{12,8},{16,12},{20,16},{24,20},{28,24},{32,28},{36,32}... | collective-permute-start | bytes 6152 | tf_op jit(solution)/shard_map/ppermute | solution.py:506
  17.5 1.0 copy-start.3
  18.5 0.9 copy-start.5
  20.5 0.9 copy-start.4
  21.4 0.8 copy-start.6
  22.2 0.7 copy-start.7
  23.0 40.7 %copy-start.1 = (bf16[384,384]{1,0:T(8,128)(2,1)}, bf16[384,384]{1,0:T(8,128)(2,1)S(1)}, u32[]{:S(2)}) copy-start(bf16[384,384]{1,0:T(8,128)(2,1)S(1)} %get-tuple-element.35.wpad_ref) | copy-start | bytes 884740
  23.0 5.3 %collective-permute-start.2 = (bf16[16,384]{1,0:T(8,128)(2,1)S(1)}, bf16[16,384]{1,0:T(8,128)(2,1)S(1)}, u32[]{:S(2)}, u32[]{:S(2)}) collective-permute-start(bf16[16,384]{1,0:T(8,128)(2,1)S(1)} %get-tuple-element.31), channel_id=1, source_target_pairs={{1,0},{2,1},{3,2},{5,4},{6,5},{7,6},{9,8},{10,9},{11,10},{13,12},{... | collective-permute-start | bytes 36872 | tf_op jit(solution)/shard_map/ppermute | solution.py:506
  24.3 4.8 %collective-permute-start.3 = (bf16[16,384]{1,0:T(8,128)(2,1)S(1)}, bf16[16,384]{1,0:T(8,128)(2,1)S(1)}, u32[]{:S(2)}, u32[]{:S(2)}) collective-permute-start(bf16[16,384]{1,0:T(8,128)(2,1)S(1)} %get-tuple-element.32), channel_id=1, source_target_pairs={{0,1},{1,2},{2,3},{4,5},{5,6},{6,7},{8,9},{9,10},{10,11},{12,13},{... | collective-permute-start | bytes 36872 | tf_op jit(solution)/shard_map/ppermute | solution.py:506
  31.3 30.4 %all-to-all-start = ((bf16[16,16,320]{2,1,0:T(8,128)(2,1)}), bf16[16,16,320]{2,1,0:T(8,128)(2,1)S(1)}, u32[]{:S(2)}, u32[]{:S(2)}) async-start(bf16[16,16,320]{2,1,0:T(8,128)(2,1)} %get-tuple-element.37), calls=%async_computation | async-start | bytes 393216 | tf_op jit(solution)/shard_map/all_to_all | solution.py:556
  43.1 11.7 %collective-permute-start.6 = (bf16[272,384]{1,0:T(8,128)(2,1)S(1)}, bf16[272,384]{1,0:T(8,128)(2,1)S(1)}, u32[]{:S(2)}, u32[]{:S(2)}) collective-permute-start(bf16[272,384]{1,0:T(8,128)(2,1)S(1)} %get-tuple-element.38), channel_id=1, source_target_pairs={{4,16},{12,24},{16,4},{20,32},{24,12},{28,40},{32,20},{36,48},{40,... | collective-permute-start | bytes 626696 | tf_op jit(solution)/shard_map/ppermute | solution.py:544
  49.8 9.4 %collective-permute-start.4 = (bf16[272,384]{1,0:T(8,128)(2,1)S(1)}, bf16[272,384]{1,0:T(8,128)(2,1)S(1)}, u32[]{:S(2)}, u32[]{:S(2)}) collective-permute-start(bf16[272,384]{1,0:T(8,128)(2,1)S(1)} %get-tuple-element.38), channel_id=1, source_target_pairs={{0,8},{4,12},{8,16},{12,20},{16,24},{20,28},{24,32},{28,36},{32,40... | collective-permute-start | bytes 626696 | tf_op jit(solution)/shard_map/ppermute | solution.py:506
  52.1 9.5 %collective-permute-start.5 = (bf16[272,384]{1,0:T(8,128)(2,1)S(1)}, bf16[272,384]{1,0:T(8,128)(2,1)S(1)}, u32[]{:S(2)}, u32[]{:S(2)}) collective-permute-start(bf16[272,384]{1,0:T(8,128)(2,1)S(1)} %get-tuple-element.38), channel_id=1, source_target_pairs={{8,0},{12,4},{16,8},{20,12},{24,16},{28,20},{32,24},{36,28},{40,32... | collective-permute-start | bytes 626696 | tf_op jit(solution)/shard_map/ppermute | solution.py:506
  61.7 12.8 %copy-start.8 = (bf16[4,272,384]{2,1,0:T(8,128)(2,1)}, bf16[4,272,384]{2,1,0:T(8,128)(2,1)S(1)}, u32[]{:S(2)}) copy-start(bf16[4,272,384]{2,1,0:T(8,128)(2,1)S(1)} %pad_maximum_fusion.own_ref) | copy-start | bytes 2506756
  63.8 13.0 %copy-start.11 = (f32[640]{0:T(1024)S(1)}, f32[640]{0:T(1024)}, u32[]{:S(2)}) copy-start(f32[640]{0:T(1024)} %param.25) | copy-start | bytes 7684
  63.8 39.7 %all-to-all-start.1 = ((bf16[32,56,640]{2,1,0:T(8,128)(2,1)}), bf16[32,56,640]{2,1,0:T(8,128)(2,1)}, u32[]{:S(2)}, u32[]{:S(2)}) async-start(bf16[32,56,640]{2,1,0:T(8,128)(2,1)} %shard_map.139), calls=%async_computation.1 | async-start | bytes 4587520 | tf_op jit(solution)/shard_map/all_to_all | solution.py:565
  74.5 4.2 %collective-permute-start.7 = (bf16[4,272,384]{2,1,0:T(8,128)(2,1)S(1)}, bf16[4,272,384]{2,1,0:T(8,128)(2,1)S(1)}, u32[]{:S(2)}, u32[]{:S(2)}) collective-permute-start(bf16[4,272,384]{2,1,0:T(8,128)(2,1)S(1)} %pad_maximum_fusion.own_ref), channel_id=1, source_target_pairs={{0,4},{4,0},{1,5},{5,1},{2,6},{6,2},{3,7},{7,3},{8,12},{12,8},{9,1... | collective-permute-start | bytes 2506760 | tf_op jit(solution)/shard_map/ppermute | solution.py:569
  76.8 26.7 %copy-start.2 = (bf16[1280,320]{0,1:T(8,128)(2,1)S(1)}, bf16[1280,320]{0,1:T(8,128)(2,1)}, u32[]{:S(2)}) copy-start(bf16[1280,320]{0,1:T(8,128)(2,1)} %param.24) | copy-start | bytes 2457604
  78.8 0.9 copy-start.9
  103.5 36.6 %copy-start.12 = (f32[320]{0:T(512)S(1)}, f32[320]{0:T(512)}, u32[]{:S(2)}) copy-start(f32[320]{0:T(512)} %param.26) | copy-start | bytes 3844
  125.9 25.5 %collective-permute-start.8 = (f32[1648,256]{1,0:T(8,128)}, f32[1648,256]{1,0:T(8,128)}, u32[]{:S(2)}, u32[]{:S(2)}) collective-permute-start(f32[1648,256]{1,0:T(8,128)} %get-tuple-element.44.own_hbm), channel_id=1, source_target_pairs={{0,4},{4,0},{1,5},{5,1},{2,6},{6,2},{3,7},{7,3},{8,12},{12,8},{9,1... | collective-permute-start | bytes 5062664 | tf_op jit(solution)/shard_map/ppermute | solution.py:587
  128.5 22.9 %all-to-all-start.3 = ((f32[16,1,128]{2,1,0:T(1,128)}), f32[16,1,128]{2,1,0:T(1,128)S(1)}, u32[]{:S(2)}, u32[]{:S(2)}) async-start(f32[16,1,128]{2,1,0:T(1,128)} %shard_map.142), calls=%async_computation.3 | async-start | bytes 16384 | tf_op jit(solution)/shard_map/all_to_all | solution.py:513
  140.2 31.7 %copy-start.10 = (bf16[2880,4]{0,1:T(4,128)(2,1)S(1)}, bf16[2880,4]{0,1:T(4,128)(2,1)}, u32[]{:S(2)}) copy-start(bf16[2880,4]{0,1:T(4,128)(2,1)} %param.21) | copy-start | bytes 69124
  140.2 35.5 %copy-start.13 = (f32[320]{0:T(512)S(1)}, f32[320]{0:T(512)}, u32[]{:S(2)}) copy-start(f32[320]{0:T(512)} %param.27) | copy-start | bytes 3844
  169.3 17.3 %collective-permute-start.9 = (f32[1104,256]{1,0:T(8,128)S(1)}, f32[1104,256]{1,0:T(8,128)S(1)}, u32[]{:S(2)}, u32[]{:S(2)}) collective-permute-start(f32[1104,256]{1,0:T(8,128)S(1)} %get-tuple-element.49.own_hbm), channel_id=1, source_target_pairs={{0,4},{4,0},{1,5},{5,1},{2,6},{6,2},{3,7},{7,3},{8,12},{12,8},{9,1... | collective-permute-start | bytes 3391496 | tf_op jit(solution)/shard_map/ppermute | solution.py:609
  172.0 14.7 %all-to-all-start.5 = ((f32[16,1,128]{2,1,0:T(1,128)}), f32[16,1,128]{2,1,0:T(1,128)S(1)}, u32[]{:S(2)}, u32[]{:S(2)}) async-start(f32[16,1,128]{2,1,0:T(1,128)} %shard_map.144), calls=%async_computation.5 | async-start | bytes 16384 | tf_op jit(solution)/shard_map/all_to_all | solution.py:513
Sparse Core Ops, SparseCore 0:
  29.3 34.4 all-gather.2

commit v5 on v4

--- a/solution.py
+++ b/solution.py
@@ -39,7 +39,7 @@
         kernel,
         out_shape=out_shape,
         in_specs=in_specs,
-        out_specs=jax.tree.map(lambda _: out_spec, out_shape),
+        out_specs=out_spec if isinstance(out_spec, tuple) else jax.tree.map(lambda _: out_spec, out_shape),
         scratch_shapes=list(scratch),
         compiler_params=pltpu.CompilerParams(vmem_limit_bytes=limit * 1024 * 1024),
     )
@@ -223,65 +223,105 @@
     one(IN_ROWS, GAP)
 
 
-def first_kernel(
-    joined_hbm, found_hbm, proj_ref, gain_ref,
-    hidden_ref, sum_ref,
-    joined_ref, found_ref, rows, wm_ref, act, merged, sems,
-):
-    copies = [pltpu.make_async_copy(found_hbm, found_ref, sems.at[0])]
-    for i, part in enumerate((slice(0, 4 * SEG), slice(4 * SEG, A_LEN))):
-        copies.append(pltpu.make_async_copy(joined_hbm.at[part], joined_ref.at[part], sems.at[i + 1]))
-    for copy in copies:
-        copy.start()
-    copies[0].wait()
-    chip_row, first_col, _ = place()
-    first_row = chip_row - 3
-    sums, shift = front_weight(found_ref, proj_ref, wm_ref, rows)
+def first_affine(sums, gain_ref):
     totals = sums / (20.0 * 131072.0)
     mean = totals[:, 0:32]
     var = totals[:, 32:64] - mean * mean
     pair = jnp.concatenate([lax.rsqrt(var + EPS), mean, jnp.zeros((6, 32), F32)], axis=0)
     spread = exact_dot(pair, same_group(32, 2 * C, 1, 20))
     scale = spread[0:1] * gain_ref[...] * 0.5
-    offset = -spread[1:2] * scale
+    return scale, -spread[1:2] * scale
+
+
+def first_build(joined_ref, act, at, size, mask, scale, offset):
+    where = slice(at, at + size)
+    for lane in range(0, 2 * C, 128):
+        part = slice(lane, lane + 128)
+        values = joined_ref[where, part].astype(F32) * scale[:, part] + offset[:, part]
+        act[where, part] = (silu_half(values) * mask[0:size]).astype(BF16)
+
+
+def merged_conv(act, wm_ref, merged, start, size):
+    taps = [act[start + a * SEG : start + a * SEG + size, :] for a in range(3)]
+    merged[start + GAP : start + GAP + size, :] = tap_dot(jnp.concatenate(taps, axis=1), wm_ref[...])
+
+
+def clear_ends(merged):
+    size = merged.shape[0]
+    merged[0:GAP, :] = jnp.zeros((GAP, MERGED), F32)
+    merged[size - GAP : size, :] = jnp.zeros((GAP, MERGED), F32)
+
+
+def first_own_kernel(
+    joined_hbm, found_hbm, proj_ref, gain_ref,
+    wm_hbm, known_ref, sum_ref,
+    joined_ref, found_ref, rows, wm_ref, act, merged, sems,
+):
+    copies = [
+        pltpu.make_async_copy(found_hbm, found_ref, sems.at[0]),
+        pltpu.make_async_copy(joined_hbm.at[2 * SEG : 2 * SEG + B_LEN], joined_ref, sems.at[1]),
+        pltpu.make_async_copy(wm_ref, wm_hbm, sems.at[2]),
+    ]
+    copies[0].start()
+    copies[1].start()
+    copies[0].wait()
+    chip_row, first_col, _ = place()
+    totals, shift = front_weight(found_ref, proj_ref, wm_ref, rows)
+    copies[2].start()
+    known_ref[...] = jnp.concatenate([totals, jnp.zeros((1, 64), F32), shift, jnp.zeros((1, 96), F32)], axis=1)
+    scale, offset = first_affine(totals, gain_ref)
+    clear_ends(merged)
+    copies[1].wait()
+    for r in range(5):
+        mask = keep_mask(r + 2, chip_row - 3, first_col)
+        first_build(joined_ref, act, r * SEG, SEG if r < 4 else GAP, mask, scale, offset)
+    merged_conv(act, wm_ref, merged, 0, 2 * SEG + GAP)
+    sums = jnp.zeros((1, HALF), F32)
+    squares = jnp.zeros((1, HALF), F32)
+    for r in range(2):
+        values = shift_add(merged, 2 * GAP + r * SEG, WIDE) + shift
+        sums = sums + jnp.sum(values, axis=0, keepdims=True)
+        squares = squares + jnp.sum(values * values, axis=0, keepdims=True)
+    send_sums(sums, squares, sum_ref)
+    copies[2].wait()
+
+
+def first_kernel(
+    joined_hbm, wm_hbm, known_ref, gain_ref,
+    hidden_ref,
+    joined_ref, wm_ref, act, merged, sems,
+):
+    copies = []
+    for i, part in enumerate((slice(0, 4 * SEG), slice(4 * SEG, A_LEN))):
+        copies.append(pltpu.make_async_copy(joined_hbm.at[part], joined_ref.at[part], sems.at[i]))
+    copies.append(pltpu.make_async_copy(wm_hbm, wm_ref, sems.at[2]))
+    for copy in copies:
+        copy.start()
+    chip_row, first_col, _ = place()
+    scale, offset = first_affine(known_ref[:, 0:64], gain_ref)
+    shift = known_ref[:, 128 : 128 + HALF]
 
     def build(r):
-        where = slice(r * SEG, r * SEG + (SEG if r < IN_ROWS else GAP))
-        mask = keep_mask(r, first_row, first_col)[0 : where.stop - where.start]
-        for lane in range(0, 2 * C, 128):
-            at = slice(lane, lane + 128)
-            values = joined_ref[where, at].astype(F32) * scale[:, at] + offset[:, at]
-            act[where, at] = (silu_half(values) * mask).astype(BF16)
-
-    def conv(start, size):
-        taps = [act[start + a * SEG : start + a * SEG + size, :] for a in range(3)]
-        merged[start + GAP : start + GAP + size, :] = tap_dot(jnp.concatenate(taps, axis=1), wm_ref[...])
-
-    merged[0:GAP, :] = jnp.zeros((GAP, MERGED), F32)
-    merged[GAP + H_LEN : GAP + H_LEN + GAP, :] = jnp.zeros((GAP, MERGED), F32)
-    copies[1].wait()
+        mask = keep_mask(r, chip_row - 3, first_col)
+        first_build(joined_ref, act, r * SEG, SEG if r < IN_ROWS else GAP, mask, scale, offset)
+
+    clear_ends(merged)
+    copies[0].wait()
     for r in range(4):
         build(r)
     copies[2].wait()
-    conv(0, 2 * SEG)
+    merged_conv(act, wm_ref, merged, 0, 2 * SEG)
+    copies[1].wait()
     build(4)
     build(5)
-    conv(2 * SEG, 2 * SEG)
+    merged_conv(act, wm_ref, merged, 2 * SEG, 2 * SEG)
     for r in range(6, 9):
         build(r)
-    conv(4 * SEG, 2 * SEG + GAP)
-
-    sums = jnp.zeros((1, HALF), F32)
-    squares = jnp.zeros((1, HALF), F32)
+    merged_conv(act, wm_ref, merged, 4 * SEG, 2 * SEG + GAP)
     for r in range(MID_ROWS + 1):
         size = SEG if r < MID_ROWS else GAP
-        values = shift_add(merged, GAP + r * SEG, size) + shift
-        hidden_ref[r * SEG : r * SEG + size, 0:HALF] = values
-        if r in (2, 3):
-            sums = sums + jnp.sum(values[GAP:], axis=0, keepdims=True)
-            squares = squares + jnp.sum(values[GAP:] * values[GAP:], axis=0, keepdims=True)
+        hidden_ref[r * SEG : r * SEG + size, 0:HALF] = shift_add(merged, GAP + r * SEG, size) + shift
     hidden_ref[:, HALF:SWAP] = jnp.zeros((H_LEN, SWAP - HALF), F32)
-    send_sums(sums, squares, sum_ref)
 
 
 def send_sums(sums, squares, sent_ref):
@@ -317,70 +357,100 @@
     return found
 
 
-def second_kernel(
+def second_build(own_ref, other_ref, act, at, size, mask, affines):
+    where = slice(at, at + size)
+    first = lax.axis_index("core") == 0
+    own, other = own_ref[where, 0:HALF], other_ref[where, 0:HALF]
+    parts = []
+    for which, (scale, offset) in enumerate(affines):
+        values = jnp.where(first, own, other) if which == 0 else jnp.where(first, other, own)
+        parts.append(silu_half(values * scale + offset) * mask[0:size])
+    parts.append(jnp.zeros((size, LANES - C), F32))
+    act[where, :] = jnp.concatenate(parts, axis=1).astype(BF16)
+
+
+def second_own_kernel(
     own_hbm, other_hbm, stat_ref, gain_ref, found_hbm, joined_hbm,
-    block_ref, sum_ref,
-    own_ref, other_ref, found_ref, joined_ref, wm_ref, skip, act, merged, sems,
+    wm_hbm, skip_hbm, sum_ref,
+    own_ref, other_ref, found_ref, joined_ref, wm_ref, skip_ref, act, merged, sems,
 ):
-    early, late = slice(0, 4 * SEG), slice(4 * SEG, H_LEN)
+    part = slice(SEG, SEG + B_LEN)
     copies = [
-        pltpu.make_async_copy(own_hbm.at[early], own_ref.at[early], sems.at[0]),
-        pltpu.make_async_copy(other_hbm.at[early], other_ref.at[early], sems.at[1]),
-        pltpu.make_async_copy(found_hbm, found_ref, sems.at[2]),
-        pltpu.make_async_copy(own_hbm.at[late], own_ref.at[late], sems.at[3]),
-        pltpu.make_async_copy(other_hbm.at[late], other_ref.at[late], sems.at[4]),
-        pltpu.make_async_copy(joined_hbm.at[2 * SEG : 2 * SEG + B_LEN], joined_ref, sems.at[5]),
+        pltpu.make_async_copy(found_hbm, found_ref, sems.at[0]),
+        pltpu.make_async_copy(own_hbm.at[part], own_ref, sems.at[1]),
+        pltpu.make_async_copy(other_hbm.at[part], other_ref, sems.at[2]),
+        pltpu.make_async_copy(joined_hbm.at[3 * SEG : 5 * SEG], joined_ref, sems.at[3]),
     ]
     for copy in copies:
         copy.start()
-    chip_row, first_col, core = place()
-    first_row = chip_row - 2
+    back = [
+        pltpu.make_async_copy(wm_ref, wm_hbm, sems.at[4]),
+        pltpu.make_async_copy(skip_ref, skip_hbm, sems.at[5]),
+    ]
+    chip_row, first_col, _ = place()
     affines = affine(stat_ref, gain_ref)
-    first = core == 0
-
-    def build(r):
-        where = slice(r * SEG, r * SEG + (SEG if r < MID_ROWS else GAP))
-        mask = keep_mask(r, first_row, first_col)[0 : where.stop - where.start]
-        own, other = own_ref[where, 0:HALF], other_ref[where, 0:HALF]
-        parts = []
-        for which, (scale, offset) in enumerate(affines):
-            values = jnp.where(first, own, other) if which == 0 else jnp.where(first, other, own)
-            parts.append(silu_half(values * scale + offset) * mask)
-        parts.append(jnp.zeros((where.stop - where.start, LANES - C), F32))
-        act[where, :] = jnp.concatenate(parts, axis=1).astype(BF16)
-
-    def conv(start, size):
-        taps = [act[start + a * SEG : start + a * SEG + size, :] for a in range(3)]
-        merged[start + GAP : start + GAP + size, :] = tap_dot(jnp.concatenate(taps, axis=1), wm_ref[...])
-
-    merged[0:GAP, :] = jnp.zeros((GAP, MERGED), F32)
-    merged[GAP + B_LEN : GAP + B_LEN + GAP, :] = jnp.zeros((GAP, MERGED), F32)
+    clear_ends(merged)
+    copies[0].wait()
+    middle_weight(found_ref, wm_ref, skip_ref)
+    for copy in back:
+        copy.start()
+    copies[1].wait()
+    copies[2].wait()
+    for r in range(5):
+        mask = keep_mask(r + 1, chip_row - 2, first_col)
+        second_build(own_ref, other_ref, act, r * SEG, SEG if r < 4 else GAP, mask, affines)
+    merged_conv(act, wm_ref, merged, 0, 2 * SEG + GAP)
+    copies[3].wait()
+    sums = jnp.zeros((1, HALF), F32)
+    squares = jnp.zeros((1, HALF), F32)
+    for r in range(2):
+        at = r * SEG + GAP
+        values = shift_add(merged, GAP + at, WIDE) + tap_dot(joined_ref[at : at + WIDE, :], skip_ref[...])
+        sums = sums + jnp.sum(values, axis=0, keepdims=True)
+        squares = squares + jnp.sum(values * values, axis=0, keepdims=True)
+    send_sums(sums, squares, sum_ref)
+    for copy in back:
+        copy.wait()
+
+
+def second_kernel(
+    own_hbm, other_hbm, stat_ref, gain_ref, wm_hbm, skip_ref, joined_hbm,
+    block_ref,
+    own_ref, other_ref, joined_ref, wm_ref, act, merged, sems,
+):
+    copies = [
+        pltpu.make_async_copy(own_hbm, own_ref, sems.at[0]),
+        pltpu.make_async_copy(other_hbm, other_ref, sems.at[1]),
+        pltpu.make_async_copy(wm_hbm, wm_ref, sems.at[2]),
+        pltpu.make_async_copy(joined_hbm.at[2 * SEG : 2 * SEG + B_LEN], joined_ref, sems.at[3]),
+    ]
+    for copy in copies:
+        copy.start()
+    chip_row, first_col, _ = place()
+    affines = affine(stat_ref, gain_ref)
+    clear_ends(merged)
     copies[0].wait()
     copies[1].wait()
+
+    def build(r):
+        mask = keep_mask(r, chip_row - 2, first_col)
+        second_build(own_ref, other_ref, act, r * SEG, SEG if r < MID_ROWS else GAP, mask, affines)
+
     for r in range(4):
         build(r)
     copies[2].wait()
-    middle_weight(found_ref, wm_ref, skip)
-    copies[3].wait()
-    copies[4].wait()
-    conv(0, 2 * SEG)
+    merged_conv(act, wm_ref, merged, 0, 2 * SEG)
     for r in range(4, 7):
         build(r)
-    conv(2 * SEG, 2 * SEG + GAP)
-    copies[5].wait()
-
-    sums = jnp.zeros((1, HALF), F32)
-    squares = jnp.zeros((1, HALF), F32)
+    merged_conv(act, wm_ref, merged, 2 * SEG, 2 * SEG + GAP)
+    copies[3].wait()
     for r in range(OUT_ROWS + 1):
         size = SEG if r < OUT_ROWS else GAP
         where = slice(r * SEG, r * SEG + size)
-        values = shift_add(merged, GAP + r * SEG, size) + tap_dot(joined_ref[where, :], skip[...])
-        block_ref[where, 0:HALF] = values
-        if r in (1, 2):
-            sums = sums + jnp.sum(values[GAP:], axis=0, keepdims=True)
-            squares = squares + jnp.sum(values[GAP:] * values[GAP:], axis=0, keepdims=True)
+        block_ref[where, 0:HALF] = shift_add(merged, GAP + r * SEG, size) + tap_dot(
+            joined_ref[where, :], skip_ref[...]
+        )
     block_ref[:, HALF:SWAP] = jnp.zeros((B_LEN, SWAP - HALF), F32)
-    send_sums(sums, squares, sum_ref)
 
 
 def third_kernel(own_hbm, other_hbm, stat_ref, gain_ref, wout_ref, noise_ref, own_ref, other_ref, sems):
@@ -508,8 +578,8 @@
 
 def summed(sums, kept):
     near = lax.all_to_all(sums, PLANE, 0, 0, tiled=True)
+    near, kept = lax.optimization_barrier((near, kept))
     near = call(plane_sums_kernel, sds((lax.axis_size(DEPTH), 1, 128), F32), [VMEM])(near)
-    near, kept = lax.optimization_barrier((near, kept))
     return lax.all_to_all(near, DEPTH, 0, 0, tiled=True), kept
 
 
@@ -520,11 +590,8 @@
     core, x, y = lax.axis_index("core"), lax.axis_index("x"), lax.axis_index("y")
     depths = lax.axis_size(DEPTH)
 
-    packed = call(share_kernel, sds((224, 4 * HALF), BF16), [VMEM] * 2)(middle_weight.T, skip_weight)
-
     above, below = shifted(latent, ROWS, 1), shifted(latent, ROWS, -1)
     quarter = lax.dynamic_slice_in_dim(jnp.pad(front_weight, ((0, 3), (0, 0))), 12 * x, 12, 0)
-    above, packed, quarter = lax.optimization_barrier((above, packed, quarter))
     cells, first, last, wpad = call(
         pack_kernel,
         (sds((WIDE, LANES), BF16), sds((GAP, LANES), BF16), sds((GAP, LANES), BF16), sds((LANES, LANES), BF16)),
@@ -532,11 +599,12 @@
         [pltpu.VMEM((LANES, WIDE), F32), pltpu.VMEM((LANES, LANES), F32)],
     )(deep.reshape(C, WIDE), above.reshape(4, WIDE), latent.reshape(4, WIDE), below.reshape(4, WIDE), in_weight)
     from_right, from_left = shifted(first, "x", -1), shifted(last, "x", 1)
-    packed, from_right, from_left = lax.optimization_barrier((packed, from_right, from_left))
-    middle_found = lax.all_gather(packed, "x", axis=0)
     row, sent = call(stats_kernel, (sds((SEG, LANES), BF16), sds((depths, 16, C), BF16)), [VMEM] * 5)(
         cells, from_left, from_right, wpad, quarter
     )
+
+    row, skip_here = lax.optimization_barrier((row, skip_weight))
+    packed = call(share_kernel, sds((224, 4 * HALF), BF16), [VMEM] * 2)(middle_weight.T, skip_here)
 
     count = lax.axis_size(ROWS)
     crossed = [(i, i + 3) if i % 2 else (i, i - 3) for i in range(count)]
@@ -561,52 +629,86 @@
     ]
     sent = call(plane_kernel, sds((32, 56, 4 * HALF), BF16), [VMEM] * 2, scratch, 52, ANY)(got, part[None])
     around = jnp.stack([before, row, after, across])
-    sent, around, middle_found = lax.optimization_barrier((sent, around, middle_found))
+    sent, around = lax.optimization_barrier((sent, around))
     found = lax.all_to_all(sent, PLANE, 0, 0, tiled=True)
     swap = [(0, 1), (1, 0)]
     joined = call(
         join_kernel, sds((A_LEN, 2 * C), BF16), [VMEM] * 3, [pltpu.VMEM((A_LEN + 2 * GAP, LANES), BF16)], 60
     )(around, lax.ppermute(around, "core", swap), wpad)
-    hidden_own, sums = call(
+    own_scratch = [
+        pltpu.VMEM((B_LEN, 2 * C), BF16),
+        pltpu.VMEM((32, 56, 4 * HALF), BF16),
+        pltpu.VMEM((1440, 4 * HALF), F32),
+        pltpu.VMEM((3 * 2 * C, MERGED), BF16),
+        pltpu.VMEM((B_LEN, 2 * C), BF16),
+        pltpu.VMEM((2 * SEG + 3 * GAP, MERGED), F32),
+        pltpu.SemaphoreType.DMA((3,)),
+    ]
+    front, known, sums = call(
+        first_own_kernel,
+        (sds((3 * 2 * C, MERGED), BF16), sds((1, 384), F32), sds((32, 1, 128), F32)),
+        [ANY, ANY, VMEM, VMEM],
+        own_scratch,
+        52,
+        (ANY, VMEM, VMEM),
+    )(joined, found, time_proj.T, input_gain[None])
+    packed, sums = lax.optimization_barrier((packed, sums))
+    middle_found = lax.all_gather(packed, "x", axis=0)
+    hidden_own = call(
         first_kernel,
-        (sds((H_LEN, SWAP), F32), sds((32, 1, 128), F32)),
+        sds((H_LEN, SWAP), F32),
         [ANY, ANY, VMEM, VMEM],
         [
             pltpu.VMEM((A_LEN, 2 * C), BF16),
-            pltpu.VMEM((32, 56, 4 * HALF), BF16),
-            pltpu.VMEM((1440, 4 * HALF), F32),
             pltpu.VMEM((3 * 2 * C, MERGED), BF16),
             pltpu.VMEM((A_LEN, 2 * C), BF16),
             pltpu.VMEM((H_LEN + 2 * GAP, MERGED), F32),
             pltpu.SemaphoreType.DMA((3,)),
         ],
         52,
-    )(joined, found, time_proj.T, input_gain[None])
-
+    )(joined, front, known, input_gain[None])
     totals, hidden_own = summed(sums, hidden_own)
     hidden_other = lax.ppermute(hidden_own, "core", swap)
-    block_own, sums = call(
+
+    gain_two = middle_gain.reshape(2, HALF)
+    middle, shortcut, sums = call(
+        second_own_kernel,
+        (sds((3 * LANES, MERGED), BF16), sds((2 * C, HALF), BF16), sds((32, 1, 128), F32)),
+        [ANY, ANY, VMEM, VMEM, ANY, ANY],
+        [
+            pltpu.VMEM((B_LEN, SWAP), F32),
+            pltpu.VMEM((B_LEN, SWAP), F32),
+            pltpu.VMEM((4, 224, 4 * HALF), BF16),
+            pltpu.VMEM((2 * SEG, 2 * C), BF16),
+            pltpu.VMEM((3 * LANES, MERGED), BF16),
+            pltpu.VMEM((2 * C, HALF), BF16),
+            pltpu.VMEM((B_LEN, LANES), BF16),
+            pltpu.VMEM((2 * SEG + 3 * GAP, MERGED), F32),
+            pltpu.SemaphoreType.DMA((6,)),
+        ],
+        52,
+        (ANY, ANY, VMEM),
+    )(hidden_own, hidden_other, totals, gain_two, middle_found, joined)
+    block_own = call(
         second_kernel,
-        (sds((B_LEN, SWAP), F32), sds((32, 1, 128), F32)),
-        [ANY, ANY, VMEM, VMEM, ANY, ANY],
+        sds((B_LEN, SWAP), F32),
+        [ANY, ANY, VMEM, VMEM, ANY, VMEM, ANY],
         [
             pltpu.VMEM((H_LEN, SWAP), F32),
             pltpu.VMEM((H_LEN, SWAP), F32),
-            pltpu.VMEM((4, 224, 4 * HALF), BF16),
             pltpu.VMEM((B_LEN, 2 * C), BF16),
             pltpu.VMEM((3 * LANES, MERGED), BF16),
-            pltpu.VMEM((2 * C, HALF), BF16),
             pltpu.VMEM((H_LEN, LANES), BF16),
             pltpu.VMEM((B_LEN + 2 * GAP, MERGED), F32),
-            pltpu.SemaphoreType.DMA((6,)),
+            pltpu.SemaphoreType.DMA((4,)),
         ],
         52,
-    )(hidden_own, hidden_other, totals, middle_gain.reshape(2, HALF), middle_found, joined)
+    )(hidden_own, hidden_other, totals, gain_two, middle, shortcut, joined)
+    totals, block_own = summed(sums, block_own)
+    block_other = lax.ppermute(block_own, "core", swap)
 
     wout = out_weight.reshape(9, 2, HALF, 4).transpose(1, 2, 0, 3)
     wout = jnp.pad(jnp.pad(wout, ((0, 0), (0, 0), (0, 0), (0, 4))).reshape(2, HALF, 72), ((0, 0), (0, 0), (0, 56)))
-    totals, block_own = summed(sums, block_own)
-    block_other = lax.ppermute(block_own, "core", swap)
     scratch = [
         pltpu.VMEM((3 * SEG + GAP, SWAP), F32),
         pltpu.VMEM((3 * SEG + GAP, SWAP), F32),

time: 197 us -> 195 us (0.990)
  blocking collectives: 23.6 us -> 0 us
  starting transfers between devices: 70.2 us -> 82.4 us
  Pallas kernels: 29.1 us -> 36.4 us
  waiting for transfers between devices: 50 us -> 54 us
    all_to_all x2 -> x0, blocking collectives: 23.6 us -> none  [summed(): near = lax.all_to_all(sums, PLANE, 0, 0, tiled=True)]
    all_to_all x0 -> x2, starting transfers between devices: none -> 13.5 us  [summed(): near = lax.all_to_all(sums, PLANE, 0, 0, tiled=True)]
    pallas_call x2 -> x4, Pallas kernels: 15.4 us -> 22.6 us  [the longest x1 6.63 us: shards(): call(first_kernel, sds((H_LEN, SWAP), F32), [ANY, ANY, VMEM, VMEM], [pltp...]
    all_to_all x1, starting transfers between devices: 11.4 us -> 14.9 us  [shards(): got = lax.all_to_all(sent, DEPTH, 0, 0, tiled=True)]
    ppermute x6, starting transfers between devices: 19.1 us -> 16.4 us  [shifted(): lax.ppermute(x, axis, [(i, i + step) for i in range(count) if 0 <= i + st...]
    ppermute x6, waiting for transfers between devices: 7.63 us -> 10.1 us  [shifted(): lax.ppermute(x, axis, [(i, i + step) for i in range(count) if 0 <= i + st...]
    all_to_all x0 -> x2, waiting for transfers between devices: none -> 1.99 us  [summed(): near = lax.all_to_all(sums, PLANE, 0, 0, tiled=True)]
    unnamed x29 -> x31, local copies, waits for them, and re-layouts: 5.24 us -> 3.67 us
  transfers between devices with their start and end apart: 15 -> 17, of which waited for: 9 -> 9; matrix products, arithmetic and copies ran while one was open for 2% -> 2% of each run, Pallas kernels for 5% -> 10%
where the time goes in v5:
time: 195 us; the launch traced here: 194 us
  starting transfers between devices  82.4 us (42%)
  waiting for transfers between devices  54 us (28%)
  Pallas kernels  36.4 us (19%)
  between operations  14.5 us (7%)
  local copies, waits for them, and re-layouts  4.86 us (2%)
    all_to_all x2, waiting for transfers between devices, summed(): return (lax.all_to_all(near, DEPTH, 0, 0, tiled=True), kept)  22.1 us
    all_to_all x1, waiting for transfers between devices, shards(): found = lax.all_to_all(sent, PLANE, 0, 0, tiled=True)  18.7 us
    ppermute x6, starting transfers between devices, shifted(): lax.ppermute(x, axis, [(i, i + step) for i in range(count) if 0 <= i + st...  16.4 us
    all_to_all x2, starting transfers between devices, summed(): return (lax.all_to_all(near, DEPTH, 0, 0, tiled=True), kept)  14.9 us
    all_to_all x1, starting transfers between devices, shards(): got = lax.all_to_all(sent, DEPTH, 0, 0, tiled=True)  14.9 us
    all_to_all x2, starting transfers between devices, summed(): near = lax.all_to_all(sums, PLANE, 0, 0, tiled=True)  13.5 us
    ppermute x6, waiting for transfers between devices, shifted(): lax.ppermute(x, axis, [(i, i + step) for i in range(count) if 0 <= i + st...  10.1 us
    all_to_all x1, starting transfers between devices, shards(): found = lax.all_to_all(sent, PLANE, 0, 0, tiled=True)  9.87 us
  transfers between devices with their start and end apart: 17, of which 9 were waited for; matrix products, arithmetic and copies ran while one was open for 2% of the time, Pallas kernels for 10%

profile of v5, /device:TPU:1, one launch (start us, length us, event | category | flops | bytes accessed | tf_op | source)
XLA Modules:
  0.0 193.9 jit_solution(15197920027848690441)
XLA Ops:
  6.5 4.7 %collective-permute-start = (bf16[4,1,256]{2,0,1:T(4,128)(2,1)}, bf16[4,1,256]{2,0,1:T(4,128)(2,1)S(1)}, u32[]{:S(2)}, u32[]{:S(2)}) collective-permute-start(bf16[4,1,256]{2,0,1:T(4,128)(2,1)} %param.14), channel_id=1, source_target_pairs={{0,4},{4,8},{8,12},{12,16},{16,20},{20,24},{24,28},{28,32},{32,36}... | collective-permute-start | bytes 6152 | tf_op jit(solution)/shard_map/ppermute | solution.py:576
  11.3 5.5 %collective-permute-start.1 = (bf16[4,1,256]{2,0,1:T(4,128)(2,1)}, bf16[4,1,256]{2,0,1:T(4,128)(2,1)S(1)}, u32[]{:S(2)}, u32[]{:S(2)}) collective-permute-start(bf16[4,1,256]{2,0,1:T(4,128)(2,1)} %param.14), channel_id=1, source_target_pairs={{4,0},{8,4},{12,8},{16,12},{20,16},{24,20},{28,24},{32,28},{36,32}... | collective-permute-start | bytes 6152 | tf_op jit(solution)/shard_map/ppermute | solution.py:576
  20.8 1.3 collective-permute-start.2
  22.1 1.3 collective-permute-start.3
  23.4 3.1 %collective-permute-done.3.right_ref = bf16[16,384]{1,0:T(8,128)(2,1)S(1)} collective-permute-done((bf16[16,384]{1,0:T(8,128)(2,1)S(1)}, bf16[16,384]{1,0:T(8,128)(2,1)S(1)}, u32[]{:S(2)}, u32[]{:S(2)}) %collective-permute-start.3) | collective-permute-done | bytes 12320 | tf_op jit(solution)/shard_map/ppermute | solution.py:576
  26.5 1.4 shard_map.137
  27.9 14.9 %all-to-all-start = ((bf16[16,16,320]{2,1,0:T(8,128)(2,1)}), bf16[16,16,320]{2,1,0:T(8,128)(2,1)S(1)}, u32[]{:S(2)}, u32[]{:S(2)}) async-start(bf16[16,16,320]{2,1,0:T(8,128)(2,1)} %get-tuple-element.33), calls=%async_computation | async-start | bytes 393216 | tf_op jit(solution)/shard_map/all_to_all | solution.py:624
  43.2 5.3 %collective-permute-start.6 = (bf16[272,384]{1,0:T(8,128)(2,1)S(1)}, bf16[272,384]{1,0:T(8,128)(2,1)S(1)}, u32[]{:S(2)}, u32[]{:S(2)}) collective-permute-start(bf16[272,384]{1,0:T(8,128)(2,1)S(1)} %get-tuple-element.34), channel_id=1, source_target_pairs={{4,16},{12,24},{16,4},{20,32},{24,12},{28,40},{32,20},{36,48},{40,... | collective-permute-start | bytes 626696 | tf_op jit(solution)/shard_map/ppermute | solution.py:612
  48.5 2.3 %collective-permute-start.4 = (bf16[272,384]{1,0:T(8,128)(2,1)S(1)}, bf16[272,384]{1,0:T(8,128)(2,1)S(1)}, u32[]{:S(2)}, u32[]{:S(2)}) collective-permute-start(bf16[272,384]{1,0:T(8,128)(2,1)S(1)} %get-tuple-element.34), channel_id=1, source_target_pairs={{0,8},{4,12},{8,16},{12,20},{16,24},{20,28},{24,32},{28,36},{32,40... | collective-permute-start | bytes 626696 | tf_op jit(solution)/shard_map/ppermute | solution.py:576
  50.8 1.3 collective-permute-start.5
  53.3 4.6 %collective-permute-done.4 = bf16[272,384]{1,0:T(8,128)(2,1)S(1)} collective-permute-done((bf16[272,384]{1,0:T(8,128)(2,1)S(1)}, bf16[272,384]{1,0:T(8,128)(2,1)S(1)}, u32[]{:S(2)}, u32[]{:S(2)}) %collective-permute-start.4) | collective-permute-done | bytes 208928 | tf_op jit(solution)/shard_map/ppermute | solution.py:576
  57.9 2.4 %collective-permute-done.5 = bf16[272,384]{1,0:T(8,128)(2,1)S(1)} collective-permute-done((bf16[272,384]{1,0:T(8,128)(2,1)S(1)}, bf16[272,384]{1,0:T(8,128)(2,1)S(1)}, u32[]{:S(2)}, u32[]{:S(2)}) %collective-permute-start.5) | collective-permute-done | bytes 208928 | tf_op jit(solution)/shard_map/ppermute | solution.py:576
  60.5 1.9 shard_map.139
  62.5 9.9 %all-to-all-start.1 = ((bf16[32,56,640]{2,1,0:T(8,128)(2,1)}), bf16[32,56,640]{2,1,0:T(8,128)(2,1)}, u32[]{:S(2)}, u32[]{:S(2)}) async-start(bf16[32,56,640]{2,1,0:T(8,128)(2,1)} %shard_map.139), calls=%async_computation.1 | async-start | bytes 4587520 | tf_op jit(solution)/shard_map/all_to_all | solution.py:633
  72.4 2.2 %collective-permute-start.7 = (bf16[4,272,384]{2,1,0:T(8,128)(2,1)S(1)}, bf16[4,272,384]{2,1,0:T(8,128)(2,1)}, u32[]{:S(2)}, u32[]{:S(2)}) collective-permute-start(bf16[4,272,384]{2,1,0:T(8,128)(2,1)S(1)} %pad_maximum_fusion.own_ref), channel_id=1, source_target_pairs={{0,4},{4,0},{1,5},{5,1},{2,6},{6,2},{3,7},{7,3},{8,12},{12,8},{9,1... | collective-permute-start | bytes 2506760 | tf_op jit(solution)/shard_map/ppermute | solution.py:637
  76.8 5.8 %shard_map.140.joined_hbm = bf16[2192,640]{1,0:T(8,128)(2,1)} custom-call(bf16[4,272,384]{2,1,0:T(8,128)(2,1)} %copy-done.10, bf16[4,272,384]{2,1,0:T(8,128)(2,1)} %collective-permute-done.7.other_ref, bf16[384,384]{1,0:T(8,128)(2,1)} %copy-done.2), custom_call_target="tpu_custom_call" | custom-call | tf_op jit(solution)/shard_map/pallas_call | solution.py:635
  82.6 18.7 %all-to-all-done.1.found_hbm = bf16[32,56,640]{2,1,0:T(8,128)(2,1)} async-done(((bf16[32,56,640]{2,1,0:T(8,128)(2,1)}), bf16[32,56,640]{2,1,0:T(8,128)(2,1)}, u32[]{:S(2)}, u32[]{:S(2)}) %all-to-all-start.1) | async-done | bytes 2293792 | tf_op jit(solution)/shard_map/all_to_all | solution.py:633
  101.4 6.1 %shard_map.141 = (bf16[1920,512]{1,0:T(8,128)(2,1)}, f32[1,384]{1,0:T(1,128)S(1)}, f32[32,1,128]{2,1,0:T(1,128)}) custom-call(bf16[2192,640]{1,0:T(8,128)(2,1)} %shard_map.140.joined_hbm, bf16[32,56,640]{2,1,0:T(8,128)(2,1)} %all-to-all-done.1.found_hbm, bf16[320,1280]{1,0:T(8,128)(2,1)S(1)} %bitcast.21, f32[1,640]{1,0:T(1,128)S(1)} %broadcast_in_dim.8.gain_ref), custom_call_target="tpu_custom_call" | custom-call | tf_op jit(solution)/shard_map/pallas_call | solution.py:647
  107.5 5.5 %all-to-all-start.2 = ((f32[32,1,128]{2,1,0:T(1,128)}), f32[32,1,128]{2,1,0:T(1,128)S(1)}, u32[]{:S(2)}, u32[]{:S(2)}) async-start(f32[32,1,128]{2,1,0:T(1,128)} %get-tuple-element.38), calls=%async_computation.2 | async-start | bytes 32768 | tf_op jit(solution)/shard_map/all_to_all | solution.py:580
  113.0 6.6 %shard_map.142.own_hbm = f32[1648,256]{1,0:T(8,128)S(1)} custom-call(bf16[2192,640]{1,0:T(8,128)(2,1)} %shard_map.140.joined_hbm, bf16[1920,512]{1,0:T(8,128)(2,1)} %get-tuple-element.39.wm_hbm, f32[1,384]{1,0:T(1,128)S(1)} %get-tuple-element.40.known_ref, f32[1,640]{1,0:T(1,128)S(1)} %broadcast_in_dim.8.gain_ref), custom_call_target="tpu_custom_call" | custom-call | tf_op jit(solution)/shard_map/pallas_call | solution.py:657
  119.9 2.7 %collective-permute-start.8 = (f32[1648,256]{1,0:T(8,128)S(1)}, f32[1648,256]{1,0:T(8,128)}, u32[]{:S(2)}, u32[]{:S(2)}) collective-permute-start(f32[1648,256]{1,0:T(8,128)S(1)} %shard_map.142.own_hbm), channel_id=1, source_target_pairs={{0,4},{4,0},{1,5},{5,1},{2,6},{6,2},{3,7},{7,3},{8,12},{12,8},{9,1... | collective-permute-start | bytes 5062664 | tf_op jit(solution)/shard_map/ppermute | solution.py:671
  123.3 11.5 %all-to-all-start.3 = ((f32[16,1,128]{2,1,0:T(1,128)}), f32[16,1,128]{2,1,0:T(1,128)S(1)}, u32[]{:S(2)}, u32[]{:S(2)}) async-start(f32[16,1,128]{2,1,0:T(1,128)} %shard_map.143), calls=%async_computation.3 | async-start | bytes 16384 | tf_op jit(solution)/shard_map/all_to_all | solution.py:583
  134.9 11.2 %all-to-all-done.3.stat_ref = f32[16,1,128]{2,1,0:T(1,128)S(1)} async-done(((f32[16,1,128]{2,1,0:T(1,128)}), f32[16,1,128]{2,1,0:T(1,128)S(1)}, u32[]{:S(2)}, u32[]{:S(2)}) %all-to-all-start.3) | async-done | bytes 8224 | tf_op jit(solution)/shard_map/all_to_all | solution.py:583
  146.1 1.2 copy-done.3
  147.4 4.7 %shard_map.144 = (bf16[1152,512]{1,0:T(8,128)(2,1)}, bf16[640,160]{1,0:T(8,128)(2,1)S(1)}, f32[32,1,128]{2,1,0:T(1,128)}) custom-call(f32[1648,256]{1,0:T(8,128)} %copy-done.1, f32[1648,256]{1,0:T(8,128)} %collective-permute-done.8.other_hbm, f32[16,1,128]{2,1,0:T(1,128)S(1)} %all-to-all-done.3.stat_ref, f32[2,160]{1,0:T(2,128)S(1)} %reshape.29.gain_ref, ...), custom_call_target="tpu_custom_call" | custom-call | tf_op jit(solution)/shard_map/pallas_call | solution.py:674
  152.1 8.0 %all-to-all-start.4 = ((f32[32,1,128]{2,1,0:T(1,128)}), f32[32,1,128]{2,1,0:T(1,128)S(1)}, u32[]{:S(2)}, u32[]{:S(2)}) async-start(f32[32,1,128]{2,1,0:T(1,128)} %get-tuple-element.44), calls=%async_computation.4 | async-start | bytes 32768 | tf_op jit(solution)/shard_map/all_to_all | solution.py:580
  160.2 5.2 %shard_map.145.own_hbm = f32[1104,256]{1,0:T(8,128)S(1)} custom-call(f32[1648,256]{1,0:T(8,128)} %copy-done.1, f32[1648,256]{1,0:T(8,128)} %collective-permute-done.8.other_hbm, f32[16,1,128]{2,1,0:T(1,128)S(1)} %all-to-all-done.3.stat_ref, f32[2,160]{1,0:T(2,128)S(1)} %reshape.29.gain_ref, bf16[1152,512]{1,0:T(8,128)(2,1)} %get-tuple-element.45.wm_hbm, ...), custom_call_target="tpu_custom_call" | custom-call | tf_op jit(solution)/shard_map/pallas_call | solution.py:692
  165.3 1.7 all-to-all-done.4.got_ref
  167.1 2.5 %collective-permute-start.9 = (f32[1104,256]{1,0:T(8,128)S(1)}, f32[1104,256]{1,0:T(8,128)S(1)}, u32[]{:S(2)}, u32[]{:S(2)}) collective-permute-start(f32[1104,256]{1,0:T(8,128)S(1)} %shard_map.145.own_hbm), channel_id=1, source_target_pairs={{0,4},{4,0},{1,5},{5,1},{2,6},{6,2},{3,7},{7,3},{8,12},{12,8},{9,1... | collective-permute-start | bytes 3391496 | tf_op jit(solution)/shard_map/ppermute | solution.py:708
  170.4 3.4 %all-to-all-start.5 = ((f32[16,1,128]{2,1,0:T(1,128)}), f32[16,1,128]{2,1,0:T(1,128)S(1)}, u32[]{:S(2)}, u32[]{:S(2)}) async-start(f32[16,1,128]{2,1,0:T(1,128)} %shard_map.146), calls=%async_computation.5 | async-start | bytes 16384 | tf_op jit(solution)/shard_map/all_to_all | solution.py:583
  174.1 10.9 %all-to-all-done.5.stat_ref = f32[16,1,128]{2,1,0:T(1,128)S(1)} async-done(((f32[16,1,128]{2,1,0:T(1,128)}), f32[16,1,128]{2,1,0:T(1,128)S(1)}, u32[]{:S(2)}, u32[]{:S(2)}) %all-to-all-start.5) | async-done | bytes 8224 | tf_op jit(solution)/shard_map/all_to_all | solution.py:583
  185.0 2.0 %shard_map.147 = f32[4,1,256]{2,1,0:T(1,128)} custom-call(f32[1104,256]{1,0:T(8,128)S(1)} %shard_map.145.own_hbm, f32[1104,256]{1,0:T(8,128)S(1)} %collective-permute-done.9.other_hbm, f32[16,1,128]{2,1,0:T(1,128)S(1)} %all-to-all-done.5.stat_ref, f32[2,160]{1,0:T(2,128)S(1)} %reshape.30.gain_ref, bf16[2,160,128]{2,1,0:T(8,128)(2,1)S(1)} %pad.14.wout_ref), custom_call_target="tpu_custom_call" | custom-call | tf_op jit(solution)/shard_map/pallas_call | solution.py:717
  (62 shorter events, 9.4 us)
Async XLA Ops:
  6.5 36.3 %copy-start = (bf16[320,1280]{1,0:T(8,128)(2,1)S(1)}, bf16[320,1280]{1,0:T(8,128)(2,1)}, u32[]{:S(2)}) copy-start(bf16[320,1280]{1,0:T(8,128)(2,1)} %param.22) | copy-start | bytes 2457604
  6.5 11.7 %collective-permute-start = (bf16[4,1,256]{2,0,1:T(4,128)(2,1)}, bf16[4,1,256]{2,0,1:T(4,128)(2,1)S(1)}, u32[]{:S(2)}, u32[]{:S(2)}) collective-permute-start(bf16[4,1,256]{2,0,1:T(4,128)(2,1)} %param.14), channel_id=1, source_target_pairs={{0,4},{4,8},{8,12},{12,16},{16,20},{20,24},{24,28},{28,32},{32,36}... | collective-permute-start | bytes 6152 | tf_op jit(solution)/shard_map/ppermute | solution.py:576
  11.3 7.0 %collective-permute-start.1 = (bf16[4,1,256]{2,0,1:T(4,128)(2,1)}, bf16[4,1,256]{2,0,1:T(4,128)(2,1)S(1)}, u32[]{:S(2)}, u32[]{:S(2)}) collective-permute-start(bf16[4,1,256]{2,0,1:T(4,128)(2,1)} %param.14), channel_id=1, source_target_pairs={{4,0},{8,4},{12,8},{16,12},{20,16},{24,20},{28,24},{32,28},{36,32}... | collective-permute-start | bytes 6152 | tf_op jit(solution)/shard_map/ppermute | solution.py:576
  18.2 0.9 copy-start.6
  19.1 0.8 copy-start.8
  19.9 0.7 copy-start.9
  20.7 41.7 %copy-start.2 = (bf16[384,384]{1,0:T(8,128)(2,1)}, bf16[384,384]{1,0:T(8,128)(2,1)S(1)}, u32[]{:S(2)}) copy-start(bf16[384,384]{1,0:T(8,128)(2,1)S(1)} %get-tuple-element.30.wpad_ref) | copy-start | bytes 884740
  20.8 2.7 %collective-permute-start.2 = (bf16[16,384]{1,0:T(8,128)(2,1)S(1)}, bf16[16,384]{1,0:T(8,128)(2,1)S(1)}, u32[]{:S(2)}, u32[]{:S(2)}) collective-permute-start(bf16[16,384]{1,0:T(8,128)(2,1)S(1)} %get-tuple-element.28), channel_id=1, source_target_pairs={{0,1},{1,2},{2,3},{4,5},{5,6},{6,7},{8,9},{9,10},{10,11},{12,13},{... | collective-permute-start | bytes 36872 | tf_op jit(solution)/shard_map/ppermute | solution.py:576
  22.1 4.4 %collective-permute-start.3 = (bf16[16,384]{1,0:T(8,128)(2,1)S(1)}, bf16[16,384]{1,0:T(8,128)(2,1)S(1)}, u32[]{:S(2)}, u32[]{:S(2)}) collective-permute-start(bf16[16,384]{1,0:T(8,128)(2,1)S(1)} %get-tuple-element.29), channel_id=1, source_target_pairs={{1,0},{2,1},{3,2},{5,4},{6,5},{7,6},{9,8},{10,9},{11,10},{13,12},{... | collective-permute-start | bytes 36872 | tf_op jit(solution)/shard_map/ppermute | solution.py:576
  27.9 32.6 %all-to-all-start = ((bf16[16,16,320]{2,1,0:T(8,128)(2,1)}), bf16[16,16,320]{2,1,0:T(8,128)(2,1)S(1)}, u32[]{:S(2)}, u32[]{:S(2)}) async-start(bf16[16,16,320]{2,1,0:T(8,128)(2,1)} %get-tuple-element.33), calls=%async_computation | async-start | bytes 393216 | tf_op jit(solution)/shard_map/all_to_all | solution.py:624
  43.2 10.1 %collective-permute-start.6 = (bf16[272,384]{1,0:T(8,128)(2,1)S(1)}, bf16[272,384]{1,0:T(8,128)(2,1)S(1)}, u32[]{:S(2)}, u32[]{:S(2)}) collective-permute-start(bf16[272,384]{1,0:T(8,128)(2,1)S(1)} %get-tuple-element.34), channel_id=1, source_target_pairs={{4,16},{12,24},{16,4},{20,32},{24,12},{28,40},{32,20},{36,48},{40,... | collective-permute-start | bytes 626696 | tf_op jit(solution)/shard_map/ppermute | solution.py:612
  48.5 9.4 %collective-permute-start.4 = (bf16[272,384]{1,0:T(8,128)(2,1)S(1)}, bf16[272,384]{1,0:T(8,128)(2,1)S(1)}, u32[]{:S(2)}, u32[]{:S(2)}) collective-permute-start(bf16[272,384]{1,0:T(8,128)(2,1)S(1)} %get-tuple-element.34), channel_id=1, source_target_pairs={{0,8},{4,12},{8,16},{12,20},{16,24},{20,28},{24,32},{28,36},{32,40... | collective-permute-start | bytes 626696 | tf_op jit(solution)/shard_map/ppermute | solution.py:576
  50.8 9.6 %collective-permute-start.5 = (bf16[272,384]{1,0:T(8,128)(2,1)S(1)}, bf16[272,384]{1,0:T(8,128)(2,1)S(1)}, u32[]{:S(2)}, u32[]{:S(2)}) collective-permute-start(bf16[272,384]{1,0:T(8,128)(2,1)S(1)} %get-tuple-element.34), channel_id=1, source_target_pairs={{8,0},{12,4},{16,8},{20,12},{24,16},{28,20},{32,24},{36,28},{40,32... | collective-permute-start | bytes 626696 | tf_op jit(solution)/shard_map/ppermute | solution.py:576
  60.5 11.9 %copy-start.10 = (bf16[4,272,384]{2,1,0:T(8,128)(2,1)}, bf16[4,272,384]{2,1,0:T(8,128)(2,1)S(1)}, u32[]{:S(2)}) copy-start(bf16[4,272,384]{2,1,0:T(8,128)(2,1)S(1)} %pad_maximum_fusion.own_ref) | copy-start | bytes 2506756
  62.4 12.2 %copy-start.12 = (f32[640]{0:T(1024)S(1)}, f32[640]{0:T(1024)}, u32[]{:S(2)}) copy-start(f32[640]{0:T(1024)} %param.25) | copy-start | bytes 7684
  62.5 12.2 %copy-start.5 = (bf16[720,320]{0,1:T(8,128)(2,1)S(1)}, bf16[720,320]{0,1:T(8,128)(2,1)}, u32[]{:S(2)}) copy-start(bf16[720,320]{0,1:T(8,128)(2,1)} %param.19) | copy-start | bytes 1382404
  62.5 12.2 %copy-start.7 = (bf16[160,320]{1,0:T(8,128)(2,1)S(1)}, bf16[160,320]{1,0:T(8,128)(2,1)}, u32[]{:S(2)}) copy-start(bf16[160,320]{1,0:T(8,128)(2,1)} %skip_ref) | copy-start | bytes 307204
  62.5 38.9 %all-to-all-start.1 = ((bf16[32,56,640]{2,1,0:T(8,128)(2,1)}), bf16[32,56,640]{2,1,0:T(8,128)(2,1)}, u32[]{:S(2)}, u32[]{:S(2)}) async-start(bf16[32,56,640]{2,1,0:T(8,128)(2,1)} %shard_map.139), calls=%async_computation.1 | async-start | bytes 4587520 | tf_op jit(solution)/shard_map/all_to_all | solution.py:633
  72.4 73.7 %all-gather.3.cloned.1.call-start = ((), (), s32[]{:S(2)}) async-start(), calls=%async_computation.6 | async-start | bytes 1433600 | tf_op jit(solution)/shard_map/all_gather | solution.py:656
  72.4 4.4 %collective-permute-start.7 = (bf16[4,272,384]{2,1,0:T(8,128)(2,1)S(1)}, bf16[4,272,384]{2,1,0:T(8,128)(2,1)}, u32[]{:S(2)}, u32[]{:S(2)}) collective-permute-start(bf16[4,272,384]{2,1,0:T(8,128)(2,1)S(1)} %pad_maximum_fusion.own_ref), channel_id=1, source_target_pairs={{0,4},{4,0},{1,5},{5,1},{2,6},{6,2},{3,7},{7,3},{8,12},{12,8},{9,1... | collective-permute-start | bytes 2506760 | tf_op jit(solution)/shard_map/ppermute | solution.py:637
  75.7 25.6 %copy-start.4 = (bf16[1280,320]{0,1:T(8,128)(2,1)S(1)}, bf16[1280,320]{0,1:T(8,128)(2,1)}, u32[]{:S(2)}) copy-start(bf16[1280,320]{0,1:T(8,128)(2,1)} %param.24) | copy-start | bytes 2457604
  107.5 12.4 %all-to-all-start.2 = ((f32[32,1,128]{2,1,0:T(1,128)}), f32[32,1,128]{2,1,0:T(1,128)S(1)}, u32[]{:S(2)}, u32[]{:S(2)}) async-start(f32[32,1,128]{2,1,0:T(1,128)} %get-tuple-element.38), calls=%async_computation.2 | async-start | bytes 32768 | tf_op jit(solution)/shard_map/all_to_all | solution.py:580
  113.0 21.8 %copy-start.13 = (f32[320]{0:T(512)S(1)}, f32[320]{0:T(512)}, u32[]{:S(2)}) copy-start(f32[320]{0:T(512)} %param.26) | copy-start | bytes 3844
  119.6 26.5 %copy-start.1 = (f32[1648,256]{1,0:T(8,128)}, f32[1648,256]{1,0:T(8,128)S(1)}, u32[]{:S(2)}) copy-start(f32[1648,256]{1,0:T(8,128)S(1)} %shard_map.142.own_hbm) | copy-start | bytes 5062660
  119.9 26.2 %collective-permute-start.8 = (f32[1648,256]{1,0:T(8,128)S(1)}, f32[1648,256]{1,0:T(8,128)}, u32[]{:S(2)}, u32[]{:S(2)}) collective-permute-start(f32[1648,256]{1,0:T(8,128)S(1)} %shard_map.142.own_hbm), channel_id=1, source_target_pairs={{0,4},{4,0},{1,5},{5,1},{2,6},{6,2},{3,7},{7,3},{8,12},{12,8},{9,1... | collective-permute-start | bytes 5062664 | tf_op jit(solution)/shard_map/ppermute | solution.py:671
  123.3 22.8 %all-to-all-start.3 = ((f32[16,1,128]{2,1,0:T(1,128)}), f32[16,1,128]{2,1,0:T(1,128)S(1)}, u32[]{:S(2)}, u32[]{:S(2)}) async-start(f32[16,1,128]{2,1,0:T(1,128)} %shard_map.143), calls=%async_computation.3 | async-start | bytes 16384 | tf_op jit(solution)/shard_map/all_to_all | solution.py:583
  146.1 1.3 copy-start.3
  152.1 15.0 %all-to-all-start.4 = ((f32[32,1,128]{2,1,0:T(1,128)}), f32[32,1,128]{2,1,0:T(1,128)S(1)}, u32[]{:S(2)}, u32[]{:S(2)}) async-start(f32[32,1,128]{2,1,0:T(1,128)} %get-tuple-element.44), calls=%async_computation.4 | async-start | bytes 32768 | tf_op jit(solution)/shard_map/all_to_all | solution.py:580
  160.1 9.5 %copy-start.11 = (bf16[2880,4]{0,1:T(4,128)(2,1)S(1)}, bf16[2880,4]{0,1:T(4,128)(2,1)}, u32[]{:S(2)}) copy-start(bf16[2880,4]{0,1:T(4,128)(2,1)} %param.21) | copy-start | bytes 69124
  160.1 13.9 %copy-start.14 = (f32[320]{0:T(512)S(1)}, f32[320]{0:T(512)}, u32[]{:S(2)}) copy-start(f32[320]{0:T(512)} %param.27) | copy-start | bytes 3844
  167.1 18.0 %collective-permute-start.9 = (f32[1104,256]{1,0:T(8,128)S(1)}, f32[1104,256]{1,0:T(8,128)S(1)}, u32[]{:S(2)}, u32[]{:S(2)}) collective-permute-start(f32[1104,256]{1,0:T(8,128)S(1)} %shard_map.145.own_hbm), channel_id=1, source_target_pairs={{0,4},{4,0},{1,5},{5,1},{2,6},{6,2},{3,7},{7,3},{8,12},{12,8},{9,1... | collective-permute-start | bytes 3391496 | tf_op jit(solution)/shard_map/ppermute | solution.py:708
  170.4 14.6 %all-to-all-start.5 = ((f32[16,1,128]{2,1,0:T(1,128)}), f32[16,1,128]{2,1,0:T(1,128)S(1)}, u32[]{:S(2)}, u32[]{:S(2)}) async-start(f32[16,1,128]{2,1,0:T(1,128)} %shard_map.146), calls=%async_computation.5 | async-start | bytes 16384 | tf_op jit(solution)/shard_map/all_to_all | solution.py:583
Sparse Core Ops, SparseCore 0:
  107.6 29.7 all-gather.2

commit v6 on v5

--- a/solution.py
+++ b/solution.py
@@ -126,8 +126,10 @@
     both = jnp.concatenate([sums, squares, jnp.zeros((6, 2 * C), F32)], axis=0)
     grouped = exact_dot(both, same_group(2 * C, 32, 20, 1))
     terms = three_terms(jnp.concatenate([grouped[0:1], grouped[1:2]], axis=1))
-    line = jnp.concatenate([*terms, jnp.zeros((1, C - 192), F32)], axis=1)
-    message = jnp.concatenate([quarter_ref[...].astype(F32), line, jnp.zeros((3, C), F32)], axis=0).astype(BF16)
+    line = jnp.concatenate([*terms, jnp.zeros((1, 2 * C - 192), F32)], axis=1)
+    quarter = quarter_ref[...].astype(F32)
+    paired = jnp.concatenate([quarter[0:6], quarter[6:12]], axis=1)
+    message = jnp.concatenate([paired, line, jnp.zeros((1, 2 * C), F32)], axis=0).astype(BF16)
     for z in range(sent_ref.shape[0]):
         sent_ref[z] = message
 
@@ -138,8 +140,10 @@
         got = got_ref[z].astype(F32)
         q, d = divmod(z, 4)
         for half in (0, 1):
-            rows[half, 12 * d : 12 * d + 12, 160 * q : 160 * (q + 1)] = got[0:12, 160 * half : 160 * (half + 1)]
-        total = total + got[12:13, 0:64] + got[12:13, 64:128] + got[12:13, 128:192]
+            for side in (0, 1):
+                at, lane = 12 * d + 6 * side, C * side + HALF * half
+                rows[half, at : at + 6, 160 * q : 160 * (q + 1)] = got[0:6, lane : lane + HALF]
+        total = total + got[6:7, 0:64] + got[6:7, 64:128] + got[6:7, 128:192]
     first = jnp.concatenate([*three_terms(total), jnp.zeros((1, 4 * HALF - 192), F32)], axis=1)
     second = jnp.concatenate([*three_terms(part_ref[...]), jnp.zeros((1, HALF), F32)], axis=1)
     tail = jnp.concatenate([first, second, jnp.zeros((6, 4 * HALF), F32)], axis=0).astype(BF16)
@@ -599,7 +603,7 @@
         [pltpu.VMEM((LANES, WIDE), F32), pltpu.VMEM((LANES, LANES), F32)],
     )(deep.reshape(C, WIDE), above.reshape(4, WIDE), latent.reshape(4, WIDE), below.reshape(4, WIDE), in_weight)
     from_right, from_left = shifted(first, "x", -1), shifted(last, "x", 1)
-    row, sent = call(stats_kernel, (sds((SEG, LANES), BF16), sds((depths, 16, C), BF16)), [VMEM] * 5)(
+    row, sent = call(stats_kernel, (sds((SEG, LANES), BF16), sds((depths, 8, 2 * C), BF16)), [VMEM] * 5)(
         cells, from_left, from_right, wpad, quarter
     )
 

time: 195 us -> 195 us (level)
  transfers between devices with their start and end apart: 17 -> 17, of which waited for: 9 -> 10; matrix products, arithmetic and copies ran while one was open for 2% -> 2% of each run, Pallas kernels for 10% -> 10%
where the time goes in v6:
time: 195 us; the launch traced here: 194 us
  starting transfers between devices  82.7 us (42%)
  waiting for transfers between devices  53.7 us (28%)
  Pallas kernels  36.4 us (19%)
  between operations  14.5 us (7%)
  local copies, waits for them, and re-layouts  4.86 us (2%)
    all_to_all x2, waiting for transfers between devices, summed(): return (lax.all_to_all(near, DEPTH, 0, 0, tiled=True), kept)  22.1 us
    all_to_all x1, waiting for transfers between devices, shards(): found = lax.all_to_all(sent, PLANE, 0, 0, tiled=True)  18.7 us
    ppermute x6, starting transfers between devices, shifted(): lax.ppermute(x, axis, [(i, i + step) for i in range(count) if 0 <= i + st...  16.4 us
    all_to_all x2, starting transfers between devices, summed(): return (lax.all_to_all(near, DEPTH, 0, 0, tiled=True), kept)  15 us
    all_to_all x1, starting transfers between devices, shards(): got = lax.all_to_all(sent, DEPTH, 0, 0, tiled=True)  14.9 us
    all_to_all x2, starting transfers between devices, summed(): near = lax.all_to_all(sums, PLANE, 0, 0, tiled=True)  13.5 us
    all_to_all x1, starting transfers between devices, shards(): found = lax.all_to_all(sent, PLANE, 0, 0, tiled=True)  10.1 us
    ppermute x6, waiting for transfers between devices, shifted(): lax.ppermute(x, axis, [(i, i + step) for i in range(count) if 0 <= i + st...  9.51 us
  transfers between devices with their start and end apart: 17, of which 10 were waited for; matrix products, arithmetic and copies ran while one was open for 2% of the time, Pallas kernels for 10%

profile of v6, /device:TPU:1, one launch (start us, length us, event | category | flops | bytes accessed | tf_op | source)
XLA Modules:
  0.0 193.9 jit_solution(6182303791109609357)
XLA Ops:
  6.5 4.7 %collective-permute-start = (bf16[4,1,256]{2,0,1:T(4,128)(2,1)}, bf16[4,1,256]{2,0,1:T(4,128)(2,1)S(1)}, u32[]{:S(2)}, u32[]{:S(2)}) collective-permute-start(bf16[4,1,256]{2,0,1:T(4,128)(2,1)} %param.14), channel_id=1, source_target_pairs={{0,4},{4,8},{8,12},{12,16},{16,20},{20,24},{24,28},{28,32},{32,36}... | collective-permute-start | bytes 6152 | tf_op jit(solution)/shard_map/ppermute | solution.py:580
  11.3 5.5 %collective-permute-start.1 = (bf16[4,1,256]{2,0,1:T(4,128)(2,1)}, bf16[4,1,256]{2,0,1:T(4,128)(2,1)S(1)}, u32[]{:S(2)}, u32[]{:S(2)}) collective-permute-start(bf16[4,1,256]{2,0,1:T(4,128)(2,1)} %param.14), channel_id=1, source_target_pairs={{4,0},{8,4},{12,8},{16,12},{20,16},{24,20},{28,24},{32,28},{36,32}... | collective-permute-start | bytes 6152 | tf_op jit(solution)/shard_map/ppermute | solution.py:580
  20.8 1.3 collective-permute-start.2
  22.1 1.3 collective-permute-start.3
  23.4 3.1 %collective-permute-done.3.right_ref = bf16[16,384]{1,0:T(8,128)(2,1)S(1)} collective-permute-done((bf16[16,384]{1,0:T(8,128)(2,1)S(1)}, bf16[16,384]{1,0:T(8,128)(2,1)S(1)}, u32[]{:S(2)}, u32[]{:S(2)}) %collective-permute-start.3) | collective-permute-done | bytes 12320 | tf_op jit(solution)/shard_map/ppermute | solution.py:580
  26.5 1.4 shard_map.137
  27.9 14.9 %all-to-all-start = ((bf16[16,8,640]{2,1,0:T(8,128)(2,1)}), bf16[16,8,640]{2,1,0:T(8,128)(2,1)S(1)}, u32[]{:S(2)}, u32[]{:S(2)}) async-start(bf16[16,8,640]{2,1,0:T(8,128)(2,1)} %get-tuple-element.33), calls=%async_computation | async-start | bytes 327680 | tf_op jit(solution)/shard_map/all_to_all | solution.py:628
  43.2 5.3 %collective-permute-start.6 = (bf16[272,384]{1,0:T(8,128)(2,1)S(1)}, bf16[272,384]{1,0:T(8,128)(2,1)S(1)}, u32[]{:S(2)}, u32[]{:S(2)}) collective-permute-start(bf16[272,384]{1,0:T(8,128)(2,1)S(1)} %get-tuple-element.34), channel_id=1, source_target_pairs={{4,16},{12,24},{16,4},{20,32},{24,12},{28,40},{32,20},{36,48},{40,... | collective-permute-start | bytes 626696 | tf_op jit(solution)/shard_map/ppermute | solution.py:616
  48.5 2.3 %collective-permute-start.4 = (bf16[272,384]{1,0:T(8,128)(2,1)S(1)}, bf16[272,384]{1,0:T(8,128)(2,1)S(1)}, u32[]{:S(2)}, u32[]{:S(2)}) collective-permute-start(bf16[272,384]{1,0:T(8,128)(2,1)S(1)} %get-tuple-element.34), channel_id=1, source_target_pairs={{0,8},{4,12},{8,16},{12,20},{16,24},{20,28},{24,32},{28,36},{32,40... | collective-permute-start | bytes 626696 | tf_op jit(solution)/shard_map/ppermute | solution.py:580
  50.8 1.3 collective-permute-start.5
  53.5 4.4 %collective-permute-done.4 = bf16[272,384]{1,0:T(8,128)(2,1)S(1)} collective-permute-done((bf16[272,384]{1,0:T(8,128)(2,1)S(1)}, bf16[272,384]{1,0:T(8,128)(2,1)S(1)}, u32[]{:S(2)}, u32[]{:S(2)}) %collective-permute-start.4) | collective-permute-done | bytes 208928 | tf_op jit(solution)/shard_map/ppermute | solution.py:580
  57.9 2.1 %collective-permute-done.5 = bf16[272,384]{1,0:T(8,128)(2,1)S(1)} collective-permute-done((bf16[272,384]{1,0:T(8,128)(2,1)S(1)}, bf16[272,384]{1,0:T(8,128)(2,1)S(1)}, u32[]{:S(2)}, u32[]{:S(2)}) %collective-permute-start.5) | collective-permute-done | bytes 208928 | tf_op jit(solution)/shard_map/ppermute | solution.py:580
  60.1 1.9 shard_map.139
  62.1 10.1 %all-to-all-start.1 = ((bf16[32,56,640]{2,1,0:T(8,128)(2,1)}), bf16[32,56,640]{2,1,0:T(8,128)(2,1)}, u32[]{:S(2)}, u32[]{:S(2)}) async-start(bf16[32,56,640]{2,1,0:T(8,128)(2,1)} %shard_map.139), calls=%async_computation.1 | async-start | bytes 4587520 | tf_op jit(solution)/shard_map/all_to_all | solution.py:637
  72.3 2.2 %collective-permute-start.7 = (bf16[4,272,384]{2,1,0:T(8,128)(2,1)S(1)}, bf16[4,272,384]{2,1,0:T(8,128)(2,1)}, u32[]{:S(2)}, u32[]{:S(2)}) collective-permute-start(bf16[4,272,384]{2,1,0:T(8,128)(2,1)S(1)} %pad_maximum_fusion.own_ref), channel_id=1, source_target_pairs={{0,4},{4,0},{1,5},{5,1},{2,6},{6,2},{3,7},{7,3},{8,12},{12,8},{9,1... | collective-permute-start | bytes 2506760 | tf_op jit(solution)/shard_map/ppermute | solution.py:641
  76.7 5.8 %shard_map.140.joined_hbm = bf16[2192,640]{1,0:T(8,128)(2,1)} custom-call(bf16[4,272,384]{2,1,0:T(8,128)(2,1)} %copy-done.10, bf16[4,272,384]{2,1,0:T(8,128)(2,1)} %collective-permute-done.7.other_ref, bf16[384,384]{1,0:T(8,128)(2,1)} %copy-done.2), custom_call_target="tpu_custom_call" | custom-call | tf_op jit(solution)/shard_map/pallas_call | solution.py:639
  82.5 18.7 %all-to-all-done.1.found_hbm = bf16[32,56,640]{2,1,0:T(8,128)(2,1)} async-done(((bf16[32,56,640]{2,1,0:T(8,128)(2,1)}), bf16[32,56,640]{2,1,0:T(8,128)(2,1)}, u32[]{:S(2)}, u32[]{:S(2)}) %all-to-all-start.1) | async-done | bytes 2293792 | tf_op jit(solution)/shard_map/all_to_all | solution.py:637
  101.2 6.1 %shard_map.141 = (bf16[1920,512]{1,0:T(8,128)(2,1)}, f32[1,384]{1,0:T(1,128)S(1)}, f32[32,1,128]{2,1,0:T(1,128)}) custom-call(bf16[2192,640]{1,0:T(8,128)(2,1)} %shard_map.140.joined_hbm, bf16[32,56,640]{2,1,0:T(8,128)(2,1)} %all-to-all-done.1.found_hbm, bf16[320,1280]{1,0:T(8,128)(2,1)S(1)} %bitcast.21, f32[1,640]{1,0:T(1,128)S(1)} %broadcast_in_dim.8.gain_ref), custom_call_target="tpu_custom_call" | custom-call | tf_op jit(solution)/shard_map/pallas_call | solution.py:651
  107.4 5.5 %all-to-all-start.2 = ((f32[32,1,128]{2,1,0:T(1,128)}), f32[32,1,128]{2,1,0:T(1,128)S(1)}, u32[]{:S(2)}, u32[]{:S(2)}) async-start(f32[32,1,128]{2,1,0:T(1,128)} %get-tuple-element.38), calls=%async_computation.2 | async-start | bytes 32768 | tf_op jit(solution)/shard_map/all_to_all | solution.py:584
  112.9 6.6 %shard_map.142.own_hbm = f32[1648,256]{1,0:T(8,128)S(1)} custom-call(bf16[2192,640]{1,0:T(8,128)(2,1)} %shard_map.140.joined_hbm, bf16[1920,512]{1,0:T(8,128)(2,1)} %get-tuple-element.39.wm_hbm, f32[1,384]{1,0:T(1,128)S(1)} %get-tuple-element.40.known_ref, f32[1,640]{1,0:T(1,128)S(1)} %broadcast_in_dim.8.gain_ref), custom_call_target="tpu_custom_call" | custom-call | tf_op jit(solution)/shard_map/pallas_call | solution.py:661
  119.8 2.7 %collective-permute-start.8 = (f32[1648,256]{1,0:T(8,128)S(1)}, f32[1648,256]{1,0:T(8,128)}, u32[]{:S(2)}, u32[]{:S(2)}) collective-permute-start(f32[1648,256]{1,0:T(8,128)S(1)} %shard_map.142.own_hbm), channel_id=1, source_target_pairs={{0,4},{4,0},{1,5},{5,1},{2,6},{6,2},{3,7},{7,3},{8,12},{12,8},{9,1... | collective-permute-start | bytes 5062664 | tf_op jit(solution)/shard_map/ppermute | solution.py:675
  123.2 11.6 %all-to-all-start.3 = ((f32[16,1,128]{2,1,0:T(1,128)}), f32[16,1,128]{2,1,0:T(1,128)S(1)}, u32[]{:S(2)}, u32[]{:S(2)}) async-start(f32[16,1,128]{2,1,0:T(1,128)} %shard_map.143), calls=%async_computation.3 | async-start | bytes 16384 | tf_op jit(solution)/shard_map/all_to_all | solution.py:587
  134.9 11.2 %all-to-all-done.3.stat_ref = f32[16,1,128]{2,1,0:T(1,128)S(1)} async-done(((f32[16,1,128]{2,1,0:T(1,128)}), f32[16,1,128]{2,1,0:T(1,128)S(1)}, u32[]{:S(2)}, u32[]{:S(2)}) %all-to-all-start.3) | async-done | bytes 8224 | tf_op jit(solution)/shard_map/all_to_all | solution.py:587
  146.1 1.2 copy-done.3
  147.3 4.7 %shard_map.144 = (bf16[1152,512]{1,0:T(8,128)(2,1)}, bf16[640,160]{1,0:T(8,128)(2,1)S(1)}, f32[32,1,128]{2,1,0:T(1,128)}) custom-call(f32[1648,256]{1,0:T(8,128)} %copy-done.1, f32[1648,256]{1,0:T(8,128)} %collective-permute-done.8.other_hbm, f32[16,1,128]{2,1,0:T(1,128)S(1)} %all-to-all-done.3.stat_ref, f32[2,160]{1,0:T(2,128)S(1)} %reshape.29.gain_ref, ...), custom_call_target="tpu_custom_call" | custom-call | tf_op jit(solution)/shard_map/pallas_call | solution.py:678
  152.1 8.0 %all-to-all-start.4 = ((f32[32,1,128]{2,1,0:T(1,128)}), f32[32,1,128]{2,1,0:T(1,128)S(1)}, u32[]{:S(2)}, u32[]{:S(2)}) async-start(f32[32,1,128]{2,1,0:T(1,128)} %get-tuple-element.44), calls=%async_computation.4 | async-start | bytes 32768 | tf_op jit(solution)/shard_map/all_to_all | solution.py:584
  160.1 5.2 %shard_map.145.own_hbm = f32[1104,256]{1,0:T(8,128)S(1)} custom-call(f32[1648,256]{1,0:T(8,128)} %copy-done.1, f32[1648,256]{1,0:T(8,128)} %collective-permute-done.8.other_hbm, f32[16,1,128]{2,1,0:T(1,128)S(1)} %all-to-all-done.3.stat_ref, f32[2,160]{1,0:T(2,128)S(1)} %reshape.29.gain_ref, bf16[1152,512]{1,0:T(8,128)(2,1)} %get-tuple-element.45.wm_hbm, ...), custom_call_target="tpu_custom_call" | custom-call | tf_op jit(solution)/shard_map/pallas_call | solution.py:696
  165.3 1.7 all-to-all-done.4.got_ref
  167.0 2.5 %collective-permute-start.9 = (f32[1104,256]{1,0:T(8,128)S(1)}, f32[1104,256]{1,0:T(8,128)S(1)}, u32[]{:S(2)}, u32[]{:S(2)}) collective-permute-start(f32[1104,256]{1,0:T(8,128)S(1)} %shard_map.145.own_hbm), channel_id=1, source_target_pairs={{0,4},{4,0},{1,5},{5,1},{2,6},{6,2},{3,7},{7,3},{8,12},{12,8},{9,1... | collective-permute-start | bytes 3391496 | tf_op jit(solution)/shard_map/ppermute | solution.py:712
  170.4 3.4 %all-to-all-start.5 = ((f32[16,1,128]{2,1,0:T(1,128)}), f32[16,1,128]{2,1,0:T(1,128)S(1)}, u32[]{:S(2)}, u32[]{:S(2)}) async-start(f32[16,1,128]{2,1,0:T(1,128)} %shard_map.146), calls=%async_computation.5 | async-start | bytes 16384 | tf_op jit(solution)/shard_map/all_to_all | solution.py:587
  174.1 10.9 %all-to-all-done.5.stat_ref = f32[16,1,128]{2,1,0:T(1,128)S(1)} async-done(((f32[16,1,128]{2,1,0:T(1,128)}), f32[16,1,128]{2,1,0:T(1,128)S(1)}, u32[]{:S(2)}, u32[]{:S(2)}) %all-to-all-start.5) | async-done | bytes 8224 | tf_op jit(solution)/shard_map/all_to_all | solution.py:587
  185.0 2.0 %shard_map.147 = f32[4,1,256]{2,1,0:T(1,128)} custom-call(f32[1104,256]{1,0:T(8,128)S(1)} %shard_map.145.own_hbm, f32[1104,256]{1,0:T(8,128)S(1)} %collective-permute-done.9.other_hbm, f32[16,1,128]{2,1,0:T(1,128)S(1)} %all-to-all-done.5.stat_ref, f32[2,160]{1,0:T(2,128)S(1)} %reshape.30.gain_ref, bf16[2,160,128]{2,1,0:T(8,128)(2,1)S(1)} %pad.14.wout_ref), custom_call_target="tpu_custom_call" | custom-call | tf_op jit(solution)/shard_map/pallas_call | solution.py:721
  (62 shorter events, 9.7 us)
Async XLA Ops:
  6.5 36.3 %copy-start = (bf16[320,1280]{1,0:T(8,128)(2,1)S(1)}, bf16[320,1280]{1,0:T(8,128)(2,1)}, u32[]{:S(2)}) copy-start(bf16[320,1280]{1,0:T(8,128)(2,1)} %param.22) | copy-start | bytes 2457604
  6.5 11.7 %collective-permute-start = (bf16[4,1,256]{2,0,1:T(4,128)(2,1)}, bf16[4,1,256]{2,0,1:T(4,128)(2,1)S(1)}, u32[]{:S(2)}, u32[]{:S(2)}) collective-permute-start(bf16[4,1,256]{2,0,1:T(4,128)(2,1)} %param.14), channel_id=1, source_target_pairs={{0,4},{4,8},{8,12},{12,16},{16,20},{20,24},{24,28},{28,32},{32,36}... | collective-permute-start | bytes 6152 | tf_op jit(solution)/shard_map/ppermute | solution.py:580
  11.3 7.0 %collective-permute-start.1 = (bf16[4,1,256]{2,0,1:T(4,128)(2,1)}, bf16[4,1,256]{2,0,1:T(4,128)(2,1)S(1)}, u32[]{:S(2)}, u32[]{:S(2)}) collective-permute-start(bf16[4,1,256]{2,0,1:T(4,128)(2,1)} %param.14), channel_id=1, source_target_pairs={{4,0},{8,4},{12,8},{16,12},{20,16},{24,20},{28,24},{32,28},{36,32}... | collective-permute-start | bytes 6152 | tf_op jit(solution)/shard_map/ppermute | solution.py:580
  18.2 0.9 copy-start.6
  19.1 0.8 copy-start.8
  19.9 0.7 copy-start.9
  20.7 41.3 %copy-start.2 = (bf16[384,384]{1,0:T(8,128)(2,1)}, bf16[384,384]{1,0:T(8,128)(2,1)S(1)}, u32[]{:S(2)}) copy-start(bf16[384,384]{1,0:T(8,128)(2,1)S(1)} %get-tuple-element.30.wpad_ref) | copy-start | bytes 884740
  20.8 2.7 %collective-permute-start.2 = (bf16[16,384]{1,0:T(8,128)(2,1)S(1)}, bf16[16,384]{1,0:T(8,128)(2,1)S(1)}, u32[]{:S(2)}, u32[]{:S(2)}) collective-permute-start(bf16[16,384]{1,0:T(8,128)(2,1)S(1)} %get-tuple-element.28), channel_id=1, source_target_pairs={{0,1},{1,2},{2,3},{4,5},{5,6},{6,7},{8,9},{9,10},{10,11},{12,13},{... | collective-permute-start | bytes 36872 | tf_op jit(solution)/shard_map/ppermute | solution.py:580
  22.1 4.4 %collective-permute-start.3 = (bf16[16,384]{1,0:T(8,128)(2,1)S(1)}, bf16[16,384]{1,0:T(8,128)(2,1)S(1)}, u32[]{:S(2)}, u32[]{:S(2)}) collective-permute-start(bf16[16,384]{1,0:T(8,128)(2,1)S(1)} %get-tuple-element.29), channel_id=1, source_target_pairs={{1,0},{2,1},{3,2},{5,4},{6,5},{7,6},{9,8},{10,9},{11,10},{13,12},{... | collective-permute-start | bytes 36872 | tf_op jit(solution)/shard_map/ppermute | solution.py:580
  27.9 32.2 %all-to-all-start = ((bf16[16,8,640]{2,1,0:T(8,128)(2,1)}), bf16[16,8,640]{2,1,0:T(8,128)(2,1)S(1)}, u32[]{:S(2)}, u32[]{:S(2)}) async-start(bf16[16,8,640]{2,1,0:T(8,128)(2,1)} %get-tuple-element.33), calls=%async_computation | async-start | bytes 327680 | tf_op jit(solution)/shard_map/all_to_all | solution.py:628
  43.2 10.4 %collective-permute-start.6 = (bf16[272,384]{1,0:T(8,128)(2,1)S(1)}, bf16[272,384]{1,0:T(8,128)(2,1)S(1)}, u32[]{:S(2)}, u32[]{:S(2)}) collective-permute-start(bf16[272,384]{1,0:T(8,128)(2,1)S(1)} %get-tuple-element.34), channel_id=1, source_target_pairs={{4,16},{12,24},{16,4},{20,32},{24,12},{28,40},{32,20},{36,48},{40,... | collective-permute-start | bytes 626696 | tf_op jit(solution)/shard_map/ppermute | solution.py:616
  48.5 9.4 %collective-permute-start.4 = (bf16[272,384]{1,0:T(8,128)(2,1)S(1)}, bf16[272,384]{1,0:T(8,128)(2,1)S(1)}, u32[]{:S(2)}, u32[]{:S(2)}) collective-permute-start(bf16[272,384]{1,0:T(8,128)(2,1)S(1)} %get-tuple-element.34), channel_id=1, source_target_pairs={{0,8},{4,12},{8,16},{12,20},{16,24},{20,28},{24,32},{28,36},{32,40... | collective-permute-start | bytes 626696 | tf_op jit(solution)/shard_map/ppermute | solution.py:580
  50.8 9.2 %collective-permute-start.5 = (bf16[272,384]{1,0:T(8,128)(2,1)S(1)}, bf16[272,384]{1,0:T(8,128)(2,1)S(1)}, u32[]{:S(2)}, u32[]{:S(2)}) collective-permute-start(bf16[272,384]{1,0:T(8,128)(2,1)S(1)} %get-tuple-element.34), channel_id=1, source_target_pairs={{8,0},{12,4},{16,8},{20,12},{24,16},{28,20},{32,24},{36,28},{40,32... | collective-permute-start | bytes 626696 | tf_op jit(solution)/shard_map/ppermute | solution.py:580
  60.1 12.2 %copy-start.10 = (bf16[4,272,384]{2,1,0:T(8,128)(2,1)}, bf16[4,272,384]{2,1,0:T(8,128)(2,1)S(1)}, u32[]{:S(2)}) copy-start(bf16[4,272,384]{2,1,0:T(8,128)(2,1)S(1)} %pad_maximum_fusion.own_ref) | copy-start | bytes 2506756
  62.1 12.4 %copy-start.12 = (f32[640]{0:T(1024)S(1)}, f32[640]{0:T(1024)}, u32[]{:S(2)}) copy-start(f32[640]{0:T(1024)} %param.25) | copy-start | bytes 7684
  62.1 12.4 %copy-start.5 = (bf16[720,320]{0,1:T(8,128)(2,1)S(1)}, bf16[720,320]{0,1:T(8,128)(2,1)}, u32[]{:S(2)}) copy-start(bf16[720,320]{0,1:T(8,128)(2,1)} %param.19) | copy-start | bytes 1382404
  62.1 12.4 %copy-start.7 = (bf16[160,320]{1,0:T(8,128)(2,1)S(1)}, bf16[160,320]{1,0:T(8,128)(2,1)}, u32[]{:S(2)}) copy-start(bf16[160,320]{1,0:T(8,128)(2,1)} %skip_ref) | copy-start | bytes 307204
  62.1 39.1 %all-to-all-start.1 = ((bf16[32,56,640]{2,1,0:T(8,128)(2,1)}), bf16[32,56,640]{2,1,0:T(8,128)(2,1)}, u32[]{:S(2)}, u32[]{:S(2)}) async-start(bf16[32,56,640]{2,1,0:T(8,128)(2,1)} %shard_map.139), calls=%async_computation.1 | async-start | bytes 4587520 | tf_op jit(solution)/shard_map/all_to_all | solution.py:637
  72.2 73.8 %all-gather.3.cloned.1.call-start = ((), (), s32[]{:S(2)}) async-start(), calls=%async_computation.6 | async-start | bytes 1433600 | tf_op jit(solution)/shard_map/all_gather | solution.py:660
  72.3 4.4 %collective-permute-start.7 = (bf16[4,272,384]{2,1,0:T(8,128)(2,1)S(1)}, bf16[4,272,384]{2,1,0:T(8,128)(2,1)}, u32[]{:S(2)}, u32[]{:S(2)}) collective-permute-start(bf16[4,272,384]{2,1,0:T(8,128)(2,1)S(1)} %pad_maximum_fusion.own_ref), channel_id=1, source_target_pairs={{0,4},{4,0},{1,5},{5,1},{2,6},{6,2},{3,7},{7,3},{8,12},{12,8},{9,1... | collective-permute-start | bytes 2506760 | tf_op jit(solution)/shard_map/ppermute | solution.py:641
  75.6 25.6 %copy-start.4 = (bf16[1280,320]{0,1:T(8,128)(2,1)S(1)}, bf16[1280,320]{0,1:T(8,128)(2,1)}, u32[]{:S(2)}) copy-start(bf16[1280,320]{0,1:T(8,128)(2,1)} %param.24) | copy-start | bytes 2457604
  107.4 12.4 %all-to-all-start.2 = ((f32[32,1,128]{2,1,0:T(1,128)}), f32[32,1,128]{2,1,0:T(1,128)S(1)}, u32[]{:S(2)}, u32[]{:S(2)}) async-start(f32[32,1,128]{2,1,0:T(1,128)} %get-tuple-element.38), calls=%async_computation.2 | async-start | bytes 32768 | tf_op jit(solution)/shard_map/all_to_all | solution.py:584
  112.9 21.9 %copy-start.13 = (f32[320]{0:T(512)S(1)}, f32[320]{0:T(512)}, u32[]{:S(2)}) copy-start(f32[320]{0:T(512)} %param.26) | copy-start | bytes 3844
  119.5 26.6 %copy-start.1 = (f32[1648,256]{1,0:T(8,128)}, f32[1648,256]{1,0:T(8,128)S(1)}, u32[]{:S(2)}) copy-start(f32[1648,256]{1,0:T(8,128)S(1)} %shard_map.142.own_hbm) | copy-start | bytes 5062660
  119.8 26.3 %collective-permute-start.8 = (f32[1648,256]{1,0:T(8,128)S(1)}, f32[1648,256]{1,0:T(8,128)}, u32[]{:S(2)}, u32[]{:S(2)}) collective-permute-start(f32[1648,256]{1,0:T(8,128)S(1)} %shard_map.142.own_hbm), channel_id=1, source_target_pairs={{0,4},{4,0},{1,5},{5,1},{2,6},{6,2},{3,7},{7,3},{8,12},{12,8},{9,1... | collective-permute-start | bytes 5062664 | tf_op jit(solution)/shard_map/ppermute | solution.py:675
  123.2 22.9 %all-to-all-start.3 = ((f32[16,1,128]{2,1,0:T(1,128)}), f32[16,1,128]{2,1,0:T(1,128)S(1)}, u32[]{:S(2)}, u32[]{:S(2)}) async-start(f32[16,1,128]{2,1,0:T(1,128)} %shard_map.143), calls=%async_computation.3 | async-start | bytes 16384 | tf_op jit(solution)/shard_map/all_to_all | solution.py:587
  146.1 1.3 copy-start.3
  152.1 15.0 %all-to-all-start.4 = ((f32[32,1,128]{2,1,0:T(1,128)}), f32[32,1,128]{2,1,0:T(1,128)S(1)}, u32[]{:S(2)}, u32[]{:S(2)}) async-start(f32[32,1,128]{2,1,0:T(1,128)} %get-tuple-element.44), calls=%async_computation.4 | async-start | bytes 32768 | tf_op jit(solution)/shard_map/all_to_all | solution.py:584
  160.1 9.5 %copy-start.11 = (bf16[2880,4]{0,1:T(4,128)(2,1)S(1)}, bf16[2880,4]{0,1:T(4,128)(2,1)}, u32[]{:S(2)}) copy-start(bf16[2880,4]{0,1:T(4,128)(2,1)} %param.21) | copy-start | bytes 69124
  160.1 13.9 %copy-start.14 = (f32[320]{0:T(512)S(1)}, f32[320]{0:T(512)}, u32[]{:S(2)}) copy-start(f32[320]{0:T(512)} %param.27) | copy-start | bytes 3844
  167.0 18.0 %collective-permute-start.9 = (f32[1104,256]{1,0:T(8,128)S(1)}, f32[1104,256]{1,0:T(8,128)S(1)}, u32[]{:S(2)}, u32[]{:S(2)}) collective-permute-start(f32[1104,256]{1,0:T(8,128)S(1)} %shard_map.145.own_hbm), channel_id=1, source_target_pairs={{0,4},{4,0},{1,5},{5,1},{2,6},{6,2},{3,7},{7,3},{8,12},{12,8},{9,1... | collective-permute-start | bytes 3391496 | tf_op jit(solution)/shard_map/ppermute | solution.py:712
  170.4 14.6 %all-to-all-start.5 = ((f32[16,1,128]{2,1,0:T(1,128)}), f32[16,1,128]{2,1,0:T(1,128)S(1)}, u32[]{:S(2)}, u32[]{:S(2)}) async-start(f32[16,1,128]{2,1,0:T(1,128)} %shard_map.146), calls=%async_computation.5 | async-start | bytes 16384 | tf_op jit(solution)/shard_map/all_to_all | solution.py:587
Sparse Core Ops, SparseCore 0:
  107.5 29.8 all-gather.2

commit v7 on v5

--- a/solution.py
+++ b/solution.py
@@ -369,38 +369,48 @@
     act[where, :] = jnp.concatenate(parts, axis=1).astype(BF16)
 
 
+def middle_weight_kernel(found_hbm, wm_hbm, skip_hbm, found_ref, wm_ref, skip_ref, sems):
+    copy = pltpu.make_async_copy(found_hbm, found_ref, sems.at[0])
+    copy.start()
+    copy.wait()
+    middle_weight(found_ref, wm_ref, skip_ref)
+    back = [
+        pltpu.make_async_copy(wm_ref, wm_hbm, sems.at[1]),
+        pltpu.make_async_copy(skip_ref, skip_hbm, sems.at[2]),
+    ]
+    for copy in back:
+        copy.start()
+    for copy in back:
+        copy.wait()
+
+
 def second_own_kernel(
-    own_hbm, other_hbm, stat_ref, gain_ref, found_hbm, joined_hbm,
-    wm_hbm, skip_hbm, sum_ref,
-    own_ref, other_ref, found_ref, joined_ref, wm_ref, skip_ref, act, merged, sems,
+    own_hbm, other_hbm, stat_ref, gain_ref, wm_hbm, skip_hbm, joined_hbm,
+    sum_ref,
+    own_ref, other_ref, joined_ref, wm_ref, skip_ref, act, merged, sems,
 ):
     part = slice(SEG, SEG + B_LEN)
     copies = [
-        pltpu.make_async_copy(found_hbm, found_ref, sems.at[0]),
-        pltpu.make_async_copy(own_hbm.at[part], own_ref, sems.at[1]),
-        pltpu.make_async_copy(other_hbm.at[part], other_ref, sems.at[2]),
+        pltpu.make_async_copy(own_hbm.at[part], own_ref, sems.at[0]),
+        pltpu.make_async_copy(other_hbm.at[part], other_ref, sems.at[1]),
+        pltpu.make_async_copy(wm_hbm, wm_ref, sems.at[2]),
         pltpu.make_async_copy(joined_hbm.at[3 * SEG : 5 * SEG], joined_ref, sems.at[3]),
+        pltpu.make_async_copy(skip_hbm, skip_ref, sems.at[4]),
     ]
     for copy in copies:
         copy.start()
-    back = [
-        pltpu.make_async_copy(wm_ref, wm_hbm, sems.at[4]),
-        pltpu.make_async_copy(skip_ref, skip_hbm, sems.at[5]),
-    ]
     chip_row, first_col, _ = place()
     affines = affine(stat_ref, gain_ref)
     clear_ends(merged)
     copies[0].wait()
-    middle_weight(found_ref, wm_ref, skip_ref)
-    for copy in back:
-        copy.start()
     copies[1].wait()
-    copies[2].wait()
     for r in range(5):
         mask = keep_mask(r + 1, chip_row - 2, first_col)
         second_build(own_ref, other_ref, act, r * SEG, SEG if r < 4 else GAP, mask, affines)
+    copies[2].wait()
     merged_conv(act, wm_ref, merged, 0, 2 * SEG + GAP)
     copies[3].wait()
+    copies[4].wait()
     sums = jnp.zeros((1, HALF), F32)
     squares = jnp.zeros((1, HALF), F32)
     for r in range(2):
@@ -409,8 +419,6 @@
         sums = sums + jnp.sum(values, axis=0, keepdims=True)
         squares = squares + jnp.sum(values * values, axis=0, keepdims=True)
     send_sums(sums, squares, sum_ref)
-    for copy in back:
-        copy.wait()
 
 
 def second_kernel(
@@ -635,6 +643,8 @@
     joined = call(
         join_kernel, sds((A_LEN, 2 * C), BF16), [VMEM] * 3, [pltpu.VMEM((A_LEN + 2 * GAP, LANES), BF16)], 60
     )(around, lax.ppermute(around, "core", swap), wpad)
+    packed, found, joined = lax.optimization_barrier((packed, found, joined))
+    middle_found = lax.all_gather(packed, "x", axis=0)
     own_scratch = [
         pltpu.VMEM((B_LEN, 2 * C), BF16),
         pltpu.VMEM((32, 56, 4 * HALF), BF16),
@@ -652,8 +662,6 @@
         52,
         (ANY, VMEM, VMEM),
     )(joined, found, time_proj.T, input_gain[None])
-    packed, sums = lax.optimization_barrier((packed, sums))
-    middle_found = lax.all_gather(packed, "x", axis=0)
     hidden_own = call(
         first_kernel,
         sds((H_LEN, SWAP), F32),
@@ -671,24 +679,35 @@
     hidden_other = lax.ppermute(hidden_own, "core", swap)
 
     gain_two = middle_gain.reshape(2, HALF)
-    middle, shortcut, sums = call(
+    middle, shortcut = call(
+        middle_weight_kernel,
+        (sds((3 * LANES, MERGED), BF16), sds((2 * C, HALF), BF16)),
+        [ANY],
+        [
+            pltpu.VMEM((4, 224, 4 * HALF), BF16),
+            pltpu.VMEM((3 * LANES, MERGED), BF16),
+            pltpu.VMEM((2 * C, HALF), BF16),
+            pltpu.SemaphoreType.DMA((3,)),
+        ],
+        52,
+        (ANY, ANY),
+    )(middle_found.reshape(4, 224, 4 * HALF))
+    sums = call(
         second_own_kernel,
-        (sds((3 * LANES, MERGED), BF16), sds((2 * C, HALF), BF16), sds((32, 1, 128), F32)),
-        [ANY, ANY, VMEM, VMEM, ANY, ANY],
+        sds((32, 1, 128), F32),
+        [ANY, ANY, VMEM, VMEM, ANY, ANY, ANY],
         [
             pltpu.VMEM((B_LEN, SWAP), F32),
             pltpu.VMEM((B_LEN, SWAP), F32),
-            pltpu.VMEM((4, 224, 4 * HALF), BF16),
             pltpu.VMEM((2 * SEG, 2 * C), BF16),
             pltpu.VMEM((3 * LANES, MERGED), BF16),
             pltpu.VMEM((2 * C, HALF), BF16),
             pltpu.VMEM((B_LEN, LANES), BF16),
             pltpu.VMEM((2 * SEG + 3 * GAP, MERGED), F32),
-            pltpu.SemaphoreType.DMA((6,)),
+            pltpu.SemaphoreType.DMA((5,)),
         ],
         52,
-        (ANY, ANY, VMEM),
-    )(hidden_own, hidden_other, totals, gain_two, middle_found, joined)
+    )(hidden_own, hidden_other, totals, gain_two, middle, shortcut, joined)
     block_own = call(
         second_kernel,
         sds((B_LEN, SWAP), F32),

time: 195 us -> 195 us (level)
  waiting for transfers between devices: 54 us -> 50 us
  local copies, waits for them, and re-layouts: 4.86 us -> 7.09 us
    all_to_all x2, waiting for transfers between devices: 22.1 us -> 19 us  [summed(): return (lax.all_to_all(near, DEPTH, 0, 0, tiled=True), kept)]
    unnamed x31 -> x35, local copies, waits for them, and re-layouts: 3.67 us -> 5.9 us
    pallas_call x1 -> x2, Pallas kernels: 4.71 us -> 6.61 us  [the longest x1 4.83 us: shards(): call(second_own_kernel, sds((32, 1, 128), F32), [ANY, ANY, VMEM, VMEM, AN...]
  transfers between devices with their start and end apart: 17 -> 17, of which waited for: 9 -> 9; matrix products, arithmetic and copies ran while one was open for 2% -> 2% of each run, Pallas kernels for 10% -> 14%
where the time goes in v7:
time: 195 us; the launch traced here: 194 us
  starting transfers between devices  82.2 us (42%)
  waiting for transfers between devices  50 us (26%)
  Pallas kernels  38.3 us (20%)
  between operations  14.5 us (7%)
  local copies, waits for them, and re-layouts  7.09 us (4%)
    all_to_all x2, waiting for transfers between devices, summed(): return (lax.all_to_all(near, DEPTH, 0, 0, tiled=True), kept)  19 us
    all_to_all x1, waiting for transfers between devices, shards(): found = lax.all_to_all(sent, PLANE, 0, 0, tiled=True)  17.9 us
    ppermute x6, starting transfers between devices, shifted(): lax.ppermute(x, axis, [(i, i + step) for i in range(count) if 0 <= i + st...  16.4 us
    all_to_all x2, starting transfers between devices, summed(): return (lax.all_to_all(near, DEPTH, 0, 0, tiled=True), kept)  14.9 us
    all_to_all x1, starting transfers between devices, shards(): got = lax.all_to_all(sent, DEPTH, 0, 0, tiled=True)  14.9 us
    all_to_all x2, starting transfers between devices, summed(): near = lax.all_to_all(sums, PLANE, 0, 0, tiled=True)  13.6 us
    ppermute x6, waiting for transfers between devices, shifted(): lax.ppermute(x, axis, [(i, i + step) for i in range(count) if 0 <= i + st...  10.1 us
    all_to_all x1, starting transfers between devices, shards(): found = lax.all_to_all(sent, PLANE, 0, 0, tiled=True)  9.89 us
  transfers between devices with their start and end apart: 17, of which 9 were waited for; matrix products, arithmetic and copies ran while one was open for 2% of the time, Pallas kernels for 14%

profile of v7, /device:TPU:1, one launch (start us, length us, event | category | flops | bytes accessed | tf_op | source)
XLA Modules:
  0.0 193.9 jit_solution(15351359690310557034)
XLA Ops:
  6.5 4.7 %collective-permute-start = (bf16[4,1,256]{2,0,1:T(4,128)(2,1)}, bf16[4,1,256]{2,0,1:T(4,128)(2,1)S(1)}, u32[]{:S(2)}, u32[]{:S(2)}) collective-permute-start(bf16[4,1,256]{2,0,1:T(4,128)(2,1)} %param.14), channel_id=1, source_target_pairs={{0,4},{4,8},{8,12},{12,16},{16,20},{20,24},{24,28},{28,32},{32,36}... | collective-permute-start | bytes 6152 | tf_op jit(solution)/shard_map/ppermute | solution.py:584
  11.3 5.5 %collective-permute-start.1 = (bf16[4,1,256]{2,0,1:T(4,128)(2,1)}, bf16[4,1,256]{2,0,1:T(4,128)(2,1)S(1)}, u32[]{:S(2)}, u32[]{:S(2)}) collective-permute-start(bf16[4,1,256]{2,0,1:T(4,128)(2,1)} %param.14), channel_id=1, source_target_pairs={{4,0},{8,4},{12,8},{16,12},{20,16},{24,20},{28,24},{32,28},{36,32}... | collective-permute-start | bytes 6152 | tf_op jit(solution)/shard_map/ppermute | solution.py:584
  20.8 1.3 collective-permute-start.2
  22.1 1.3 collective-permute-start.3
  23.4 3.1 %collective-permute-done.3.right_ref = bf16[16,384]{1,0:T(8,128)(2,1)S(1)} collective-permute-done((bf16[16,384]{1,0:T(8,128)(2,1)S(1)}, bf16[16,384]{1,0:T(8,128)(2,1)S(1)}, u32[]{:S(2)}, u32[]{:S(2)}) %collective-permute-start.3) | collective-permute-done | bytes 12320 | tf_op jit(solution)/shard_map/ppermute | solution.py:584
  26.5 1.4 shard_map.137
  27.9 14.9 %all-to-all-start = ((bf16[16,16,320]{2,1,0:T(8,128)(2,1)}), bf16[16,16,320]{2,1,0:T(8,128)(2,1)S(1)}, u32[]{:S(2)}, u32[]{:S(2)}) async-start(bf16[16,16,320]{2,1,0:T(8,128)(2,1)} %get-tuple-element.33), calls=%async_computation | async-start | bytes 393216 | tf_op jit(solution)/shard_map/all_to_all | solution.py:632
  43.2 5.3 %collective-permute-start.6 = (bf16[272,384]{1,0:T(8,128)(2,1)S(1)}, bf16[272,384]{1,0:T(8,128)(2,1)S(1)}, u32[]{:S(2)}, u32[]{:S(2)}) collective-permute-start(bf16[272,384]{1,0:T(8,128)(2,1)S(1)} %get-tuple-element.34), channel_id=1, source_target_pairs={{4,16},{12,24},{16,4},{20,32},{24,12},{28,40},{32,20},{36,48},{40,... | collective-permute-start | bytes 626696 | tf_op jit(solution)/shard_map/ppermute | solution.py:620
  48.5 2.3 %collective-permute-start.4 = (bf16[272,384]{1,0:T(8,128)(2,1)S(1)}, bf16[272,384]{1,0:T(8,128)(2,1)S(1)}, u32[]{:S(2)}, u32[]{:S(2)}) collective-permute-start(bf16[272,384]{1,0:T(8,128)(2,1)S(1)} %get-tuple-element.34), channel_id=1, source_target_pairs={{0,8},{4,12},{8,16},{12,20},{16,24},{20,28},{24,32},{28,36},{32,40... | collective-permute-start | bytes 626696 | tf_op jit(solution)/shard_map/ppermute | solution.py:584
  50.8 1.3 collective-permute-start.5
  53.3 4.6 %collective-permute-done.4 = bf16[272,384]{1,0:T(8,128)(2,1)S(1)} collective-permute-done((bf16[272,384]{1,0:T(8,128)(2,1)S(1)}, bf16[272,384]{1,0:T(8,128)(2,1)S(1)}, u32[]{:S(2)}, u32[]{:S(2)}) %collective-permute-start.4) | collective-permute-done | bytes 208928 | tf_op jit(solution)/shard_map/ppermute | solution.py:584
  57.9 2.4 %collective-permute-done.5 = bf16[272,384]{1,0:T(8,128)(2,1)S(1)} collective-permute-done((bf16[272,384]{1,0:T(8,128)(2,1)S(1)}, bf16[272,384]{1,0:T(8,128)(2,1)S(1)}, u32[]{:S(2)}, u32[]{:S(2)}) %collective-permute-start.5) | collective-permute-done | bytes 208928 | tf_op jit(solution)/shard_map/ppermute | solution.py:584
  60.5 1.9 shard_map.139
  62.5 9.9 %all-to-all-start.1 = ((bf16[32,56,640]{2,1,0:T(8,128)(2,1)}), bf16[32,56,640]{2,1,0:T(8,128)(2,1)}, u32[]{:S(2)}, u32[]{:S(2)}) async-start(bf16[32,56,640]{2,1,0:T(8,128)(2,1)} %shard_map.139), calls=%async_computation.1 | async-start | bytes 4587520 | tf_op jit(solution)/shard_map/all_to_all | solution.py:641
  72.4 2.2 %collective-permute-start.7 = (bf16[4,272,384]{2,1,0:T(8,128)(2,1)S(1)}, bf16[4,272,384]{2,1,0:T(8,128)(2,1)S(1)}, u32[]{:S(2)}, u32[]{:S(2)}) collective-permute-start(bf16[4,272,384]{2,1,0:T(8,128)(2,1)S(1)} %pad_maximum_fusion.own_ref), channel_id=1, source_target_pairs={{0,4},{4,0},{1,5},{5,1},{2,6},{6,2},{3,7},{7,3},{8,12},{12,8},{9,1... | collective-permute-start | bytes 2506760 | tf_op jit(solution)/shard_map/ppermute | solution.py:645
  77.6 5.8 %shard_map.140.joined_hbm = bf16[2192,640]{1,0:T(8,128)(2,1)} custom-call(bf16[4,272,384]{2,1,0:T(8,128)(2,1)} %copy-done.11, bf16[4,272,384]{2,1,0:T(8,128)(2,1)} %copy-done.12, bf16[384,384]{1,0:T(8,128)(2,1)} %copy-done.3), custom_call_target="tpu_custom_call" | custom-call | tf_op jit(solution)/shard_map/pallas_call | solution.py:643
  83.4 17.9 %all-to-all-done.1.found_hbm = bf16[32,56,640]{2,1,0:T(8,128)(2,1)} async-done(((bf16[32,56,640]{2,1,0:T(8,128)(2,1)}), bf16[32,56,640]{2,1,0:T(8,128)(2,1)}, u32[]{:S(2)}, u32[]{:S(2)}) %all-to-all-start.1) | async-done | bytes 2293792 | tf_op jit(solution)/shard_map/all_to_all | solution.py:641
  101.4 6.1 %shard_map.141 = (bf16[1920,512]{1,0:T(8,128)(2,1)}, f32[1,384]{1,0:T(1,128)S(1)}, f32[32,1,128]{2,1,0:T(1,128)}) custom-call(bf16[2192,640]{1,0:T(8,128)(2,1)} %shard_map.140.joined_hbm, bf16[32,56,640]{2,1,0:T(8,128)(2,1)} %all-to-all-done.1.found_hbm, bf16[320,1280]{1,0:T(8,128)(2,1)S(1)} %bitcast.21, f32[1,640]{1,0:T(1,128)S(1)} %broadcast_in_dim.8.gain_ref), custom_call_target="tpu_custom_call" | custom-call | tf_op jit(solution)/shard_map/pallas_call | solution.py:657
  107.5 5.5 %all-to-all-start.2 = ((f32[32,1,128]{2,1,0:T(1,128)}), f32[32,1,128]{2,1,0:T(1,128)S(1)}, u32[]{:S(2)}, u32[]{:S(2)}) async-start(f32[32,1,128]{2,1,0:T(1,128)} %get-tuple-element.39), calls=%async_computation.2 | async-start | bytes 32768 | tf_op jit(solution)/shard_map/all_to_all | solution.py:588
  113.0 6.6 %shard_map.142.own_hbm = f32[1648,256]{1,0:T(8,128)S(1)} custom-call(bf16[2192,640]{1,0:T(8,128)(2,1)} %shard_map.140.joined_hbm, bf16[1920,512]{1,0:T(8,128)(2,1)} %get-tuple-element.40.wm_hbm, f32[1,384]{1,0:T(1,128)S(1)} %get-tuple-element.41.known_ref, f32[1,640]{1,0:T(1,128)S(1)} %broadcast_in_dim.8.gain_ref), custom_call_target="tpu_custom_call" | custom-call | tf_op jit(solution)/shard_map/pallas_call | solution.py:665
  119.9 2.5 %collective-permute-start.8 = (f32[1648,256]{1,0:T(8,128)S(1)}, f32[1648,256]{1,0:T(8,128)}, u32[]{:S(2)}, u32[]{:S(2)}) collective-permute-start(f32[1648,256]{1,0:T(8,128)S(1)} %shard_map.142.own_hbm), channel_id=1, source_target_pairs={{0,4},{4,0},{1,5},{5,1},{2,6},{6,2},{3,7},{7,3},{8,12},{12,8},{9,1... | collective-permute-start | bytes 5062664 | tf_op jit(solution)/shard_map/ppermute | solution.py:679
  123.2 11.5 %all-to-all-start.3 = ((f32[16,1,128]{2,1,0:T(1,128)}), f32[16,1,128]{2,1,0:T(1,128)S(1)}, u32[]{:S(2)}, u32[]{:S(2)}) async-start(f32[16,1,128]{2,1,0:T(1,128)} %shard_map.143), calls=%async_computation.3 | async-start | bytes 16384 | tf_op jit(solution)/shard_map/all_to_all | solution.py:591
  136.0 1.8 shard_map.144
  137.8 8.1 %all-to-all-done.3.stat_ref = f32[16,1,128]{2,1,0:T(1,128)S(1)} async-done(((f32[16,1,128]{2,1,0:T(1,128)}), f32[16,1,128]{2,1,0:T(1,128)S(1)}, u32[]{:S(2)}, u32[]{:S(2)}) %all-to-all-start.3) | async-done | bytes 8224 | tf_op jit(solution)/shard_map/all_to_all | solution.py:591
  147.2 4.8 %shard_map.145 = f32[32,1,128]{2,1,0:T(1,128)} custom-call(f32[1648,256]{1,0:T(8,128)} %copy-done.1, f32[1648,256]{1,0:T(8,128)} %collective-permute-done.8.other_hbm, f32[16,1,128]{2,1,0:T(1,128)S(1)} %all-to-all-done.3.stat_ref, f32[2,160]{1,0:T(2,128)S(1)} %reshape.29.gain_ref, bf16[1152,512]{1,0:T(8,128)(2,1)S(1)} %copy-done.2, ...), custom_call_target="tpu_custom_call" | custom-call | tf_op jit(solution)/shard_map/pallas_call | solution.py:695
  152.0 8.1 %all-to-all-start.4 = ((f32[32,1,128]{2,1,0:T(1,128)}), f32[32,1,128]{2,1,0:T(1,128)S(1)}, u32[]{:S(2)}, u32[]{:S(2)}) async-start(f32[32,1,128]{2,1,0:T(1,128)} %shard_map.145), calls=%async_computation.4 | async-start | bytes 32768 | tf_op jit(solution)/shard_map/all_to_all | solution.py:588
  160.2 5.2 %shard_map.146.own_hbm = f32[1104,256]{1,0:T(8,128)S(1)} custom-call(f32[1648,256]{1,0:T(8,128)} %copy-done.1, f32[1648,256]{1,0:T(8,128)} %collective-permute-done.8.other_hbm, f32[16,1,128]{2,1,0:T(1,128)S(1)} %all-to-all-done.3.stat_ref, f32[2,160]{1,0:T(2,128)S(1)} %reshape.29.gain_ref, bf16[1152,512]{1,0:T(8,128)(2,1)} %get-tuple-element.45.wm_hbm, ...), custom_call_target="tpu_custom_call" | custom-call | tf_op jit(solution)/shard_map/pallas_call | solution.py:711
  165.4 1.7 all-to-all-done.4.got_ref
  167.0 2.5 %collective-permute-start.9 = (f32[1104,256]{1,0:T(8,128)S(1)}, f32[1104,256]{1,0:T(8,128)S(1)}, u32[]{:S(2)}, u32[]{:S(2)}) collective-permute-start(f32[1104,256]{1,0:T(8,128)S(1)} %shard_map.146.own_hbm), channel_id=1, source_target_pairs={{0,4},{4,0},{1,5},{5,1},{2,6},{6,2},{3,7},{7,3},{8,12},{12,8},{9,1... | collective-permute-start | bytes 3391496 | tf_op jit(solution)/shard_map/ppermute | solution.py:727
  170.4 3.4 %all-to-all-start.5 = ((f32[16,1,128]{2,1,0:T(1,128)}), f32[16,1,128]{2,1,0:T(1,128)S(1)}, u32[]{:S(2)}, u32[]{:S(2)}) async-start(f32[16,1,128]{2,1,0:T(1,128)} %shard_map.147), calls=%async_computation.5 | async-start | bytes 16384 | tf_op jit(solution)/shard_map/all_to_all | solution.py:591
  174.1 10.9 %all-to-all-done.5.stat_ref = f32[16,1,128]{2,1,0:T(1,128)S(1)} async-done(((f32[16,1,128]{2,1,0:T(1,128)}), f32[16,1,128]{2,1,0:T(1,128)S(1)}, u32[]{:S(2)}, u32[]{:S(2)}) %all-to-all-start.5) | async-done | bytes 8224 | tf_op jit(solution)/shard_map/all_to_all | solution.py:591
  185.0 2.0 %shard_map.148 = f32[4,1,256]{2,1,0:T(1,128)} custom-call(f32[1104,256]{1,0:T(8,128)S(1)} %shard_map.146.own_hbm, f32[1104,256]{1,0:T(8,128)S(1)} %collective-permute-done.9.other_hbm, f32[16,1,128]{2,1,0:T(1,128)S(1)} %all-to-all-done.5.stat_ref, f32[2,160]{1,0:T(2,128)S(1)} %reshape.30.gain_ref, bf16[2,160,128]{2,1,0:T(8,128)(2,1)S(1)} %pad.14.wout_ref), custom_call_target="tpu_custom_call" | custom-call | tf_op jit(solution)/shard_map/pallas_call | solution.py:736
  (67 shorter events, 12.8 us)
Async XLA Ops:
  6.5 36.3 %copy-start = (bf16[320,1280]{1,0:T(8,128)(2,1)S(1)}, bf16[320,1280]{1,0:T(8,128)(2,1)}, u32[]{:S(2)}) copy-start(bf16[320,1280]{1,0:T(8,128)(2,1)} %param.22) | copy-start | bytes 2457604
  6.5 11.7 %collective-permute-start = (bf16[4,1,256]{2,0,1:T(4,128)(2,1)}, bf16[4,1,256]{2,0,1:T(4,128)(2,1)S(1)}, u32[]{:S(2)}, u32[]{:S(2)}) collective-permute-start(bf16[4,1,256]{2,0,1:T(4,128)(2,1)} %param.14), channel_id=1, source_target_pairs={{0,4},{4,8},{8,12},{12,16},{16,20},{20,24},{24,28},{28,32},{32,36}... | collective-permute-start | bytes 6152 | tf_op jit(solution)/shard_map/ppermute | solution.py:584
  11.3 7.0 %collective-permute-start.1 = (bf16[4,1,256]{2,0,1:T(4,128)(2,1)}, bf16[4,1,256]{2,0,1:T(4,128)(2,1)S(1)}, u32[]{:S(2)}, u32[]{:S(2)}) collective-permute-start(bf16[4,1,256]{2,0,1:T(4,128)(2,1)} %param.14), channel_id=1, source_target_pairs={{4,0},{8,4},{12,8},{16,12},{20,16},{24,20},{28,24},{32,28},{36,32}... | collective-permute-start | bytes 6152 | tf_op jit(solution)/shard_map/ppermute | solution.py:584
  18.2 0.9 copy-start.7
  20.7 41.7 %copy-start.3 = (bf16[384,384]{1,0:T(8,128)(2,1)}, bf16[384,384]{1,0:T(8,128)(2,1)S(1)}, u32[]{:S(2)}) copy-start(bf16[384,384]{1,0:T(8,128)(2,1)S(1)} %get-tuple-element.30.wpad_ref) | copy-start | bytes 884740
  20.8 2.7 %collective-permute-start.2 = (bf16[16,384]{1,0:T(8,128)(2,1)S(1)}, bf16[16,384]{1,0:T(8,128)(2,1)S(1)}, u32[]{:S(2)}, u32[]{:S(2)}) collective-permute-start(bf16[16,384]{1,0:T(8,128)(2,1)S(1)} %get-tuple-element.28), channel_id=1, source_target_pairs={{0,1},{1,2},{2,3},{4,5},{5,6},{6,7},{8,9},{9,10},{10,11},{12,13},{... | collective-permute-start | bytes 36872 | tf_op jit(solution)/shard_map/ppermute | solution.py:584
  22.1 4.4 %collective-permute-start.3 = (bf16[16,384]{1,0:T(8,128)(2,1)S(1)}, bf16[16,384]{1,0:T(8,128)(2,1)S(1)}, u32[]{:S(2)}, u32[]{:S(2)}) collective-permute-start(bf16[16,384]{1,0:T(8,128)(2,1)S(1)} %get-tuple-element.29), channel_id=1, source_target_pairs={{1,0},{2,1},{3,2},{5,4},{6,5},{7,6},{9,8},{10,9},{11,10},{13,12},{... | collective-permute-start | bytes 36872 | tf_op jit(solution)/shard_map/ppermute | solution.py:584
  27.9 32.6 %all-to-all-start = ((bf16[16,16,320]{2,1,0:T(8,128)(2,1)}), bf16[16,16,320]{2,1,0:T(8,128)(2,1)S(1)}, u32[]{:S(2)}, u32[]{:S(2)}) async-start(bf16[16,16,320]{2,1,0:T(8,128)(2,1)} %get-tuple-element.33), calls=%async_computation | async-start | bytes 393216 | tf_op jit(solution)/shard_map/all_to_all | solution.py:632
  43.2 10.1 %collective-permute-start.6 = (bf16[272,384]{1,0:T(8,128)(2,1)S(1)}, bf16[272,384]{1,0:T(8,128)(2,1)S(1)}, u32[]{:S(2)}, u32[]{:S(2)}) collective-permute-start(bf16[272,384]{1,0:T(8,128)(2,1)S(1)} %get-tuple-element.34), channel_id=1, source_target_pairs={{4,16},{12,24},{16,4},{20,32},{24,12},{28,40},{32,20},{36,48},{40,... | collective-permute-start | bytes 626696 | tf_op jit(solution)/shard_map/ppermute | solution.py:620
  48.5 9.4 %collective-permute-start.4 = (bf16[272,384]{1,0:T(8,128)(2,1)S(1)}, bf16[272,384]{1,0:T(8,128)(2,1)S(1)}, u32[]{:S(2)}, u32[]{:S(2)}) collective-permute-start(bf16[272,384]{1,0:T(8,128)(2,1)S(1)} %get-tuple-element.34), channel_id=1, source_target_pairs={{0,8},{4,12},{8,16},{12,20},{16,24},{20,28},{24,32},{28,36},{32,40... | collective-permute-start | bytes 626696 | tf_op jit(solution)/shard_map/ppermute | solution.py:584
  50.8 9.5 %collective-permute-start.5 = (bf16[272,384]{1,0:T(8,128)(2,1)S(1)}, bf16[272,384]{1,0:T(8,128)(2,1)S(1)}, u32[]{:S(2)}, u32[]{:S(2)}) collective-permute-start(bf16[272,384]{1,0:T(8,128)(2,1)S(1)} %get-tuple-element.34), channel_id=1, source_target_pairs={{8,0},{12,4},{16,8},{20,12},{24,16},{28,20},{32,24},{36,28},{40,32... | collective-permute-start | bytes 626696 | tf_op jit(solution)/shard_map/ppermute | solution.py:584
  60.5 11.9 %copy-start.11 = (bf16[4,272,384]{2,1,0:T(8,128)(2,1)}, bf16[4,272,384]{2,1,0:T(8,128)(2,1)S(1)}, u32[]{:S(2)}) copy-start(bf16[4,272,384]{2,1,0:T(8,128)(2,1)S(1)} %pad_maximum_fusion.own_ref) | copy-start | bytes 2506756
  62.4 12.2 %copy-start.6 = (bf16[720,320]{0,1:T(8,128)(2,1)S(1)}, bf16[720,320]{0,1:T(8,128)(2,1)}, u32[]{:S(2)}) copy-start(bf16[720,320]{0,1:T(8,128)(2,1)} %param.19) | copy-start | bytes 1382404
  62.4 12.2 %copy-start.8 = (bf16[160,320]{1,0:T(8,128)(2,1)S(1)}, bf16[160,320]{1,0:T(8,128)(2,1)}, u32[]{:S(2)}) copy-start(bf16[160,320]{1,0:T(8,128)(2,1)} %skip_ref) | copy-start | bytes 307204
  62.5 38.9 %all-to-all-start.1 = ((bf16[32,56,640]{2,1,0:T(8,128)(2,1)}), bf16[32,56,640]{2,1,0:T(8,128)(2,1)}, u32[]{:S(2)}, u32[]{:S(2)}) async-start(bf16[32,56,640]{2,1,0:T(8,128)(2,1)} %shard_map.139), calls=%async_computation.1 | async-start | bytes 4587520 | tf_op jit(solution)/shard_map/all_to_all | solution.py:641
  72.3 62.4 %all-gather.3.cloned.1.call-start = ((), (), s32[]{:S(2)}) async-start(), calls=%async_computation.6 | async-start | bytes 1433600 | tf_op jit(solution)/shard_map/all_gather | solution.py:647
  72.4 4.2 %collective-permute-start.7 = (bf16[4,272,384]{2,1,0:T(8,128)(2,1)S(1)}, bf16[4,272,384]{2,1,0:T(8,128)(2,1)S(1)}, u32[]{:S(2)}, u32[]{:S(2)}) collective-permute-start(bf16[4,272,384]{2,1,0:T(8,128)(2,1)S(1)} %pad_maximum_fusion.own_ref), channel_id=1, source_target_pairs={{0,4},{4,0},{1,5},{5,1},{2,6},{6,2},{3,7},{7,3},{8,12},{12,8},{9,1... | collective-permute-start | bytes 2506760 | tf_op jit(solution)/shard_map/ppermute | solution.py:645
  75.7 25.7 %copy-start.14 = (f32[640]{0:T(1024)S(1)}, f32[640]{0:T(1024)}, u32[]{:S(2)}) copy-start(f32[640]{0:T(1024)} %param.25) | copy-start | bytes 7684
  75.7 25.7 %copy-start.5 = (bf16[1280,320]{0,1:T(8,128)(2,1)S(1)}, bf16[1280,320]{0,1:T(8,128)(2,1)}, u32[]{:S(2)}) copy-start(bf16[1280,320]{0,1:T(8,128)(2,1)} %param.24) | copy-start | bytes 2457604
  76.7 1.0 copy-start.12
  107.5 12.4 %all-to-all-start.2 = ((f32[32,1,128]{2,1,0:T(1,128)}), f32[32,1,128]{2,1,0:T(1,128)S(1)}, u32[]{:S(2)}, u32[]{:S(2)}) async-start(f32[32,1,128]{2,1,0:T(1,128)} %get-tuple-element.39), calls=%async_computation.2 | async-start | bytes 32768 | tf_op jit(solution)/shard_map/all_to_all | solution.py:588
  113.0 21.6 %copy-start.15 = (f32[320]{0:T(512)S(1)}, f32[320]{0:T(512)}, u32[]{:S(2)}) copy-start(f32[320]{0:T(512)} %param.26) | copy-start | bytes 3844
  119.7 26.3 %copy-start.1 = (f32[1648,256]{1,0:T(8,128)}, f32[1648,256]{1,0:T(8,128)S(1)}, u32[]{:S(2)}) copy-start(f32[1648,256]{1,0:T(8,128)S(1)} %shard_map.142.own_hbm) | copy-start | bytes 5062660
  119.9 26.0 %collective-permute-start.8 = (f32[1648,256]{1,0:T(8,128)S(1)}, f32[1648,256]{1,0:T(8,128)}, u32[]{:S(2)}, u32[]{:S(2)}) collective-permute-start(f32[1648,256]{1,0:T(8,128)S(1)} %shard_map.142.own_hbm), channel_id=1, source_target_pairs={{0,4},{4,0},{1,5},{5,1},{2,6},{6,2},{3,7},{7,3},{8,12},{12,8},{9,1... | collective-permute-start | bytes 5062664 | tf_op jit(solution)/shard_map/ppermute | solution.py:679
  123.2 22.8 %all-to-all-start.3 = ((f32[16,1,128]{2,1,0:T(1,128)}), f32[16,1,128]{2,1,0:T(1,128)S(1)}, u32[]{:S(2)}, u32[]{:S(2)}) async-start(f32[16,1,128]{2,1,0:T(1,128)} %shard_map.143), calls=%async_computation.3 | async-start | bytes 16384 | tf_op jit(solution)/shard_map/all_to_all | solution.py:591
  134.7 1.3 copy-start.4
  145.9 1.3 copy-start.2
  152.0 15.0 %all-to-all-start.4 = ((f32[32,1,128]{2,1,0:T(1,128)}), f32[32,1,128]{2,1,0:T(1,128)S(1)}, u32[]{:S(2)}, u32[]{:S(2)}) async-start(f32[32,1,128]{2,1,0:T(1,128)} %shard_map.145), calls=%async_computation.4 | async-start | bytes 32768 | tf_op jit(solution)/shard_map/all_to_all | solution.py:588
  160.1 9.5 %copy-start.13 = (bf16[2880,4]{0,1:T(4,128)(2,1)S(1)}, bf16[2880,4]{0,1:T(4,128)(2,1)}, u32[]{:S(2)}) copy-start(bf16[2880,4]{0,1:T(4,128)(2,1)} %param.21) | copy-start | bytes 69124
  160.1 13.9 %copy-start.16 = (f32[320]{0:T(512)S(1)}, f32[320]{0:T(512)}, u32[]{:S(2)}) copy-start(f32[320]{0:T(512)} %param.27) | copy-start | bytes 3844
  167.0 18.0 %collective-permute-start.9 = (f32[1104,256]{1,0:T(8,128)S(1)}, f32[1104,256]{1,0:T(8,128)S(1)}, u32[]{:S(2)}, u32[]{:S(2)}) collective-permute-start(f32[1104,256]{1,0:T(8,128)S(1)} %shard_map.146.own_hbm), channel_id=1, source_target_pairs={{0,4},{4,0},{1,5},{5,1},{2,6},{6,2},{3,7},{7,3},{8,12},{12,8},{9,1... | collective-permute-start | bytes 3391496 | tf_op jit(solution)/shard_map/ppermute | solution.py:727
  170.4 14.6 %all-to-all-start.5 = ((f32[16,1,128]{2,1,0:T(1,128)}), f32[16,1,128]{2,1,0:T(1,128)S(1)}, u32[]{:S(2)}, u32[]{:S(2)}) async-start(f32[16,1,128]{2,1,0:T(1,128)} %shard_map.147), calls=%async_computation.5 | async-start | bytes 16384 | tf_op jit(solution)/shard_map/all_to_all | solution.py:591
  (2 other events, 1.4 us)
Sparse Core Ops, SparseCore 0:
  101.5 29.7 all-gather.2

commit v8 on v7

--- a/solution.py
+++ b/solution.py
@@ -706,7 +706,7 @@
             pltpu.VMEM((2 * SEG + 3 * GAP, MERGED), F32),
             pltpu.SemaphoreType.DMA((5,)),
         ],
-        52,
+        60,
     )(hidden_own, hidden_other, totals, gain_two, middle, shortcut, joined)
     block_own = call(
         second_kernel,

time: 195 us -> 196 us (level)
  waiting for transfers between devices: 50 us -> 47.9 us
    unnamed x35 -> x43, local copies, waits for them, and re-layouts: 5.9 us -> 6.67 us
where the time goes in v8:
time: 196 us; the launch traced here: 195 us
  starting transfers between devices  82.7 us (42%)
  waiting for transfers between devices  47.9 us (24%)
  Pallas kernels  39.1 us (20%)
  between operations  14.5 us (7%)
  local copies, waits for them, and re-layouts  8.44 us (4%)
    all_to_all x1, waiting for transfers between devices, shards(): found = lax.all_to_all(sent, PLANE, 0, 0, tiled=True)  17.9 us
    all_to_all x2, waiting for transfers between devices, summed(): return (lax.all_to_all(near, DEPTH, 0, 0, tiled=True), kept)  17.7 us
    ppermute x6, starting transfers between devices, shifted(): lax.ppermute(x, axis, [(i, i + step) for i in range(count) if 0 <= i + st...  16.4 us
    all_to_all x2, starting transfers between devices, summed(): return (lax.all_to_all(near, DEPTH, 0, 0, tiled=True), kept)  15.3 us
    all_to_all x1, starting transfers between devices, shards(): got = lax.all_to_all(sent, DEPTH, 0, 0, tiled=True)  14.9 us
    all_to_all x2, starting transfers between devices, summed(): near = lax.all_to_all(sums, PLANE, 0, 0, tiled=True)  13.6 us
    ppermute x6, waiting for transfers between devices, shifted(): lax.ppermute(x, axis, [(i, i + step) for i in range(count) if 0 <= i + st...  10.1 us
    all_to_all x1, starting transfers between devices, shards(): found = lax.all_to_all(sent, PLANE, 0, 0, tiled=True)  9.89 us
  transfers between devices with their start and end apart: 17, of which 9 were waited for; matrix products, arithmetic and copies ran while one was open for 2% of the time, Pallas kernels for 14%

profile of v8, /device:TPU:1, one launch (start us, length us, event | category | flops | bytes accessed | tf_op | source)
XLA Modules:
  0.0 194.5 jit_solution(69215211247678660)
XLA Ops:
  6.5 4.7 %collective-permute-start = (bf16[4,1,256]{2,0,1:T(4,128)(2,1)}, bf16[4,1,256]{2,0,1:T(4,128)(2,1)S(1)}, u32[]{:S(2)}, u32[]{:S(2)}) collective-permute-start(bf16[4,1,256]{2,0,1:T(4,128)(2,1)} %param.14), channel_id=1, source_target_pairs={{0,4},{4,8},{8,12},{12,16},{16,20},{20,24},{24,28},{28,32},{32,36}... | collective-permute-start | bytes 6152 | tf_op jit(solution)/shard_map/ppermute | solution.py:584
  11.3 5.5 %collective-permute-start.1 = (bf16[4,1,256]{2,0,1:T(4,128)(2,1)}, bf16[4,1,256]{2,0,1:T(4,128)(2,1)S(1)}, u32[]{:S(2)}, u32[]{:S(2)}) collective-permute-start(bf16[4,1,256]{2,0,1:T(4,128)(2,1)} %param.14), channel_id=1, source_target_pairs={{4,0},{8,4},{12,8},{16,12},{20,16},{24,20},{28,24},{32,28},{36,32}... | collective-permute-start | bytes 6152 | tf_op jit(solution)/shard_map/ppermute | solution.py:584
  20.8 1.3 collective-permute-start.2
  22.1 1.3 collective-permute-start.3
  23.4 3.1 %collective-permute-done.3.right_ref = bf16[16,384]{1,0:T(8,128)(2,1)S(1)} collective-permute-done((bf16[16,384]{1,0:T(8,128)(2,1)S(1)}, bf16[16,384]{1,0:T(8,128)(2,1)S(1)}, u32[]{:S(2)}, u32[]{:S(2)}) %collective-permute-start.3) | collective-permute-done | bytes 12320 | tf_op jit(solution)/shard_map/ppermute | solution.py:584
  26.5 1.4 shard_map.137
  27.9 14.9 %all-to-all-start = ((bf16[16,16,320]{2,1,0:T(8,128)(2,1)}), bf16[16,16,320]{2,1,0:T(8,128)(2,1)S(1)}, u32[]{:S(2)}, u32[]{:S(2)}) async-start(bf16[16,16,320]{2,1,0:T(8,128)(2,1)} %get-tuple-element.33), calls=%async_computation | async-start | bytes 393216 | tf_op jit(solution)/shard_map/all_to_all | solution.py:632
  43.2 5.3 %collective-permute-start.6 = (bf16[272,384]{1,0:T(8,128)(2,1)S(1)}, bf16[272,384]{1,0:T(8,128)(2,1)S(1)}, u32[]{:S(2)}, u32[]{:S(2)}) collective-permute-start(bf16[272,384]{1,0:T(8,128)(2,1)S(1)} %get-tuple-element.34), channel_id=1, source_target_pairs={{4,16},{12,24},{16,4},{20,32},{24,12},{28,40},{32,20},{36,48},{40,... | collective-permute-start | bytes 626696 | tf_op jit(solution)/shard_map/ppermute | solution.py:620
  48.5 2.3 %collective-permute-start.4 = (bf16[272,384]{1,0:T(8,128)(2,1)S(1)}, bf16[272,384]{1,0:T(8,128)(2,1)S(1)}, u32[]{:S(2)}, u32[]{:S(2)}) collective-permute-start(bf16[272,384]{1,0:T(8,128)(2,1)S(1)} %get-tuple-element.34), channel_id=1, source_target_pairs={{0,8},{4,12},{8,16},{12,20},{16,24},{20,28},{24,32},{28,36},{32,40... | collective-permute-start | bytes 626696 | tf_op jit(solution)/shard_map/ppermute | solution.py:584
  50.8 1.3 collective-permute-start.5
  53.3 4.6 %collective-permute-done.4 = bf16[272,384]{1,0:T(8,128)(2,1)S(1)} collective-permute-done((bf16[272,384]{1,0:T(8,128)(2,1)S(1)}, bf16[272,384]{1,0:T(8,128)(2,1)S(1)}, u32[]{:S(2)}, u32[]{:S(2)}) %collective-permute-start.4) | collective-permute-done | bytes 208928 | tf_op jit(solution)/shard_map/ppermute | solution.py:584
  57.9 2.4 %collective-permute-done.5 = bf16[272,384]{1,0:T(8,128)(2,1)S(1)} collective-permute-done((bf16[272,384]{1,0:T(8,128)(2,1)S(1)}, bf16[272,384]{1,0:T(8,128)(2,1)S(1)}, u32[]{:S(2)}, u32[]{:S(2)}) %collective-permute-start.5) | collective-permute-done | bytes 208928 | tf_op jit(solution)/shard_map/ppermute | solution.py:584
  60.5 1.9 shard_map.139
  62.4 9.9 %all-to-all-start.1 = ((bf16[32,56,640]{2,1,0:T(8,128)(2,1)}), bf16[32,56,640]{2,1,0:T(8,128)(2,1)}, u32[]{:S(2)}, u32[]{:S(2)}) async-start(bf16[32,56,640]{2,1,0:T(8,128)(2,1)} %shard_map.139), calls=%async_computation.1 | async-start | bytes 4587520 | tf_op jit(solution)/shard_map/all_to_all | solution.py:641
  72.4 2.2 %collective-permute-start.7 = (bf16[4,272,384]{2,1,0:T(8,128)(2,1)S(1)}, bf16[4,272,384]{2,1,0:T(8,128)(2,1)S(1)}, u32[]{:S(2)}, u32[]{:S(2)}) collective-permute-start(bf16[4,272,384]{2,1,0:T(8,128)(2,1)S(1)} %pad_maximum_fusion.own_ref), channel_id=1, source_target_pairs={{0,4},{4,0},{1,5},{5,1},{2,6},{6,2},{3,7},{7,3},{8,12},{12,8},{9,1... | collective-permute-start | bytes 2506760 | tf_op jit(solution)/shard_map/ppermute | solution.py:645
  77.6 5.8 %shard_map.140.joined_hbm = bf16[2192,640]{1,0:T(8,128)(2,1)} custom-call(bf16[4,272,384]{2,1,0:T(8,128)(2,1)} %copy-done.15, bf16[4,272,384]{2,1,0:T(8,128)(2,1)} %copy-done.16, bf16[384,384]{1,0:T(8,128)(2,1)} %copy-done.4), custom_call_target="tpu_custom_call" | custom-call | tf_op jit(solution)/shard_map/pallas_call | solution.py:643
  83.4 17.9 %all-to-all-done.1.found_hbm = bf16[32,56,640]{2,1,0:T(8,128)(2,1)} async-done(((bf16[32,56,640]{2,1,0:T(8,128)(2,1)}), bf16[32,56,640]{2,1,0:T(8,128)(2,1)}, u32[]{:S(2)}, u32[]{:S(2)}) %all-to-all-start.1) | async-done | bytes 2293792 | tf_op jit(solution)/shard_map/all_to_all | solution.py:641
  101.4 6.1 %shard_map.141 = (bf16[1920,512]{1,0:T(8,128)(2,1)}, f32[1,384]{1,0:T(1,128)S(1)}, f32[32,1,128]{2,1,0:T(1,128)}) custom-call(bf16[2192,640]{1,0:T(8,128)(2,1)} %shard_map.140.joined_hbm, bf16[32,56,640]{2,1,0:T(8,128)(2,1)} %all-to-all-done.1.found_hbm, bf16[320,1280]{1,0:T(8,128)(2,1)S(1)} %bitcast.21, f32[1,640]{1,0:T(1,128)S(1)} %broadcast_in_dim.8.gain_ref), custom_call_target="tpu_custom_call" | custom-call | tf_op jit(solution)/shard_map/pallas_call | solution.py:657
  107.5 5.5 %all-to-all-start.2 = ((f32[32,1,128]{2,1,0:T(1,128)}), f32[32,1,128]{2,1,0:T(1,128)S(1)}, u32[]{:S(2)}, u32[]{:S(2)}) async-start(f32[32,1,128]{2,1,0:T(1,128)} %get-tuple-element.39), calls=%async_computation.2 | async-start | bytes 32768 | tf_op jit(solution)/shard_map/all_to_all | solution.py:588
  113.0 6.6 %shard_map.142.own_hbm = f32[1648,256]{1,0:T(8,128)S(1)} custom-call(bf16[2192,640]{1,0:T(8,128)(2,1)} %shard_map.140.joined_hbm, bf16[1920,512]{1,0:T(8,128)(2,1)} %get-tuple-element.40.wm_hbm, f32[1,384]{1,0:T(1,128)S(1)} %get-tuple-element.41.known_ref, f32[1,640]{1,0:T(1,128)S(1)} %broadcast_in_dim.8.gain_ref), custom_call_target="tpu_custom_call" | custom-call | tf_op jit(solution)/shard_map/pallas_call | solution.py:665
  119.9 2.5 %collective-permute-start.8 = (f32[1648,256]{1,0:T(8,128)S(1)}, f32[1648,256]{1,0:T(8,128)}, u32[]{:S(2)}, u32[]{:S(2)}) collective-permute-start(f32[1648,256]{1,0:T(8,128)S(1)} %shard_map.142.own_hbm), channel_id=1, source_target_pairs={{0,4},{4,0},{1,5},{5,1},{2,6},{6,2},{3,7},{7,3},{8,12},{12,8},{9,1... | collective-permute-start | bytes 5062664 | tf_op jit(solution)/shard_map/ppermute | solution.py:679
  123.1 11.5 %all-to-all-start.3 = ((f32[16,1,128]{2,1,0:T(1,128)}), f32[16,1,128]{2,1,0:T(1,128)S(1)}, u32[]{:S(2)}, u32[]{:S(2)}) async-start(f32[16,1,128]{2,1,0:T(1,128)} %shard_map.143), calls=%async_computation.3 | async-start | bytes 16384 | tf_op jit(solution)/shard_map/all_to_all | solution.py:591
  135.3 1.3 copy-done.5
  136.5 1.8 shard_map.144
  139.1 6.8 %all-to-all-done.3.stat_ref = f32[16,1,128]{2,1,0:T(1,128)S(1)} async-done(((f32[16,1,128]{2,1,0:T(1,128)}), f32[16,1,128]{2,1,0:T(1,128)S(1)}, u32[]{:S(2)}, u32[]{:S(2)}) %all-to-all-start.3) | async-done | bytes 8224 | tf_op jit(solution)/shard_map/all_to_all | solution.py:591
  146.5 5.6 %shard_map.145 = f32[32,1,128]{2,1,0:T(1,128)} custom-call(f32[1648,256]{1,0:T(8,128)} %copy-done.1, f32[1648,256]{1,0:T(8,128)} %collective-permute-done.8.other_hbm, f32[16,1,128]{2,1,0:T(1,128)} %copy-done.10, f32[2,160]{1,0:T(2,128)} %reshape.29.gain_ref, bf16[1152,512]{1,0:T(8,128)(2,1)} %get-tuple-element.45.wm_hbm, bf16[640,160]{1,0:T(8,128)(2,1)} %copy-done.2, ...), custom_call_target="tpu_custom_call" | custom-call | tf_op jit(solution)/shard_map/pallas_call | solution.py:695
  152.1 8.1 %all-to-all-start.4 = ((f32[32,1,128]{2,1,0:T(1,128)}), f32[32,1,128]{2,1,0:T(1,128)S(1)}, u32[]{:S(2)}, u32[]{:S(2)}) async-start(f32[32,1,128]{2,1,0:T(1,128)} %shard_map.145), calls=%async_computation.4 | async-start | bytes 32768 | tf_op jit(solution)/shard_map/all_to_all | solution.py:588
  160.9 5.2 %shard_map.146.own_hbm = f32[1104,256]{1,0:T(8,128)S(1)} custom-call(f32[1648,256]{1,0:T(8,128)} %copy-done.1, f32[1648,256]{1,0:T(8,128)} %collective-permute-done.8.other_hbm, f32[16,1,128]{2,1,0:T(1,128)S(1)} %copy-done.11, f32[2,160]{1,0:T(2,128)S(1)} %copy-done.13, bf16[1152,512]{1,0:T(8,128)(2,1)} %get-tuple-element.45.wm_hbm, ...), custom_call_target="tpu_custom_call" | custom-call | tf_op jit(solution)/shard_map/pallas_call | solution.py:711
  167.1 2.5 %collective-permute-start.9 = (f32[1104,256]{1,0:T(8,128)S(1)}, f32[1104,256]{1,0:T(8,128)S(1)}, u32[]{:S(2)}, u32[]{:S(2)}) collective-permute-start(f32[1104,256]{1,0:T(8,128)S(1)} %shard_map.146.own_hbm), channel_id=1, source_target_pairs={{0,4},{4,0},{1,5},{5,1},{2,6},{6,2},{3,7},{7,3},{8,12},{12,8},{9,1... | collective-permute-start | bytes 3391496 | tf_op jit(solution)/shard_map/ppermute | solution.py:727
  170.5 3.9 %all-to-all-start.5 = ((f32[16,1,128]{2,1,0:T(1,128)}), f32[16,1,128]{2,1,0:T(1,128)S(1)}, u32[]{:S(2)}, u32[]{:S(2)}) async-start(f32[16,1,128]{2,1,0:T(1,128)} %shard_map.147), calls=%async_computation.5 | async-start | bytes 16384 | tf_op jit(solution)/shard_map/all_to_all | solution.py:591
  174.6 11.0 %all-to-all-done.5.stat_ref = f32[16,1,128]{2,1,0:T(1,128)S(1)} async-done(((f32[16,1,128]{2,1,0:T(1,128)}), f32[16,1,128]{2,1,0:T(1,128)S(1)}, u32[]{:S(2)}, u32[]{:S(2)}) %all-to-all-start.5) | async-done | bytes 8224 | tf_op jit(solution)/shard_map/all_to_all | solution.py:591
  185.6 2.0 %shard_map.148 = f32[4,1,256]{2,1,0:T(1,128)} custom-call(f32[1104,256]{1,0:T(8,128)S(1)} %shard_map.146.own_hbm, f32[1104,256]{1,0:T(8,128)S(1)} %collective-permute-done.9.other_hbm, f32[16,1,128]{2,1,0:T(1,128)S(1)} %all-to-all-done.5.stat_ref, f32[2,160]{1,0:T(2,128)S(1)} %reshape.30.gain_ref, bf16[2,160,128]{2,1,0:T(8,128)(2,1)S(1)} %pad.14.wout_ref), custom_call_target="tpu_custom_call" | custom-call | tf_op jit(solution)/shard_map/pallas_call | solution.py:736
  (75 shorter events, 13.8 us)
Async XLA Ops:
  6.5 36.3 %copy-start = (bf16[320,1280]{1,0:T(8,128)(2,1)S(1)}, bf16[320,1280]{1,0:T(8,128)(2,1)}, u32[]{:S(2)}) copy-start(bf16[320,1280]{1,0:T(8,128)(2,1)} %param.22) | copy-start | bytes 2457604
  6.5 11.7 %collective-permute-start = (bf16[4,1,256]{2,0,1:T(4,128)(2,1)}, bf16[4,1,256]{2,0,1:T(4,128)(2,1)S(1)}, u32[]{:S(2)}, u32[]{:S(2)}) collective-permute-start(bf16[4,1,256]{2,0,1:T(4,128)(2,1)} %param.14), channel_id=1, source_target_pairs={{0,4},{4,8},{8,12},{12,16},{16,20},{20,24},{24,28},{28,32},{32,36}... | collective-permute-start | bytes 6152 | tf_op jit(solution)/shard_map/ppermute | solution.py:584
  11.3 7.0 %collective-permute-start.1 = (bf16[4,1,256]{2,0,1:T(4,128)(2,1)}, bf16[4,1,256]{2,0,1:T(4,128)(2,1)S(1)}, u32[]{:S(2)}, u32[]{:S(2)}) collective-permute-start(bf16[4,1,256]{2,0,1:T(4,128)(2,1)} %param.14), channel_id=1, source_target_pairs={{4,0},{8,4},{12,8},{16,12},{20,16},{24,20},{28,24},{32,28},{36,32}... | collective-permute-start | bytes 6152 | tf_op jit(solution)/shard_map/ppermute | solution.py:584
  20.7 41.6 %copy-start.4 = (bf16[384,384]{1,0:T(8,128)(2,1)}, bf16[384,384]{1,0:T(8,128)(2,1)S(1)}, u32[]{:S(2)}) copy-start(bf16[384,384]{1,0:T(8,128)(2,1)S(1)} %get-tuple-element.30.wpad_ref) | copy-start | bytes 884740
  20.8 2.7 %collective-permute-start.2 = (bf16[16,384]{1,0:T(8,128)(2,1)S(1)}, bf16[16,384]{1,0:T(8,128)(2,1)S(1)}, u32[]{:S(2)}, u32[]{:S(2)}) collective-permute-start(bf16[16,384]{1,0:T(8,128)(2,1)S(1)} %get-tuple-element.28), channel_id=1, source_target_pairs={{0,1},{1,2},{2,3},{4,5},{5,6},{6,7},{8,9},{9,10},{10,11},{12,13},{... | collective-permute-start | bytes 36872 | tf_op jit(solution)/shard_map/ppermute | solution.py:584
  22.1 4.4 %collective-permute-start.3 = (bf16[16,384]{1,0:T(8,128)(2,1)S(1)}, bf16[16,384]{1,0:T(8,128)(2,1)S(1)}, u32[]{:S(2)}, u32[]{:S(2)}) collective-permute-start(bf16[16,384]{1,0:T(8,128)(2,1)S(1)} %get-tuple-element.29), channel_id=1, source_target_pairs={{1,0},{2,1},{3,2},{5,4},{6,5},{7,6},{9,8},{10,9},{11,10},{13,12},{... | collective-permute-start | bytes 36872 | tf_op jit(solution)/shard_map/ppermute | solution.py:584
  27.9 32.6 %all-to-all-start = ((bf16[16,16,320]{2,1,0:T(8,128)(2,1)}), bf16[16,16,320]{2,1,0:T(8,128)(2,1)S(1)}, u32[]{:S(2)}, u32[]{:S(2)}) async-start(bf16[16,16,320]{2,1,0:T(8,128)(2,1)} %get-tuple-element.33), calls=%async_computation | async-start | bytes 393216 | tf_op jit(solution)/shard_map/all_to_all | solution.py:632
  43.2 10.1 %collective-permute-start.6 = (bf16[272,384]{1,0:T(8,128)(2,1)S(1)}, bf16[272,384]{1,0:T(8,128)(2,1)S(1)}, u32[]{:S(2)}, u32[]{:S(2)}) collective-permute-start(bf16[272,384]{1,0:T(8,128)(2,1)S(1)} %get-tuple-element.34), channel_id=1, source_target_pairs={{4,16},{12,24},{16,4},{20,32},{24,12},{28,40},{32,20},{36,48},{40,... | collective-permute-start | bytes 626696 | tf_op jit(solution)/shard_map/ppermute | solution.py:620
  48.5 9.4 %collective-permute-start.4 = (bf16[272,384]{1,0:T(8,128)(2,1)S(1)}, bf16[272,384]{1,0:T(8,128)(2,1)S(1)}, u32[]{:S(2)}, u32[]{:S(2)}) collective-permute-start(bf16[272,384]{1,0:T(8,128)(2,1)S(1)} %get-tuple-element.34), channel_id=1, source_target_pairs={{0,8},{4,12},{8,16},{12,20},{16,24},{20,28},{24,32},{28,36},{32,40... | collective-permute-start | bytes 626696 | tf_op jit(solution)/shard_map/ppermute | solution.py:584
  50.8 9.5 %collective-permute-start.5 = (bf16[272,384]{1,0:T(8,128)(2,1)S(1)}, bf16[272,384]{1,0:T(8,128)(2,1)S(1)}, u32[]{:S(2)}, u32[]{:S(2)}) collective-permute-start(bf16[272,384]{1,0:T(8,128)(2,1)S(1)} %get-tuple-element.34), channel_id=1, source_target_pairs={{8,0},{12,4},{16,8},{20,12},{24,16},{28,20},{32,24},{36,28},{40,32... | collective-permute-start | bytes 626696 | tf_op jit(solution)/shard_map/ppermute | solution.py:584
  60.5 11.9 %copy-start.15 = (bf16[4,272,384]{2,1,0:T(8,128)(2,1)}, bf16[4,272,384]{2,1,0:T(8,128)(2,1)S(1)}, u32[]{:S(2)}) copy-start(bf16[4,272,384]{2,1,0:T(8,128)(2,1)S(1)} %pad_maximum_fusion.own_ref) | copy-start | bytes 2506756
  62.4 12.2 %copy-start.7 = (bf16[720,320]{0,1:T(8,128)(2,1)S(1)}, bf16[720,320]{0,1:T(8,128)(2,1)}, u32[]{:S(2)}) copy-start(bf16[720,320]{0,1:T(8,128)(2,1)} %param.19) | copy-start | bytes 1382404
  62.4 12.2 %copy-start.9 = (bf16[160,320]{1,0:T(8,128)(2,1)S(1)}, bf16[160,320]{1,0:T(8,128)(2,1)}, u32[]{:S(2)}) copy-start(bf16[160,320]{1,0:T(8,128)(2,1)} %skip_ref) | copy-start | bytes 307204
  62.4 38.9 %all-to-all-start.1 = ((bf16[32,56,640]{2,1,0:T(8,128)(2,1)}), bf16[32,56,640]{2,1,0:T(8,128)(2,1)}, u32[]{:S(2)}, u32[]{:S(2)}) async-start(bf16[32,56,640]{2,1,0:T(8,128)(2,1)} %shard_map.139), calls=%async_computation.1 | async-start | bytes 4587520 | tf_op jit(solution)/shard_map/all_to_all | solution.py:641
  72.3 63.0 %all-gather.3.cloned.1.call-start = ((), (), s32[]{:S(2)}) async-start(), calls=%async_computation.6 | async-start | bytes 1433600 | tf_op jit(solution)/shard_map/all_gather | solution.py:647
  72.4 4.2 %collective-permute-start.7 = (bf16[4,272,384]{2,1,0:T(8,128)(2,1)S(1)}, bf16[4,272,384]{2,1,0:T(8,128)(2,1)S(1)}, u32[]{:S(2)}, u32[]{:S(2)}) collective-permute-start(bf16[4,272,384]{2,1,0:T(8,128)(2,1)S(1)} %pad_maximum_fusion.own_ref), channel_id=1, source_target_pairs={{0,4},{4,0},{1,5},{5,1},{2,6},{6,2},{3,7},{7,3},{8,12},{12,8},{9,1... | collective-permute-start | bytes 2506760 | tf_op jit(solution)/shard_map/ppermute | solution.py:645
  75.7 25.7 %copy-start.18 = (f32[640]{0:T(1024)S(1)}, f32[640]{0:T(1024)}, u32[]{:S(2)}) copy-start(f32[640]{0:T(1024)} %param.25) | copy-start | bytes 7684
  75.7 25.7 %copy-start.6 = (bf16[1280,320]{0,1:T(8,128)(2,1)S(1)}, bf16[1280,320]{0,1:T(8,128)(2,1)}, u32[]{:S(2)}) copy-start(bf16[1280,320]{0,1:T(8,128)(2,1)} %param.24) | copy-start | bytes 2457604
  76.6 1.0 copy-start.16
  107.5 12.4 %all-to-all-start.2 = ((f32[32,1,128]{2,1,0:T(1,128)}), f32[32,1,128]{2,1,0:T(1,128)S(1)}, u32[]{:S(2)}, u32[]{:S(2)}) async-start(f32[32,1,128]{2,1,0:T(1,128)} %get-tuple-element.39), calls=%async_computation.2 | async-start | bytes 32768 | tf_op jit(solution)/shard_map/all_to_all | solution.py:588
  113.0 21.6 %copy-start.19 = (f32[320]{0:T(512)S(1)}, f32[320]{0:T(512)}, u32[]{:S(2)}) copy-start(f32[320]{0:T(512)} %param.26) | copy-start | bytes 3844
  119.6 26.2 %copy-start.1 = (f32[1648,256]{1,0:T(8,128)}, f32[1648,256]{1,0:T(8,128)S(1)}, u32[]{:S(2)}) copy-start(f32[1648,256]{1,0:T(8,128)S(1)} %shard_map.142.own_hbm) | copy-start | bytes 5062660
  119.9 26.0 %collective-permute-start.8 = (f32[1648,256]{1,0:T(8,128)S(1)}, f32[1648,256]{1,0:T(8,128)}, u32[]{:S(2)}, u32[]{:S(2)}) collective-permute-start(f32[1648,256]{1,0:T(8,128)S(1)} %shard_map.142.own_hbm), channel_id=1, source_target_pairs={{0,4},{4,0},{1,5},{5,1},{2,6},{6,2},{3,7},{7,3},{8,12},{12,8},{9,1... | collective-permute-start | bytes 5062664 | tf_op jit(solution)/shard_map/ppermute | solution.py:679
  123.1 22.7 %all-to-all-start.3 = ((f32[16,1,128]{2,1,0:T(1,128)}), f32[16,1,128]{2,1,0:T(1,128)S(1)}, u32[]{:S(2)}, u32[]{:S(2)}) async-start(f32[16,1,128]{2,1,0:T(1,128)} %shard_map.143), calls=%async_computation.3 | async-start | bytes 16384 | tf_op jit(solution)/shard_map/all_to_all | solution.py:591
  135.3 1.3 copy-start.5
  146.5 13.7 %copy-start.3 = (bf16[640,160]{1,0:T(8,128)(2,1)S(1)}, bf16[640,160]{1,0:T(8,128)(2,1)}, u32[]{:S(2)}) copy-start(bf16[640,160]{1,0:T(8,128)(2,1)} %copy-done.2) | copy-start | bytes 614404
  146.5 13.7 %copy-start.13 = (f32[2,160]{1,0:T(2,128)S(1)}, f32[2,160]{1,0:T(2,128)}, u32[]{:S(2)}) copy-start(f32[2,160]{1,0:T(2,128)} %reshape.29.gain_ref) | copy-start | bytes 3844
  152.1 15.0 %all-to-all-start.4 = ((f32[32,1,128]{2,1,0:T(1,128)}), f32[32,1,128]{2,1,0:T(1,128)S(1)}, u32[]{:S(2)}, u32[]{:S(2)}) async-start(f32[32,1,128]{2,1,0:T(1,128)} %shard_map.145), calls=%async_computation.4 | async-start | bytes 32768 | tf_op jit(solution)/shard_map/all_to_all | solution.py:588
  160.9 8.8 %copy-start.17 = (bf16[2880,4]{0,1:T(4,128)(2,1)S(1)}, bf16[2880,4]{0,1:T(4,128)(2,1)}, u32[]{:S(2)}) copy-start(bf16[2880,4]{0,1:T(4,128)(2,1)} %param.21) | copy-start | bytes 69124
  160.9 13.6 %copy-start.20 = (f32[320]{0:T(512)S(1)}, f32[320]{0:T(512)}, u32[]{:S(2)}) copy-start(f32[320]{0:T(512)} %param.27) | copy-start | bytes 3844
  167.1 18.5 %collective-permute-start.9 = (f32[1104,256]{1,0:T(8,128)S(1)}, f32[1104,256]{1,0:T(8,128)S(1)}, u32[]{:S(2)}, u32[]{:S(2)}) collective-permute-start(f32[1104,256]{1,0:T(8,128)S(1)} %shard_map.146.own_hbm), channel_id=1, source_target_pairs={{0,4},{4,0},{1,5},{5,1},{2,6},{6,2},{3,7},{7,3},{8,12},{12,8},{9,1... | collective-permute-start | bytes 3391496 | tf_op jit(solution)/shard_map/ppermute | solution.py:727
  170.5 15.1 %all-to-all-start.5 = ((f32[16,1,128]{2,1,0:T(1,128)}), f32[16,1,128]{2,1,0:T(1,128)S(1)}, u32[]{:S(2)}, u32[]{:S(2)}) async-start(f32[16,1,128]{2,1,0:T(1,128)} %shard_map.147), calls=%async_computation.5 | async-start | bytes 16384 | tf_op jit(solution)/shard_map/all_to_all | solution.py:591
  (6 other events, 4.4 us)
Sparse Core Ops, SparseCore 0:
  101.4 29.7 all-gather.2
